TPU v7x, 256 devices: a whole 4x4x8 slice. The times are simulated.
256 devices in a mesh: wide: 64 (over y_hi, x, z), narrow: 4 (over y_lo, core).
Axes of the slice: x: 4, y: 4 (y_hi: 2, y_lo: 2; y = y_hi * 2 + y_lo), z: 8, core: 2. Of those that a mesh axis runs over, the one named last changes fastest.
Arguments:
- src_emb: float32 [65536, 400], P(('wide', 'narrow')), may hold values from -1.5 to 1.5
- src_state: float32 [65536], P(('wide', 'narrow')), may hold values from 0.0001 to 0.01
- dst_emb: float32 [65536, 400], P('wide'), may hold values from -1.5 to 1.5
- dst_state: float32 [65536], P('wide'), may hold values from 0.0001 to 0.01
- relations: bfloat16 [7424, 400], replicated, may hold values from -3 to 3
- src_index: int32 [256, 2, 256], P(('wide', 'narrow')), may hold values from 0 to 255
- dst_index: int32 [256, 2, 256], P(('wide', 'narrow')), may hold values from 0 to 1023
- rel_index: int32 [256, 2, 256], P(('wide', 'narrow')), may hold values from 0 to 7423
- neg_index: int32 [64, 2, 2048], P('wide'), may hold values from 0 to 1023
Outputs:
- src_out: float32 [65536, 400], P(('wide', 'narrow'))
- dst_out: float32 [65536, 400], P('wide')
All inputs are finite; a program needn't handle non-finite values.
Results may differ from a plain program's by a relative error of at most 0.0029.
Values may be sent and summed in bfloat16 or wider, within the bound.
No kernel may reach another device: no remote copies, remote signals or barrier semaphores. Data moves between devices by JAX's collectives and lax.ppermute only.
A program may use at most 128 MiB of HBM per device.

v0:
```python
import jax
import jax.numpy as jnp
from jax import lax
from jax.sharding import PartitionSpec as P

LEARNING_RATE = 0.1


def passed_along(value, axis, steps):
    count = lax.axis_size(axis)
    pairs = [(source, (source + steps) % count) for source in range(count)]
    return lax.ppermute(value, axis, pairs)


def bucket_grads(src_rows, relations, block_bf, src_pick, dst_pick, rel_pick, neg_pick):
    rel_rows = relations[rel_pick].astype(jnp.float32)
    query_bf = (src_rows[src_pick] * rel_rows).astype(jnp.bfloat16)
    target = block_bf[dst_pick]
    positive = jnp.sum(query_bf.astype(jnp.float32) * target.astype(jnp.float32), axis=-1)
    neg_rows = block_bf[neg_pick]
    scores = lax.dot_general(
        query_bf, neg_rows, (((1,), (1,)), ((), ())), preferred_element_type=jnp.float32
    )
    weights = (jax.nn.sigmoid(scores) / neg_rows.shape[0]).astype(jnp.bfloat16)
    pull_grad = -jax.nn.sigmoid(-positive)
    query_grad = pull_grad[:, None] * target.astype(jnp.float32) + jnp.dot(
        weights, neg_rows, preferred_element_type=jnp.float32
    )
    src_grad = jnp.zeros(src_rows.shape, jnp.float32).at[src_pick].add(query_grad * rel_rows)
    neg_grad = lax.dot_general(
        weights, query_bf, (((0,), (0,)), ((), ())), preferred_element_type=jnp.float32
    )
    dst_grad = (
        jnp.zeros(block_bf.shape, jnp.float32)
        .at[dst_pick]
        .add(pull_grad[:, None] * query_bf.astype(jnp.float32))
    )
    dst_grad = dst_grad.at[neg_pick].add(neg_grad)
    return (src_grad, dst_grad)


def adagrad(embedding, accum_state, gradient):
    accum_state = accum_state + jnp.mean(gradient * gradient, axis=-1)
    return (embedding - LEARNING_RATE * gradient / jnp.sqrt(accum_state)[:, None], accum_state)


def body(
    src_emb, src_state, dst_emb, dst_state, relations, src_index, dst_index, rel_index, neg_index
):
    bucket_count = src_index.shape[1]
    dest_block = dst_emb
    dest_state = dst_state
    for bucket in range(bucket_count):
        dest_block, dest_state = passed_along((dest_block, dest_state), "wide", 1)
        src_grad, dst_grad = bucket_grads(
            src_emb,
            relations,
            dest_block.astype(jnp.bfloat16),
            src_index[0, bucket],
            dst_index[0, bucket],
            rel_index[0, bucket],
            neg_index[0, bucket],
        )
        dst_grad = lax.psum(dst_grad.astype(jnp.bfloat16), "narrow").astype(jnp.float32)
        src_emb, src_state = adagrad(src_emb, src_state, src_grad)
        dest_block, dest_state = adagrad(dest_block, dest_state, dst_grad)
    dst_result = passed_along(dest_block, "wide", -bucket_count)
    return (src_emb, dst_result)


def solution(mesh):
    in_specs = (
        P(("wide", "narrow"), None),
        P(("wide", "narrow")),
        P("wide", None),
        P("wide"),
        P(),
        P(("wide", "narrow"), None, None),
        P(("wide", "narrow"), None, None),
        P(("wide", "narrow"), None, None),
        P("wide", None, None),
    )
    out_specs = (P(("wide", "narrow"), None), P("wide", None))
    return jax.shard_map(body, mesh=mesh, in_specs=in_specs, out_specs=out_specs, check_vma=False)
```

profile of v0, /device:TPU:1, one launch (start us, length us, event | category | flops | bytes accessed | tf_op | source)
XLA Modules:
  0.0 358.5 jit_solution(16337860781987830835)
XLA Ops:
  7.2 2.5 collective-permute-start
  9.8 1.2 copy.73
  11.0 1.3 compare_select_fusion.4
  12.3 1.0 gather_fusion
  13.2 0.9 copy.69
  14.2 9.6 %copy.67 = bf16[7424,400]{1,0:T(8,128)(2,1)} copy(bf16[7424,400]{0,1:T(8,128)(2,1)} %param.13) | data formatting | bytes 11878400 | tf_op args[4]
  23.8 5.3 %gather_fusion.1 = bf16[256,400]{1,0:T(8,128)(2,1)S(1)} fusion(bf16[7424,400]{1,0:T(8,128)(2,1)} %copy.67, s32[1024]{0:T(1024)S(1)} %pad_clamp_fusion.4), kind=kCustom, calls=%fused_computation.1 | custom fusion | bytes 410624 | tf_op jit(solution)/shard_map/gather | solution.py:16
  30.5 23.8 %collective-permute-done = f32[1024,400]{0,1:T(8,128)S(1)} collective-permute-done((f32[1024,400]{0,1:T(8,128)}, f32[1024,400]{0,1:T(8,128)S(1)}, u32[]{:S(2)}, u32[]{:S(2)}) %collective-permute-start) | collective-permute-done | bytes 1638432 | tf_op jit(solution)/shard_map/ppermute | solution.py:12
  54.8 1.8 gather_fusion.2
  56.7 1.8 copy.71
  58.4 9.2 %gather_fusion.3 = bf16[2048,400]{1,0:T(8,128)(2,1)} fusion(bf16[1024,400]{1,0:T(8,128)(2,1)S(1)} %copy.70, s32[2048]{0:T(1024)S(1)} %broadcast_clamp_fusion.1), kind=kCustom, calls=%fused_computation.3 | custom fusion | bytes 3284992 | tf_op jit(solution)/shard_map/gather | solution.py:20
  67.6 1.3 fusion.23
  68.9 0.8 convert_multiply_fusion.10
  69.7 2.0 copy.77
  71.7 0.9 fusion.6
  72.6 1.0 copy-done.3
  73.6 2.8 fusion.34
  76.4 3.1 scatter_custom_fusion.1
  79.5 14.0 %scatter_fusion = f32[1024,400]{1,0:T(8,128)S(1)} fusion(f32[1024,400]{1,0:T(8,128)S(1)} %scatter_custom_fusion.1, s32[2048]{0:T(1024)S(1)} %bitcast.39, f32[2048,400]{1,0:T(8,128)} %fusion.34), kind=kCustom, calls=%fused_computation.10 | custom fusion | flops 819200 | bytes 9838592 | tf_op jit(solution)/shard_map/scatter-add | solution.py:38
  93.5 1.4 copy.79
  95.2 40.7 %all-reduce.3.cloned.1.call-done = bf16[1024,400]{0,1:T(8,128)(2,1)} async-done(((bf16[1024,400]{0,1:T(8,128)(2,1)}), bf16[1024,400]{0,1:T(8,128)(2,1)}) %all-reduce.3.cloned.1.call-update) | async-done | bytes 819216 | tf_op jit(solution)/shard_map/psum | solution.py:64
  135.9 1.3 fusion.12
  137.9 2.6 fusion.11
  140.5 1.4 collective-permute-start.2
  141.8 5.3 %gather_fusion.5 = bf16[256,400]{1,0:T(8,128)(2,1)S(1)} fusion(bf16[7424,400]{1,0:T(8,128)(2,1)} %copy.67, s32[1024]{0:T(1024)S(1)} %pad_clamp_fusion.1), kind=kCustom, calls=%fused_computation.5 | custom fusion | bytes 410624 | tf_op jit(solution)/shard_map/gather | solution.py:16
  147.4 2.9 fusion.16
  150.3 1.2 copy.72
  151.5 2.3 scatter_custom_fusion
  154.1 1.0 gather_fusion.4
  155.3 28.9 %collective-permute-done.2 = f32[1024,400]{0,1:T(8,128)} collective-permute-done((f32[1024,400]{0,1:T(8,128)}, f32[1024,400]{0,1:T(8,128)}, u32[]{:S(2)}, u32[]{:S(2)}) %collective-permute-start.2) | collective-permute-done | bytes 1638432 | tf_op jit(solution)/shard_map/ppermute | solution.py:12
  184.1 1.6 copy.80
  185.7 1.2 gather_fusion.6
  187.2 1.0 copy.83
  188.2 9.2 %gather_fusion.7 = bf16[2048,400]{1,0:T(8,128)(2,1)} fusion(bf16[1024,400]{1,0:T(8,128)(2,1)S(1)} %copy.80, s32[2048]{0:T(1024)S(1)} %broadcast_clamp_fusion), kind=kCustom, calls=%fused_computation.7 | custom fusion | bytes 3284992 | tf_op jit(solution)/shard_map/gather | solution.py:20
  197.4 3.5 fusion.9
  200.9 3.1 scatter_custom_fusion.4
  204.0 3.9 %fusion.35 = f32[2048,400]{1,0:T(8,128)} fusion(bf16[256,2048]{1,0:T(8,128)(2,1)} %fusion.9, bf16[256,400]{0,1:T(8,128)(2,1)S(1)} %get-tuple-element.11), kind=kOutput, calls=%fused_computation.89 | convolution fusion | flops 419430400 | bytes 4530176 | tf_op jit(solution)/shard_map/dot_general | solution.py:30
  207.9 14.2 %scatter_fusion.1 = f32[1024,400]{1,0:T(8,128)S(1)} fusion(f32[1024,400]{1,0:T(8,128)S(1)} %scatter_custom_fusion.4, s32[2048]{0:T(1024)S(1)} %bitcast.37, f32[2048,400]{1,0:T(8,128)} %fusion.35), kind=kCustom, calls=%fused_computation.13 | custom fusion | flops 819200 | bytes 9838592 | tf_op jit(solution)/shard_map/scatter-add | solution.py:38
  222.1 1.3 copy.85
  223.5 41.6 %all-reduce.5.cloned.1.call-done = bf16[1024,400]{0,1:T(8,128)(2,1)} async-done(((bf16[1024,400]{0,1:T(8,128)(2,1)}), bf16[1024,400]{0,1:T(8,128)(2,1)}) %all-reduce.5.cloned.1.call-update) | async-done | bytes 819216 | tf_op jit(solution)/shard_map/psum | solution.py:64
  265.2 1.3 fusion.15
  266.5 3.3 fusion.14
  269.9 8.1 %collective-permute-start.4 = (f32[1024,400]{0,1:T(8,128)}, f32[1024,400]{0,1:T(8,128)}, u32[]{:S(2)}, u32[]{:S(2)}) collective-permute-start(f32[1024,400]{0,1:T(8,128)} %fusion.14), channel_id=1, source_target_pairs={{0,248},{4,252},{8,0},{12,4},{16,8},{20,12},{24,16},{28,20},{32,24... | collective-permute-start | bytes 4915208 | tf_op jit(solution)/shard_map/ppermute | solution.py:12
  278.0 0.9 fusion.17
  279.1 2.3 scatter_custom_fusion.3
  281.8 0.9 copy.86
  282.7 66.2 %collective-permute-done.4 = f32[1024,400]{0,1:T(8,128)} collective-permute-done((f32[1024,400]{0,1:T(8,128)}, f32[1024,400]{0,1:T(8,128)}, u32[]{:S(2)}, u32[]{:S(2)}) %collective-permute-start.4) | collective-permute-done | bytes 1638432 | tf_op jit(solution)/shard_map/ppermute | solution.py:12
  348.9 2.8 copy.94
  (76 shorter events, 4.4 us)
Async XLA Ops:
  7.2 128.8 %all-reduce.3.cloned.1.call-start = ((), (), s32[]{:S(2)}) async-start(), calls=%async_computation | async-start | bytes 1638400 | tf_op jit(solution)/shard_map/psum | solution.py:64
  7.2 47.0 %collective-permute-start = (f32[1024,400]{0,1:T(8,128)}, f32[1024,400]{0,1:T(8,128)S(1)}, u32[]{:S(2)}, u32[]{:S(2)}) collective-permute-start(f32[1024,400]{0,1:T(8,128)} %param.11), channel_id=1, source_target_pairs={{0,4},{4,8},{8,12},{12,16},{16,20},{20,24},{24,28},{28,32},{32,36}... | collective-permute-start | bytes 4915208 | tf_op jit(solution)/shard_map/ppermute | solution.py:12
  12.2 1.0 copy-start.15
  14.2 9.6 %copy-start.17 = (s32[1,2,256]{2,1,0:T(2,128)S(1)}, s32[1,2,256]{2,1,0:T(2,128)}, u32[]{:S(2)}) copy-start(s32[1,2,256]{2,1,0:T(2,128)} %param.16) | copy-start | bytes 6148
  23.7 5.5 %copy-start.18 = (s32[1,2,256]{2,1,0:T(2,128)S(1)}, s32[1,2,256]{2,1,0:T(2,128)}, u32[]{:S(2)}) copy-start(s32[1,2,256]{2,1,0:T(2,128)} %param.15) | copy-start | bytes 6148
  23.7 6.1 %copy-start.10 = (s32[1,2,2048]{2,1,0:T(2,128)S(1)}, s32[1,2,2048]{2,1,0:T(2,128)}, u32[]{:S(2)}) copy-start(s32[1,2,2048]{2,1,0:T(2,128)} %param.17) | copy-start | bytes 49156
  54.3 2.4 copy-start.5
  58.4 9.2 %copy-start.7 = (bf16[256,400]{0,1:T(8,128)(2,1)S(1)}, bf16[256,400]{0,1:T(8,128)(2,1)}, u32[]{:S(2)}) copy-start(bf16[256,400]{0,1:T(8,128)(2,1)} %copy.71) | copy-start | bytes 614404
  67.6 4.1 %copy-start = (bf16[2048,400]{1,0:T(8,128)(2,1)S(1)}, bf16[2048,400]{1,0:T(8,128)(2,1)}, u32[]{:S(2)}) copy-start(bf16[2048,400]{1,0:T(8,128)(2,1)} %gather_fusion.3) | copy-start | bytes 4915204
  72.6 1.0 copy-start.3
  93.5 1.4 copy-start.19
  94.9 43.0 %copy-start.6 = (f32[1024,400]{0,1:T(8,128)S(1)}, f32[1024,400]{0,1:T(8,128)}, u32[]{:S(2)}) copy-start(f32[1024,400]{0,1:T(8,128)} %copy-done.5) | copy-start | bytes 4915204
  94.9 170.3 %all-reduce.5.cloned.1.call-start = ((), (), s32[]{:S(2)}) async-start(), calls=%async_computation.1 | async-start | bytes 1638400 | tf_op jit(solution)/shard_map/psum | solution.py:64
  95.0 42.3 %collective-permute-start.1 = (f32[1024]{0:T(1024)S(1)}, f32[1024]{0:T(1024)S(1)}, u32[]{:S(2)}, u32[]{:S(2)}) collective-permute-start(f32[1024]{0:T(1024)S(1)} %copy-done.19), channel_id=1, source_target_pairs={{0,4},{4,8},{8,12},{12,16},{16,20},{20,24},{24,28},{28,32},{32,36}... | collective-permute-start | bytes 12296 | tf_op jit(solution)/shard_map/ppermute | solution.py:12
  140.5 6.9 %copy-start.14 = (s32[256,1]{0,1:T(1,128)S(1)}, s32[256,1]{0,1:T(1,128)}, u32[]{:S(2)}) copy-start(s32[256,1]{0,1:T(1,128)} %get-tuple-element.20) | copy-start | bytes 3076
  140.5 6.9 %copy-start.13 = (s32[256,1]{0,1:T(1,128)S(1)}, s32[256,1]{0,1:T(1,128)}, u32[]{:S(2)}) copy-start(s32[256,1]{0,1:T(1,128)} %get-tuple-element.22) | copy-start | bytes 3076
  140.5 6.9 %copy-start.8 = (s32[2048,1]{0,1:T(1,128)S(1)}, s32[2048,1]{0,1:T(1,128)}, u32[]{:S(2)}) copy-start(s32[2048,1]{0,1:T(1,128)} %get-tuple-element.16) | copy-start | bytes 24580
  140.5 6.9 %copy-start.1 = (bf16[2048,400]{1,0:T(8,128)(2,1)S(1)}, bf16[2048,400]{1,0:T(8,128)(2,1)}, u32[]{:S(2)}) copy-start(bf16[2048,400]{1,0:T(8,128)(2,1)} %gather_fusion.3) | copy-start | bytes 4915204
  140.5 43.7 %collective-permute-start.2 = (f32[1024,400]{0,1:T(8,128)}, f32[1024,400]{0,1:T(8,128)}, u32[]{:S(2)}, u32[]{:S(2)}) collective-permute-start(f32[1024,400]{0,1:T(8,128)} %fusion.11), channel_id=1, source_target_pairs={{0,4},{4,8},{8,12},{12,16},{16,20},{20,24},{24,28},{28,32},{32,36}... | collective-permute-start | bytes 4915208 | tf_op jit(solution)/shard_map/ppermute | solution.py:12
  147.4 6.6 %copy-start.11 = (f32[256]{0:T(256)S(1)}, f32[256]{0:T(256)}, u32[]{:S(2)}) copy-start(f32[256]{0:T(256)} %param.10) | copy-start | bytes 3076
  204.0 3.9 %copy-start.9 = (s32[2048,1]{0,1:T(1,128)S(1)}, s32[2048,1]{0,1:T(1,128)}, u32[]{:S(2)}) copy-start(s32[2048,1]{0,1:T(1,128)} %get-tuple-element.16) | copy-start | bytes 24580
  222.1 1.3 copy-start.16
  223.4 43.1 %collective-permute-start.3 = (f32[1024]{0:T(1024)S(1)}, f32[1024]{0:T(1024)S(1)}, u32[]{:S(2)}, u32[]{:S(2)}) collective-permute-start(f32[1024]{0:T(1024)S(1)} %copy-done.16), channel_id=1, source_target_pairs={{0,4},{4,8},{8,12},{12,16},{16,20},{20,24},{24,28},{28,32},{32,36}... | collective-permute-start | bytes 12296 | tf_op jit(solution)/shard_map/ppermute | solution.py:12
  266.5 11.5 %copy-start.2 = (bf16[2048,400]{1,0:T(8,128)(2,1)S(1)}, bf16[2048,400]{1,0:T(8,128)(2,1)}, u32[]{:S(2)}) copy-start(bf16[2048,400]{1,0:T(8,128)(2,1)} %gather_fusion.7) | copy-start | bytes 4915204
  266.5 11.5 %copy-start.4 = (bf16[256,2048]{1,0:T(8,128)(2,1)S(1)}, bf16[256,2048]{1,0:T(8,128)(2,1)}, u32[]{:S(2)}) copy-start(bf16[256,2048]{1,0:T(8,128)(2,1)} %fusion.9) | copy-start | bytes 3145732
  269.9 11.7 %copy-start.12 = (f32[256]{0:T(256)S(1)}, f32[256]{0:T(256)}, u32[]{:S(2)}) copy-start(f32[256]{0:T(256)} %param.10) | copy-start | bytes 3076
  269.9 79.0 %collective-permute-start.4 = (f32[1024,400]{0,1:T(8,128)}, f32[1024,400]{0,1:T(8,128)}, u32[]{:S(2)}, u32[]{:S(2)}) collective-permute-start(f32[1024,400]{0,1:T(8,128)} %fusion.14), channel_id=1, source_target_pairs={{0,248},{4,252},{8,0},{12,4},{16,8},{20,12},{24,16},{28,20},{32,24... | collective-permute-start | bytes 4915208 | tf_op jit(solution)/shard_map/ppermute | solution.py:12
Sparse Core Ops, SparseCore 0:
  95.0 40.8 all-reduce.2
  223.6 41.5 all-reduce.4
where the time goes:
time: 359 us; the launch traced here: 358 us
  waiting for transfers between devices  201 us (56%)
  local copies, waits for them, and re-layouts  61.9 us (17%)
  other arithmetic  53.6 us (15%)
  matrix products  14.9 us (4%)
  between operations  14.4 us (4%)
  starting transfers between devices  12.5 us (3%)
    ppermute x5, waiting for transfers between devices, passed_along(): return lax.ppermute(value, axis, pairs)  119 us
    psum x2, waiting for transfers between devices, body(): lax.psum(dst_grad.astype(jnp.bfloat16), 'narrow').astype(jnp.float32)  82.3 us
    scatter-add x2, other arithmetic, bucket_grads(): dst_grad = dst_grad.at[neg_pick].add(neg_grad)  28.2 us
    gather x2, local copies, waits for them, and re-layouts, bucket_grads(): neg_rows = block_bf[neg_pick]  18.3 us
    unnamed x44, local copies, waits for them, and re-layouts  15.5 us
    ppermute x5, starting transfers between devices, passed_along(): return lax.ppermute(value, axis, pairs)  12.4 us
    gather x4, local copies, waits for them, and re-layouts, bucket_grads(): rel_rows = relations[rel_pick].astype(jnp.float32)  11 us
  transfers between devices with their start and end apart: 7, of which 5 were waited for; matrix products, arithmetic and copies ran while one was open for 12% of the time, Pallas kernels for 0%

commit v1 on v0

v1 whole, which is shorter than its diff:
```python
import functools

import jax
import jax.numpy as jnp
from jax import lax
from jax.experimental import pallas as pl
from jax.experimental.pallas import tpu as pltpu
from jax.sharding import PartitionSpec as P

LEARNING_RATE = 0.1
BF = jnp.bfloat16
F32 = jnp.float32
I32 = jnp.int32
META = 16
FINE = 32
LANES = 128


def dot(a, b):
    return lax.dot_general(a, b, (((1,), (0,)), ((), ())), preferred_element_type=F32)


def dot_nt(a, b):
    return lax.dot_general(a, b, (((1,), (1,)), ((), ())), preferred_element_type=F32)


def core():
    return lax.rem(lax.axis_index("narrow"), 2)


def iota(shape, dim):
    return lax.broadcasted_iota(I32, shape, dim)


def one_hot(rows, index):
    return (iota((rows, index.shape[1]), 0) == index).astype(F32).astype(BF)


def eye(n):
    return (iota((n, n), 0) == iota((n, n), 1)).astype(F32).astype(BF)


def two_rows(first, second, width):
    at = iota((META, width), 0)
    return jnp.where(at == 0, first, jnp.where(at == 1, second, 0.0)).astype(BF)


def index_rows(index):
    fine = lax.rem(index, FINE)
    coarse = lax.div(index, FINE)
    return two_rows(coarse.astype(F32), fine.astype(F32), index.shape[1])


def split(value):
    high = value.astype(BF)
    return high, (value - high.astype(F32)).astype(BF)


def picked(value, hot):
    high, low = split(value)
    return dot(high, hot) + dot(low, hot)


def summed(value, hot):
    high, low = split(value)
    return dot_nt(high, hot) + dot_nt(low, hot)


def coefficients(scores, count, is_target, negatives):
    tanh = jnp.tanh(0.5 * scores)
    scale = count * (0.5 / negatives)
    pull = jnp.where(is_target, 0.5 * tanh - 0.5, 0.0)
    return (scale * tanh + scale + pull).astype(BF)


def step_size(state, gradient):
    state = state + jnp.mean(gradient * gradient, axis=0, keepdims=True)
    return state, LEARNING_RATE / jnp.sqrt(state)


def cast_kernel(emb_ref, state_ref, out_ref, held, sem):
    depth, half = held.shape
    columns = pl.ds(pl.multiple_of(core() * half, half), half)
    copy = pltpu.make_async_copy(emb_ref.at[:, columns], held, sem)
    copy.start()
    state = state_ref[:, columns]
    high = state.astype(BF).astype(F32)
    out_ref[depth:, :] = two_rows(high, state - high, half)
    copy.wait()
    out_ref[:depth, :] = held[...].astype(BF)


def count_grid(index, blocks):
    return one_hot(blocks, lax.div(index, LANES)), one_hot(LANES, lax.rem(index, LANES))


def prep_kernel(
    chunks, rows, rel_ref, src_ref, src_index, dst_index, rel_index, neg_index,
    q_ref, qt_ref, at_ref, rel0_ref, rel1_ref, count_ref, column_ref, held, sems,
):
    depth, edges = src_ref.shape
    copies = []
    start = 0
    for i, size in enumerate(chunks):
        part = pl.ds(start, size)
        copies.append(pltpu.make_async_copy(rel_ref.at[:, part], held.at[:, part], sems.at[i]))
        copies[-1].start()
        start += size

    flip = core() * (rows // 2)
    coarse, fine = count_grid(neg_index[0:1, :] ^ flip, rows // LANES)
    counts = dot_nt(coarse, fine)
    for i in range(rows // LANES):
        count_ref[:, i * LANES : (i + 1) * LANES] = counts[i : i + 1, :]
    column_ref[...] = dot_nt(fine, coarse)

    src_rows = picked(src_ref[...], one_hot(edges, src_index[0:1, :]))
    which = jnp.concatenate([rel_index[0:1, :], rel_index[1:2, :]], axis=1)
    block = lax.div(which, LANES)
    within = one_hot(LANES, lax.rem(which, LANES))
    found = jnp.zeros((depth, 2 * edges), F32)
    start = 0
    for copy, size in zip(copies, chunks):
        hot = jnp.concatenate(
            [
                within * (block == start // LANES + i).astype(F32).astype(BF)
                for i in range(size // LANES)
            ],
            axis=0,
        )
        copy.wait()
        found = found + dot(held[:, start : start + size], hot)
        start += size
    rel0_ref[...] = found[:, :edges].astype(BF)
    rel1_ref[...] = found[:, edges:].astype(BF)
    query = (src_rows * found[:, :edges]).astype(BF)
    meta = index_rows(dst_index[0:1, :])
    q_ref[:depth, :] = query
    q_ref[depth:, :] = meta
    turn = eye(edges)
    qt_ref[...] = dot_nt(turn, query).astype(BF)
    parts = dot_nt(turn, meta)
    local = (parts[:, 0:1] * FINE + parts[:, 1:2]).astype(I32) ^ flip
    at_ref[...] = jnp.broadcast_to(local, at_ref.shape)


def src0_kernel(
    negatives, own_ref, other_ref, qt_ref, at_ref, count_ref, src_ref, state_ref,
    rel0_ref, rel1_ref, src_index, dst_index, q_ref, src_out, state_out,
):
    depth, edges = src_ref.shape
    half = own_ref.shape[1]
    query_grad = jnp.zeros((depth, edges), F32)
    for i, block_ref in enumerate((own_ref, other_ref)):
        block = block_ref[:depth, :]
        scores = dot(qt_ref[...], block)
        target = iota(scores.shape, 1) + i * half == at_ref[:, 0:1]
        count = count_ref[:, i * half : (i + 1) * half]
        query_grad += dot_nt(block, coefficients(scores, count, target, negatives))
    gradient = summed(
        query_grad * rel0_ref[...].astype(F32), one_hot(edges, src_index[0:1, :])
    )
    state, size = step_size(state_ref[...], gradient)
    src = src_ref[...] - gradient * size
    src_out[...] = src
    state_out[...] = state
    rows = picked(src, one_hot(edges, src_index[1:2, :]))
    q_ref[:depth, :] = (rows * rel1_ref[...].astype(F32)).astype(BF)
    q_ref[depth:, :] = index_rows(dst_index[1:2, :])


def targets(q_ref, depth, flip):
    parts = q_ref[depth:, :].astype(F32)
    return (parts[0:1, :] * FINE + parts[1:2, :]).astype(I32) ^ flip


def row_coefficients(block_t, start, q_ref, column, flip, negatives):
    rows, depth = block_t.shape
    scores = dot(block_t, q_ref[:depth, :])
    target = iota(scores.shape, 0) + start == targets(q_ref, depth, flip)
    first = start // LANES
    count = jnp.concatenate(
        [column[:, first + i : first + i + 1] for i in range(rows // LANES)], axis=0
    )
    return coefficients(scores, count, target, negatives)


def dst_gradient(block_t, start, q_refs, column, flip, negatives):
    rows, depth = block_t.shape
    total = jnp.zeros((depth, rows), F32)
    for q_ref in q_refs:
        weights = row_coefficients(block_t, start, q_ref, column, flip, negatives)
        total += dot_nt(q_ref[:depth, :], weights)
    return total


def dst0_kernel(
    negatives, own_ref, other_ref, qa, qb, qc, qd, column_ref, neg_index,
    block_out, turned_out, delta_out, state_out, column_out,
):
    depth, half = delta_out.shape
    flip = core() * half
    turn = eye(2 * LANES)
    column = column_ref[...]
    for i, block_ref in enumerate((own_ref, other_ref)):
        block = block_ref[:depth, :]
        turned = jnp.concatenate(
            [
                dot_nt(turn, block[:, k : k + 2 * LANES]).astype(BF)
                for k in range(0, half, 2 * LANES)
            ],
            axis=0,
        )
        gradient = dst_gradient(turned, i * half, (qa, qb, qc, qd), column, flip, negatives)
        parts = block_ref[depth:, :].astype(F32)
        state, size = step_size(parts[0:1, :] + parts[1:2, :], gradient)
        delta = gradient * size
        block = (block.astype(F32) - delta).astype(BF)
        block_out[:, i * half : (i + 1) * half] = block
        for k in range(0, half, 2 * LANES):
            turned_out[i * half + k : i * half + k + 2 * LANES, :] = dot_nt(
                turn, block[:, k : k + 2 * LANES]
            ).astype(BF)
        if i == 0:
            delta_out[...] = delta
            state_out[...] = state
    coarse, fine = count_grid(neg_index[...] ^ flip, 2 * half // LANES)
    column_out[...] = dot_nt(fine, coarse)


def dst1_kernel(
    negatives, turned_ref, qa, qb, qc, qd, column_ref, delta_ref, state_ref, delta_out
):
    half = delta_ref.shape[1]
    flip = core() * half
    gradient = dst_gradient(
        turned_ref[:half, :], 0, (qa, qb, qc, qd), column_ref[...], flip, negatives
    )
    _, size = step_size(state_ref[...], gradient)
    delta_out[...] = (delta_ref[...] + gradient * size).astype(BF)


def query1_kernel(negatives, turned_ref, block_ref, q_ref, column_ref, out_ref):
    rows = turned_ref.shape[0]
    weights = row_coefficients(
        turned_ref[...], 0, q_ref, column_ref[...], core() * (rows // 2), negatives
    )
    out_ref[...] = dot(block_ref[...], weights).astype(BF)


def src1_kernel(grad_ref, rel_ref, src_ref, state_ref, src_index, src_out):
    edges = src_ref.shape[1]
    gradient = summed(
        grad_ref[...].astype(F32) * rel_ref[...].astype(F32), one_hot(edges, src_index[1:2, :])
    )
    _, size = step_size(state_ref[...], gradient)
    src_out[...] = src_ref[...] - gradient * size


def final_kernel(emb_ref, own_ref, other_ref, out_ref):
    half = own_ref.shape[1]
    here = core()
    for place, delta_ref in ((here, own_ref), (1 - here, other_ref)):
        columns = pl.ds(pl.multiple_of(place * half, half), half)
        out_ref[:, columns] = emb_ref[:, columns] - delta_ref[...].astype(F32)


def call(kernel, outs, args, name, flops=0, scratch=(), hbm=(), limit=32):
    vmem = pl.BlockSpec(memory_space=pltpu.VMEM)
    anywhere = pl.BlockSpec(memory_space=pl.ANY)
    shapes = [jax.ShapeDtypeStruct(shape, dtype) for shape, dtype in outs]
    size = sum(a.size * a.dtype.itemsize for a in [*args, *shapes])
    result = pl.pallas_call(
        kernel,
        out_shape=shapes,
        in_specs=[anywhere if i in hbm else vmem for i in range(len(args))],
        out_specs=[vmem] * len(shapes),
        scratch_shapes=list(scratch),
        compiler_params=pltpu.CompilerParams(vmem_limit_bytes=limit << 20),
        cost_estimate=pl.CostEstimate(flops=flops, bytes_accessed=size, transcendentals=0),
        name=name,
    )(*args)
    return result[0] if len(shapes) == 1 else result


def body(
    src_emb, src_state, dst_emb, dst_state, relations, src_index, dst_index, rel_index, neg_index
):
    wide, narrow = lax.axis_size("wide"), lax.axis_size("narrow")

    def moved(value, along=0, to=0):
        pairs = [
            (w * narrow + n, ((w + along) % wide) * narrow + (n ^ to))
            for w in range(wide)
            for n in range(narrow)
        ]
        return lax.ppermute(value, ("wide", "narrow"), pairs)

    rows, depth = dst_emb.shape
    edges = src_emb.shape[0]
    half = rows // 2
    relation_count = relations.shape[0]
    src_index, dst_index, rel_index, neg_index = (
        a[0] for a in (src_index, dst_index, rel_index, neg_index)
    )
    negatives = neg_index.shape[1]
    dst, src, rel = dst_emb.T, src_emb.T, relations.T
    tall = depth + META

    payload = call(
        cast_kernel,
        [((tall, half), BF)],
        [dst, dst_state.reshape(1, rows)],
        "cast_block",
        scratch=[pltpu.VMEM((depth, half), F32), pltpu.SemaphoreType.DMA],
        hbm=(0,),
        limit=8,
    )
    own = moved(payload, along=1)
    negs_next = moved(neg_index[1:2, :], along=-1)

    pieces = relation_count // (2 * LANES)
    chunks = [(pieces // 4 + (i < pieces % 4)) * 2 * LANES for i in range(4)]
    chunks[-1] += relation_count - sum(chunks)
    query, query_t, target_at, rel0, rel1, count, column = call(
        functools.partial(prep_kernel, tuple(chunks), rows),
        [
            ((tall, edges), BF),
            ((edges, depth), BF),
            ((edges, LANES), I32),
            ((depth, edges), BF),
            ((depth, edges), BF),
            ((1, rows), F32),
            ((LANES, rows // LANES), F32),
        ],
        [rel, src, src_index, dst_index, rel_index, neg_index],
        "relation_rows",
        flops=4 * depth * edges * relation_count,
        scratch=[pltpu.VMEM((depth, relation_count), BF), pltpu.SemaphoreType.DMA((4,))],
        hbm=(0,),
        limit=40,
    )
    other = moved(own, to=1)
    query_y = moved(query, to=2)
    query_c, query_cy = moved(query, to=1), moved(query_y, to=1)

    matmul = 2 * edges * rows * depth
    query1, src1, src_state1 = call(
        functools.partial(src0_kernel, negatives),
        [((tall, edges), BF), ((depth, edges), F32), ((1, edges), F32)],
        [
            own, other, query_t, target_at, count, src, src_state.reshape(1, edges),
            rel0, rel1, src_index, dst_index,
        ],
        "source_step0",
        flops=2 * matmul,
        limit=24,
    )
    next_own, next_y = moved(query1, along=-1), moved(query1, along=-1, to=2)

    block1, turned1, delta0, dst_state1, column1 = call(
        functools.partial(dst0_kernel, negatives),
        [
            ((depth, rows), BF),
            ((rows, depth), BF),
            ((depth, half), F32),
            ((1, half), F32),
            ((LANES, rows // LANES), F32),
        ],
        [own, other, query, query_y, query_c, query_cy, column, negs_next],
        "destination_step0",
        flops=8 * matmul,
        limit=32,
    )
    next_c, next_cy = moved(next_own, to=1), moved(next_y, to=1)

    delta = call(
        functools.partial(dst1_kernel, negatives),
        [((depth, half), BF)],
        [turned1, next_own, next_y, next_c, next_cy, column1, delta0, dst_state1],
        "destination_step1",
        flops=4 * matmul,
        limit=24,
    )
    home_own = moved(delta, along=-1)
    query_grad = call(
        functools.partial(query1_kernel, negatives),
        [((depth, edges), BF)],
        [turned1, block1, next_own, column1],
        "query_gradient_step1",
        flops=2 * matmul,
        limit=24,
    )
    home_grad = moved(query_grad, along=1)
    home_other = moved(home_own, to=1)
    src_out = call(
        src1_kernel,
        [((depth, edges), F32)],
        [home_grad, rel1, src1, src_state1, src_index],
        "source_step1",
        limit=16,
    )
    dst_out = call(
        final_kernel,
        [((depth, rows), F32)],
        [dst, home_own, home_other],
        "destination_out",
        limit=16,
    )
    return src_out.T, dst_out.T


def solution(mesh):
    in_specs = (
        P(("wide", "narrow"), None),
        P(("wide", "narrow")),
        P("wide", None),
        P("wide"),
        P(),
        P(("wide", "narrow"), None, None),
        P(("wide", "narrow"), None, None),
        P(("wide", "narrow"), None, None),
        P("wide", None, None),
    )
    out_specs = (P(("wide", "narrow"), None), P("wide", None))
    return jax.shard_map(body, mesh=mesh, in_specs=in_specs, out_specs=out_specs, check_vma=False)
```

time: 359 us -> 97.9 us (0.27)
  waiting for transfers between devices: 201 us -> 46.4 us
  local copies, waits for them, and re-layouts: 61.9 us -> 4.83 us
  other arithmetic: 53.6 us -> 0 us
  Pallas kernels: 0 us -> 17.8 us
  starting transfers between devices: 12.5 us -> 27.9 us
  matrix products: 14.9 us -> 0 us
  between operations: 14.4 us -> 0.76 us
    psum x2 -> x0, waiting for transfers between devices: 82.3 us -> none  [body(): lax.psum(dst_grad.astype(jnp.bfloat16), 'narrow').astype(jnp.float32)]
    ppermute x5 -> x13, waiting for transfers between devices: 119 us -> 46.4 us  [moved(): return lax.ppermute(value, ('wide', 'narrow'), pairs)]
    scatter-add x6 -> x0, other arithmetic: 39.1 us -> none  [the longest x2 28.2 us: bucket_grads(): dst_grad = dst_grad.at[neg_pick].add(neg_grad)]
    gather x14 -> x0, local copies, waits for them, and re-layouts: 37.2 us -> none  [the longest x2 18.3 us: bucket_grads(): neg_rows = block_bf[neg_pick]]
    pallas_call x0 -> x8, Pallas kernels: none -> 17.8 us  [call(): pl.pallas_call(kernel, out_shape=shapes, in_specs=[anywhere if i in hbm e...]
    ppermute x5 -> x13, starting transfers between devices: 12.4 us -> 27.9 us  [moved(): return lax.ppermute(value, ('wide', 'narrow'), pairs)]
    dot_general x6 -> x0, matrix products: 14.9 us -> none  [the longest x2 6.75 us: bucket_grads(): lax.dot_general(weights, query_bf, (((0,), (0,)), ((), ())), preferred_el...]
    unnamed x44 -> x20, local copies, waits for them, and re-layouts: 15.5 us -> 4.82 us
  transfers between devices with their start and end apart: 7 -> 13, of which waited for: 5 -> 7; matrix products, arithmetic and copies ran while one was open for 12% -> 0% of each run, Pallas kernels for 0% -> 14%
where the time goes in v1:
time: 97.9 us; the launch traced here: 97.7 us
  waiting for transfers between devices  46.4 us (47%)
  starting transfers between devices  27.9 us (28%)
  Pallas kernels  17.8 us (18%)
  local copies, waits for them, and re-layouts  4.83 us (5%)
    ppermute x13, waiting for transfers between devices, moved(): return lax.ppermute(value, ('wide', 'narrow'), pairs)  46.4 us
    ppermute x13, starting transfers between devices, moved(): return lax.ppermute(value, ('wide', 'narrow'), pairs)  27.9 us
    pallas_call x8, Pallas kernels, call(): pl.pallas_call(kernel, out_shape=shapes, in_specs=[anywhere if i in hbm e...  17.8 us
    unnamed x20, local copies, waits for them, and re-layouts  4.82 us
  transfers between devices with their start and end apart: 13, of which 7 were waited for; matrix products, arithmetic and copies ran while one was open for 0% of the time, Pallas kernels for 14%

profile of v1, /device:TPU:1, one launch (start us, length us, event | category | flops | bytes accessed | tf_op | source)
XLA Modules:
  0.0 97.7 jit_solution(1118037241055855651)
XLA Ops:
  0.6 0.0 copy-start.3
  0.6 0.0 copy-start
  0.7 1.4 %copy-done = f32[1024,400]{0,1:T(8,128)S(1)} copy-done((f32[1024,400]{0,1:T(8,128)S(1)}, f32[1024,400]{0,1:T(8,128)}, u32[]{:S(2)}) %copy-start) | copy-done | bytes 1638424
  2.1 0.7 copy-done.4
  2.8 0.0 copy-start.2
  2.8 0.2 cast_block.1
  2.9 2.5 %collective-permute-start = (bf16[416,512]{1,0:T(8,128)(2,1)S(1)}, bf16[416,512]{1,0:T(8,128)(2,1)S(1)}, u32[]{:S(2)}, u32[]{:S(2)}) collective-permute-start(bf16[416,512]{1,0:T(8,128)(2,1)S(1)} %cast_block.1), channel_id=1, source_target_pairs={{0,4},{1,5},{2,6},{3,7},{4,8},{5,9},{6,10},{7,11},{8,12},{9,13},{1... | collective-permute-start | bytes 1277960 | tf_op jit(solution)/shard_map/ppermute | solution.py:297
  5.5 18.3 %collective-permute-done.own_ref = bf16[416,512]{1,0:T(8,128)(2,1)S(1)} collective-permute-done((bf16[416,512]{1,0:T(8,128)(2,1)S(1)}, bf16[416,512]{1,0:T(8,128)(2,1)S(1)}, u32[]{:S(2)}, u32[]{:S(2)}) %collective-permute-start) | collective-permute-done | bytes 426016 | tf_op jit(solution)/shard_map/ppermute | solution.py:297
  23.8 1.2 %collective-permute-start.1 = (bf16[416,512]{1,0:T(8,128)(2,1)S(1)}, bf16[416,512]{1,0:T(8,128)(2,1)S(1)}, u32[]{:S(2)}, u32[]{:S(2)}) collective-permute-start(bf16[416,512]{1,0:T(8,128)(2,1)S(1)} %collective-permute-done.own_ref), channel_id=1, source_target_pairs={{0,1},{1,0},{2,3},{3,2},{4,5},{5,4},{6,7},{7,6},{8,9},{9,8},{10,11... | collective-permute-start | bytes 1277960 | tf_op jit(solution)/shard_map/ppermute | solution.py:297
  25.0 0.0 copy-done.3
  25.0 0.0 copy-done.2
  25.0 0.0 copy-done.5
  25.0 0.0 copy-done.6
  25.0 0.0 copy-done.9
  25.0 0.0 copy-start.8
  25.1 2.7 %copy-done.8 = bf16[7424,400]{0,1:T(8,128)(2,1)S(1)} copy-done((bf16[7424,400]{0,1:T(8,128)(2,1)S(1)}, bf16[7424,400]{0,1:T(8,128)(2,1)}, u32[]{:S(2)}) %copy-start.8) | copy-done | bytes 5939224
  27.7 5.0 %relation_rows.1 = (bf16[416,256]{1,0:T(8,128)(2,1)S(1)}, bf16[256,400]{1,0:T(8,128)(2,1)S(1)}, s32[256,128]{1,0:T(8,128)S(1)}, bf16[400,256]{1,0:T(8,128)(2,1)S...) custom-call(bf16[400,7424]{1,0:T(8,128)(2,1)S(1)} %bitcast.25, ...), custom_call_target="tpu_custom_call" | custom-call | flops 3040870400 | bytes 7337984 | tf_op jit(solution)/shard_map/relation_rows/pallas_call | solution.py:273
  32.7 0.5 collective-permute-start.2
  33.2 0.0 collective-permute-done.1.other_ref
  33.2 0.0 copy-done.7
  33.2 1.7 %source_step0.1 = (bf16[416,256]{1,0:T(8,128)(2,1)S(1)}, f32[400,256]{1,0:T(8,128)S(1)}, f32[1,256]{1,0:T(1,128)S(1)}) custom-call(bf16[416,512]{1,0:T(8,128)(2,1)S(1)} %collective-permute-done.own_ref, bf16[416,512]{1,0:T(8,128)(2,1)S(1)} %collective-permute-done.1.other_ref, bf16[256,400]{1,0:T(8,128)(2,1)S(1)} %get-tuple-element.21.qt_ref, ...), custom_call_target="tpu_custom_call" | custom-call | flops 419430400 | bytes 2639872 | tf_op jit(solution)/shard_map/source_step0/pallas_call | solution.py:273
  34.9 2.1 %collective-permute-start.6 = (bf16[416,256]{1,0:T(8,128)(2,1)S(1)}, bf16[416,256]{1,0:T(8,128)(2,1)S(1)}, u32[]{:S(2)}, u32[]{:S(2)}) collective-permute-start(bf16[416,256]{1,0:T(8,128)(2,1)S(1)} %get-tuple-element.26), channel_id=1, source_target_pairs={{0,252},{1,253},{2,254},{3,255},{4,0},{5,1},{6,2},{7,3},{8,4},{9,5... | collective-permute-start | bytes 638984 | tf_op jit(solution)/shard_map/ppermute | solution.py:297
  37.1 0.0 collective-permute-start.8
  37.1 0.9 collective-permute-start.3
  37.9 1.7 %collective-permute-done.2.qb = bf16[416,256]{1,0:T(8,128)(2,1)S(1)} collective-permute-done((bf16[416,256]{1,0:T(8,128)(2,1)S(1)}, bf16[416,256]{1,0:T(8,128)(2,1)S(1)}, u32[]{:S(2)}, u32[]{:S(2)}) %collective-permute-start.2) | collective-permute-done | bytes 213024 | tf_op jit(solution)/shard_map/ppermute | solution.py:297
  39.7 0.8 collective-permute-start.4
  40.5 1.1 %collective-permute-done.6.q_ref.qa = bf16[416,256]{1,0:T(8,128)(2,1)S(1)} collective-permute-done((bf16[416,256]{1,0:T(8,128)(2,1)S(1)}, bf16[416,256]{1,0:T(8,128)(2,1)S(1)}, u32[]{:S(2)}, u32[]{:S(2)}) %collective-permute-start.6) | collective-permute-done | bytes 213024 | tf_op jit(solution)/shard_map/ppermute | solution.py:297
  41.6 1.8 %collective-permute-start.9 = (bf16[416,256]{1,0:T(8,128)(2,1)S(1)}, bf16[416,256]{1,0:T(8,128)(2,1)S(1)}, u32[]{:S(2)}, u32[]{:S(2)}) collective-permute-start(bf16[416,256]{1,0:T(8,128)(2,1)S(1)} %collective-permute-done.6.q_ref.qa), channel_id=1, source_target_pairs={{0,1},{1,0},{2,3},{3,2},{4,5},{5,4},{6,7},{7,6},{8,9},{9,8},{10,11... | collective-permute-start | bytes 638984 | tf_op jit(solution)/shard_map/ppermute | solution.py:297
  43.4 3.5 %collective-permute-done.8.qb = bf16[416,256]{1,0:T(8,128)(2,1)S(1)} collective-permute-done((bf16[416,256]{1,0:T(8,128)(2,1)S(1)}, bf16[416,256]{1,0:T(8,128)(2,1)S(1)}, u32[]{:S(2)}, u32[]{:S(2)}) %collective-permute-start.8) | collective-permute-done | bytes 213024 | tf_op jit(solution)/shard_map/ppermute | solution.py:297
  46.9 1.1 %collective-permute-start.10 = (bf16[416,256]{1,0:T(8,128)(2,1)S(1)}, bf16[416,256]{1,0:T(8,128)(2,1)S(1)}, u32[]{:S(2)}, u32[]{:S(2)}) collective-permute-start(bf16[416,256]{1,0:T(8,128)(2,1)S(1)} %collective-permute-done.8.qb), channel_id=1, source_target_pairs={{0,1},{1,0},{2,3},{3,2},{4,5},{5,4},{6,7},{7,6},{8,9},{9,8},{10,11... | collective-permute-start | bytes 638984 | tf_op jit(solution)/shard_map/ppermute | solution.py:297
  48.0 7.3 %collective-permute-start.5 = (s32[1,2048]{1,0:T(1,128)S(1)}, s32[1,2048]{1,0:T(1,128)S(1)}, u32[]{:S(2)}, u32[]{:S(2)}) collective-permute-start(s32[1,2048]{1,0:T(1,128)S(1)} %slice_bitcast_fusion), channel_id=1, source_target_pairs={{0,252},{1,253},{2,254},{3,255},{4,0},{5,1},{6,2},{7,3},{8,4},{9,5... | collective-permute-start | bytes 24584 | tf_op jit(solution)/shard_map/ppermute | solution.py:297
  55.3 0.8 collective-permute-done.5.neg_index
  56.1 0.0 collective-permute-done.3.qc
  56.1 0.0 collective-permute-done.4.qd
  56.1 5.2 %destination_step0.1 = (bf16[400,1024]{1,0:T(8,128)(2,1)S(1)}, bf16[1024,400]{1,0:T(8,128)(2,1)S(1)}, f32[400,512]{1,0:T(8,128)S(1)}, f32[1,512]{1,0:T(1,128)S(1)}, f32[128,8]{1,0:T(8,128)S(1)}) custom-call(bf16[416,512]{1,0:T(8,128)(2,1)S(1)} %collective-permute-done.own_ref, bf16[416,512]{1,0:T(8,128)(2,1)S(1)} %collective-permute-done.1.other_ref, ...), custom_call_target="tpu_custom_call" | custom-call | flops 1677721600 | bytes 4179968 | tf_op jit(solution)/shard_map/destination_step0/pallas_call | solution.py:273
  61.2 0.0 collective-permute-done.9.qc
  61.3 0.0 collective-permute-done.10.qd
  61.3 2.2 %destination_step1.1 = bf16[400,512]{1,0:T(8,128)(2,1)S(1)} custom-call(bf16[1024,400]{1,0:T(8,128)(2,1)S(1)} %get-tuple-element.19.turned_ref, bf16[416,256]{1,0:T(8,128)(2,1)S(1)} %collective-permute-done.6.q_ref.qa, bf16[416,256]{1,0:T(8,128)(2,1)S(1)} %collective-permute-done.8.qb, bf16[416,256]{1,0:T(8,128)(2,1)S(1)} %collective-permute-done.9.qc, ...), custom_call_target="tpu_custom_call" | custom-call | flops 838860800 | bytes 2906112 | tf_op jit(solution)/shard_map/destination_step1/pallas_call | solution.py:273
  63.4 7.5 %collective-permute-start.11 = (bf16[400,512]{1,0:T(8,128)(2,1)S(1)}, bf16[400,512]{1,0:T(8,128)(2,1)S(1)}, u32[]{:S(2)}, u32[]{:S(2)}) collective-permute-start(bf16[400,512]{1,0:T(8,128)(2,1)S(1)} %destination_step1.1), channel_id=1, source_target_pairs={{0,252},{1,253},{2,254},{3,255},{4,0},{5,1},{6,2},{7,3},{8,4},{9,5... | collective-permute-start | bytes 1228808 | tf_op jit(solution)/shard_map/ppermute | solution.py:297
  70.9 7.6 %collective-permute-done.11.own_ref = bf16[400,512]{1,0:T(8,128)(2,1)S(1)} collective-permute-done((bf16[400,512]{1,0:T(8,128)(2,1)S(1)}, bf16[400,512]{1,0:T(8,128)(2,1)S(1)}, u32[]{:S(2)}, u32[]{:S(2)}) %collective-permute-start.11) | collective-permute-done | bytes 409632 | tf_op jit(solution)/shard_map/ppermute | solution.py:297
  78.5 2.1 %collective-permute-start.12 = (bf16[400,512]{1,0:T(8,128)(2,1)S(1)}, bf16[400,512]{1,0:T(8,128)(2,1)S(1)}, u32[]{:S(2)}, u32[]{:S(2)}) collective-permute-start(bf16[400,512]{1,0:T(8,128)(2,1)S(1)} %collective-permute-done.11.own_ref), channel_id=1, source_target_pairs={{0,1},{1,0},{2,3},{3,2},{4,5},{5,4},{6,7},{7,6},{8,9},{9,8},{10,11... | collective-permute-start | bytes 1228808 | tf_op jit(solution)/shard_map/ppermute | solution.py:297
  80.6 1.1 %query_gradient_step1.1 = bf16[400,256]{1,0:T(8,128)(2,1)S(1)} custom-call(bf16[1024,400]{1,0:T(8,128)(2,1)S(1)} %get-tuple-element.19.turned_ref, bf16[400,1024]{1,0:T(8,128)(2,1)S(1)} %get-tuple-element.20.block_ref, bf16[416,256]{1,0:T(8,128)(2,1)S(1)} %collective-permute-done.6.q_ref.qa, f32[128,8]{1,0:T(8,128)S(1)} %get-tuple-element.27.column_ref), custom_call_target="tpu_custom_call" | custom-call | flops 419430400 | bytes 2060288 | tf_op jit(solution)/shard_map/query_gradient_step1/pallas_call | solution.py:273
  81.8 0.1 collective-permute-start.7
  81.9 13.4 %collective-permute-done.7.grad_ref = bf16[400,256]{1,0:T(8,128)(2,1)S(1)} collective-permute-done((bf16[400,256]{1,0:T(8,128)(2,1)S(1)}, bf16[400,256]{1,0:T(8,128)(2,1)S(1)}, u32[]{:S(2)}, u32[]{:S(2)}) %collective-permute-start.7) | collective-permute-done | bytes 204832 | tf_op jit(solution)/shard_map/ppermute | solution.py:297
  95.2 1.2 %source_step1.1 = f32[400,256]{1,0:T(8,128)} custom-call(bf16[400,256]{1,0:T(8,128)(2,1)S(1)} %collective-permute-done.7.grad_ref, bf16[400,256]{1,0:T(8,128)(2,1)S(1)} %get-tuple-element.25.rel1_ref.rel_ref, f32[400,256]{1,0:T(8,128)S(1)} %get-tuple-element.28.src_ref, f32[1,256]{1,0:T(1,128)S(1)} %get-tuple-element.29.state_ref, s32[2,256]{1,0:T(2,128)S(1)} %bitcast.19), custom_call_target="tpu_custom_call" | custom-call | bytes 1231872 | tf_op jit(solution)/shard_map/source_step1/pallas_call | solution.py:273
  96.4 0.0 collective-permute-done.12.other_ref
  96.4 0.0 copy-done.1
  96.4 1.3 %destination_out.1 = f32[400,1024]{1,0:T(8,128)} custom-call(f32[400,1024]{1,0:T(8,128)S(1)} %bitcast.14, bf16[400,512]{1,0:T(8,128)(2,1)S(1)} %collective-permute-done.11.own_ref, bf16[400,512]{1,0:T(8,128)(2,1)S(1)} %collective-permute-done.12.other_ref), custom_call_target="tpu_custom_call" | custom-call | bytes 4096000 | tf_op jit(solution)/shard_map/destination_out/pallas_call | solution.py:273
  (7 shorter events, 0.0 us)
Async XLA Ops:
  0.6 24.4 %copy-start.3 = (s32[1,2,256]{2,1,0:T(2,128)S(1)}, s32[1,2,256]{2,1,0:T(2,128)}, u32[]{:S(2)}) copy-start(s32[1,2,256]{2,1,0:T(2,128)} %param.14) | copy-start | bytes 6148
  0.6 1.4 %copy-start = (f32[1024,400]{0,1:T(8,128)S(1)}, f32[1024,400]{0,1:T(8,128)}, u32[]{:S(2)}) copy-start(f32[1024,400]{0,1:T(8,128)} %param.11) | copy-start | bytes 4915204
  2.1 0.7 copy-start.4
  2.8 22.3 %copy-start.2 = (f32[256,400]{0,1:T(8,128)S(1)}, f32[256,400]{0,1:T(8,128)}, u32[]{:S(2)}) copy-start(f32[256,400]{0,1:T(8,128)} %param.9) | copy-start | bytes 1228804
  2.8 22.3 %copy-start.5 = (s32[1,2,2048]{2,1,0:T(2,128)S(1)}, s32[1,2,2048]{2,1,0:T(2,128)}, u32[]{:S(2)}) copy-start(s32[1,2,2048]{2,1,0:T(2,128)} %param.17) | copy-start | bytes 49156
  2.8 22.3 %copy-start.6 = (s32[1,2,256]{2,1,0:T(2,128)S(1)}, s32[1,2,256]{2,1,0:T(2,128)}, u32[]{:S(2)}) copy-start(s32[1,2,256]{2,1,0:T(2,128)} %param.15) | copy-start | bytes 6148
  2.8 22.3 %copy-start.9 = (s32[1,2,256]{2,1,0:T(2,128)S(1)}, s32[1,2,256]{2,1,0:T(2,128)}, u32[]{:S(2)}) copy-start(s32[1,2,256]{2,1,0:T(2,128)} %param.16) | copy-start | bytes 6148
  2.9 20.9 %collective-permute-start = (bf16[416,512]{1,0:T(8,128)(2,1)S(1)}, bf16[416,512]{1,0:T(8,128)(2,1)S(1)}, u32[]{:S(2)}, u32[]{:S(2)}) collective-permute-start(bf16[416,512]{1,0:T(8,128)(2,1)S(1)} %cast_block.1), channel_id=1, source_target_pairs={{0,4},{1,5},{2,6},{3,7},{4,8},{5,9},{6,10},{7,11},{8,12},{9,13},{1... | collective-permute-start | bytes 1277960 | tf_op jit(solution)/shard_map/ppermute | solution.py:297
  23.8 9.4 %collective-permute-start.1 = (bf16[416,512]{1,0:T(8,128)(2,1)S(1)}, bf16[416,512]{1,0:T(8,128)(2,1)S(1)}, u32[]{:S(2)}, u32[]{:S(2)}) collective-permute-start(bf16[416,512]{1,0:T(8,128)(2,1)S(1)} %collective-permute-done.own_ref), channel_id=1, source_target_pairs={{0,1},{1,0},{2,3},{3,2},{4,5},{5,4},{6,7},{7,6},{8,9},{9,8},{10,11... | collective-permute-start | bytes 1277960 | tf_op jit(solution)/shard_map/ppermute | solution.py:297
  25.0 2.7 %copy-start.8 = (bf16[7424,400]{0,1:T(8,128)(2,1)S(1)}, bf16[7424,400]{0,1:T(8,128)(2,1)}, u32[]{:S(2)}) copy-start(bf16[7424,400]{0,1:T(8,128)(2,1)} %param.13) | copy-start | bytes 17817604
  27.7 5.5 %copy-start.7 = (f32[256]{0:T(256)S(1)}, f32[256]{0:T(256)}, u32[]{:S(2)}) copy-start(f32[256]{0:T(256)} %param.10) | copy-start | bytes 3076
  32.7 7.0 %collective-permute-start.2 = (bf16[416,256]{1,0:T(8,128)(2,1)S(1)}, bf16[416,256]{1,0:T(8,128)(2,1)S(1)}, u32[]{:S(2)}, u32[]{:S(2)}) collective-permute-start(bf16[416,256]{1,0:T(8,128)(2,1)S(1)} %get-tuple-element.17.qa), channel_id=1, source_target_pairs={{0,2},{1,3},{2,0},{3,1},{4,6},{5,7},{6,4},{7,5},{8,10},{9,11},{10,... | collective-permute-start | bytes 638984 | tf_op jit(solution)/shard_map/ppermute | solution.py:297
  34.9 6.6 %collective-permute-start.6 = (bf16[416,256]{1,0:T(8,128)(2,1)S(1)}, bf16[416,256]{1,0:T(8,128)(2,1)S(1)}, u32[]{:S(2)}, u32[]{:S(2)}) collective-permute-start(bf16[416,256]{1,0:T(8,128)(2,1)S(1)} %get-tuple-element.26), channel_id=1, source_target_pairs={{0,252},{1,253},{2,254},{3,255},{4,0},{5,1},{6,2},{7,3},{8,4},{9,5... | collective-permute-start | bytes 638984 | tf_op jit(solution)/shard_map/ppermute | solution.py:297
  37.1 9.8 %collective-permute-start.8 = (bf16[416,256]{1,0:T(8,128)(2,1)S(1)}, bf16[416,256]{1,0:T(8,128)(2,1)S(1)}, u32[]{:S(2)}, u32[]{:S(2)}) collective-permute-start(bf16[416,256]{1,0:T(8,128)(2,1)S(1)} %get-tuple-element.26), channel_id=1, source_target_pairs={{0,254},{1,255},{2,252},{3,253},{4,2},{5,3},{6,0},{7,1},{8,6},{9,7... | collective-permute-start | bytes 638984 | tf_op jit(solution)/shard_map/ppermute | solution.py:297
  37.1 19.0 %collective-permute-start.3 = (bf16[416,256]{1,0:T(8,128)(2,1)S(1)}, bf16[416,256]{1,0:T(8,128)(2,1)S(1)}, u32[]{:S(2)}, u32[]{:S(2)}) collective-permute-start(bf16[416,256]{1,0:T(8,128)(2,1)S(1)} %get-tuple-element.17.qa), channel_id=1, source_target_pairs={{0,1},{1,0},{2,3},{3,2},{4,5},{5,4},{6,7},{7,6},{8,9},{9,8},{10,11... | collective-permute-start | bytes 638984 | tf_op jit(solution)/shard_map/ppermute | solution.py:297
  39.7 16.4 %collective-permute-start.4 = (bf16[416,256]{1,0:T(8,128)(2,1)S(1)}, bf16[416,256]{1,0:T(8,128)(2,1)S(1)}, u32[]{:S(2)}, u32[]{:S(2)}) collective-permute-start(bf16[416,256]{1,0:T(8,128)(2,1)S(1)} %collective-permute-done.2.qb), channel_id=1, source_target_pairs={{0,1},{1,0},{2,3},{3,2},{4,5},{5,4},{6,7},{7,6},{8,9},{9,8},{10,11... | collective-permute-start | bytes 638984 | tf_op jit(solution)/shard_map/ppermute | solution.py:297
  41.6 19.7 %collective-permute-start.9 = (bf16[416,256]{1,0:T(8,128)(2,1)S(1)}, bf16[416,256]{1,0:T(8,128)(2,1)S(1)}, u32[]{:S(2)}, u32[]{:S(2)}) collective-permute-start(bf16[416,256]{1,0:T(8,128)(2,1)S(1)} %collective-permute-done.6.q_ref.qa), channel_id=1, source_target_pairs={{0,1},{1,0},{2,3},{3,2},{4,5},{5,4},{6,7},{7,6},{8,9},{9,8},{10,11... | collective-permute-start | bytes 638984 | tf_op jit(solution)/shard_map/ppermute | solution.py:297
  46.9 14.4 %collective-permute-start.10 = (bf16[416,256]{1,0:T(8,128)(2,1)S(1)}, bf16[416,256]{1,0:T(8,128)(2,1)S(1)}, u32[]{:S(2)}, u32[]{:S(2)}) collective-permute-start(bf16[416,256]{1,0:T(8,128)(2,1)S(1)} %collective-permute-done.8.qb), channel_id=1, source_target_pairs={{0,1},{1,0},{2,3},{3,2},{4,5},{5,4},{6,7},{7,6},{8,9},{9,8},{10,11... | collective-permute-start | bytes 638984 | tf_op jit(solution)/shard_map/ppermute | solution.py:297
  48.0 8.1 %collective-permute-start.5 = (s32[1,2048]{1,0:T(1,128)S(1)}, s32[1,2048]{1,0:T(1,128)S(1)}, u32[]{:S(2)}, u32[]{:S(2)}) collective-permute-start(s32[1,2048]{1,0:T(1,128)S(1)} %slice_bitcast_fusion), channel_id=1, source_target_pairs={{0,252},{1,253},{2,254},{3,255},{4,0},{5,1},{6,2},{7,3},{8,4},{9,5... | collective-permute-start | bytes 24584 | tf_op jit(solution)/shard_map/ppermute | solution.py:297
  63.4 15.1 %collective-permute-start.11 = (bf16[400,512]{1,0:T(8,128)(2,1)S(1)}, bf16[400,512]{1,0:T(8,128)(2,1)S(1)}, u32[]{:S(2)}, u32[]{:S(2)}) collective-permute-start(bf16[400,512]{1,0:T(8,128)(2,1)S(1)} %destination_step1.1), channel_id=1, source_target_pairs={{0,252},{1,253},{2,254},{3,255},{4,0},{5,1},{6,2},{7,3},{8,4},{9,5... | collective-permute-start | bytes 1228808 | tf_op jit(solution)/shard_map/ppermute | solution.py:297
  78.5 17.9 %collective-permute-start.12 = (bf16[400,512]{1,0:T(8,128)(2,1)S(1)}, bf16[400,512]{1,0:T(8,128)(2,1)S(1)}, u32[]{:S(2)}, u32[]{:S(2)}) collective-permute-start(bf16[400,512]{1,0:T(8,128)(2,1)S(1)} %collective-permute-done.11.own_ref), channel_id=1, source_target_pairs={{0,1},{1,0},{2,3},{3,2},{4,5},{5,4},{6,7},{7,6},{8,9},{9,8},{10,11... | collective-permute-start | bytes 1228808 | tf_op jit(solution)/shard_map/ppermute | solution.py:297
  80.6 15.8 %copy-start.1 = (f32[1024,400]{0,1:T(8,128)S(1)}, f32[1024,400]{0,1:T(8,128)}, u32[]{:S(2)}) copy-start(f32[1024,400]{0,1:T(8,128)} %param.11) | copy-start | bytes 4915204
  81.8 13.5 %collective-permute-start.7 = (bf16[400,256]{1,0:T(8,128)(2,1)S(1)}, bf16[400,256]{1,0:T(8,128)(2,1)S(1)}, u32[]{:S(2)}, u32[]{:S(2)}) collective-permute-start(bf16[400,256]{1,0:T(8,128)(2,1)S(1)} %query_gradient_step1.1), channel_id=1, source_target_pairs={{0,4},{1,5},{2,6},{3,7},{4,8},{5,9},{6,10},{7,11},{8,12},{9,13},{1... | collective-permute-start | bytes 614408 | tf_op jit(solution)/shard_map/ppermute | solution.py:297

commit v2 on v1

--- a/solution.py
+++ b/solution.py
@@ -14,6 +14,7 @@
 META = 16
 FINE = 32
 LANES = 128
+PIECE = 1920
 
 
 def dot(a, b):
@@ -78,12 +79,15 @@
     return state, LEARNING_RATE / jnp.sqrt(state)
 
 
-def cast_kernel(emb_ref, state_ref, out_ref, held, sem):
+def cast_kernel(emb_ref, state_ref, out_ref, held, held_state, sems):
     depth, half = held.shape
     columns = pl.ds(pl.multiple_of(core() * half, half), half)
-    copy = pltpu.make_async_copy(emb_ref.at[:, columns], held, sem)
+    copy = pltpu.make_async_copy(emb_ref.at[:, columns], held, sems.at[0])
+    copy_state = pltpu.make_async_copy(state_ref.at[:, columns], held_state, sems.at[1])
     copy.start()
-    state = state_ref[:, columns]
+    copy_state.start()
+    copy_state.wait()
+    state = held_state[...]
     high = state.astype(BF).astype(F32)
     out_ref[depth:, :] = two_rows(high, state - high, half)
     copy.wait()
@@ -94,33 +98,35 @@
     return one_hot(blocks, lax.div(index, LANES)), one_hot(LANES, lax.rem(index, LANES))
 
 
+def count_rows(index, blocks):
+    coarse, fine = count_grid(index, blocks)
+    return dot_nt(coarse, fine)
+
+
 def prep_kernel(
-    chunks, rows, rel_ref, src_ref, src_index, dst_index, rel_index, neg_index,
-    q_ref, qt_ref, at_ref, rel0_ref, rel1_ref, count_ref, column_ref, held, sems,
+    rows, rel_ref, src_ref, src_index, dst_index, rel_index, neg_index,
+    q_ref, qt_ref, at_ref, rel0_ref, rel1_ref, count_ref, column_ref, next_ref,
 ):
     depth, edges = src_ref.shape
-    copies = []
-    start = 0
-    for i, size in enumerate(chunks):
-        part = pl.ds(start, size)
-        copies.append(pltpu.make_async_copy(rel_ref.at[:, part], held.at[:, part], sems.at[i]))
-        copies[-1].start()
-        start += size
-
+    relations = rel_ref.shape[1]
+    blocks = rows // LANES
     flip = core() * (rows // 2)
-    coarse, fine = count_grid(neg_index[0:1, :] ^ flip, rows // LANES)
+    coarse, fine = count_grid(neg_index[0:1, :] ^ flip, blocks)
     counts = dot_nt(coarse, fine)
-    for i in range(rows // LANES):
+    for i in range(blocks):
         count_ref[:, i * LANES : (i + 1) * LANES] = counts[i : i + 1, :]
     column_ref[...] = dot_nt(fine, coarse)
+    counts = count_rows(neg_index[1:2, :] ^ flip, blocks)
+    high = jnp.floor(counts * (1.0 / FINE))
+    next_ref[...] = jnp.concatenate([high, counts - high * FINE], axis=0)
 
     src_rows = picked(src_ref[...], one_hot(edges, src_index[0:1, :]))
     which = jnp.concatenate([rel_index[0:1, :], rel_index[1:2, :]], axis=1)
     block = lax.div(which, LANES)
     within = one_hot(LANES, lax.rem(which, LANES))
     found = jnp.zeros((depth, 2 * edges), F32)
-    start = 0
-    for copy, size in zip(copies, chunks):
+    for start in range(0, relations, PIECE):
+        size = min(PIECE, relations - start)
         hot = jnp.concatenate(
             [
                 within * (block == start // LANES + i).astype(F32).astype(BF)
@@ -128,9 +134,7 @@
             ],
             axis=0,
         )
-        copy.wait()
-        found = found + dot(held[:, start : start + size], hot)
-        start += size
+        found = found + dot(rel_ref[:, start : start + size], hot)
     rel0_ref[...] = found[:, :edges].astype(BF)
     rel1_ref[...] = found[:, edges:].astype(BF)
     query = (src_rows * found[:, :edges]).astype(BF)
@@ -146,7 +150,7 @@
 
 def src0_kernel(
     negatives, own_ref, other_ref, qt_ref, at_ref, count_ref, src_ref, state_ref,
-    rel0_ref, rel1_ref, src_index, dst_index, q_ref, src_out, state_out,
+    rel0_ref, rel1_ref, src_index, dst_index, next_ref, q_ref, src_out, state_out,
 ):
     depth, edges = src_ref.shape
     half = own_ref.shape[1]
@@ -166,12 +170,22 @@
     state_out[...] = state
     rows = picked(src, one_hot(edges, src_index[1:2, :]))
     q_ref[:depth, :] = (rows * rel1_ref[...].astype(F32)).astype(BF)
-    q_ref[depth:, :] = index_rows(dst_index[1:2, :])
+    blocks = next_ref.shape[0] // 2
+    counts = jnp.concatenate([next_ref[:blocks, :], next_ref[blocks:, :]], axis=1)
+    gap = jnp.zeros((META // 2, edges), F32)
+    meta = index_rows(dst_index[1:2, :]).astype(F32)
+    q_ref[depth:, :] = (meta + jnp.concatenate([gap, counts], axis=0)).astype(BF)
 
 
 def targets(q_ref, depth, flip):
     parts = q_ref[depth:, :].astype(F32)
     return (parts[0:1, :] * FINE + parts[1:2, :]).astype(I32) ^ flip
+
+
+def sent_counts(q_ref, depth):
+    parts = dot_nt(eye(LANES), q_ref[depth:, :LANES]) * FINE
+    parts = parts + dot_nt(eye(LANES), q_ref[depth:, LANES : 2 * LANES])
+    return parts[:, META // 2 :]
 
 
 def row_coefficients(block_t, start, q_ref, column, flip, negatives):
@@ -195,8 +209,8 @@
 
 
 def dst0_kernel(
-    negatives, own_ref, other_ref, qa, qb, qc, qd, column_ref, neg_index,
-    block_out, turned_out, delta_out, state_out, column_out,
+    negatives, own_ref, other_ref, qa, qb, qc, qd, column_ref,
+    block_out, turned_out, delta_out, state_out,
 ):
     depth, half = delta_out.shape
     flip = core() * half
@@ -224,26 +238,24 @@
         if i == 0:
             delta_out[...] = delta
             state_out[...] = state
-    coarse, fine = count_grid(neg_index[...] ^ flip, 2 * half // LANES)
-    column_out[...] = dot_nt(fine, coarse)
 
 
 def dst1_kernel(
-    negatives, turned_ref, qa, qb, qc, qd, column_ref, delta_ref, state_ref, delta_out
+    negatives, turned_ref, qa, qb, qc, qd, delta_ref, state_ref, delta_out
 ):
-    half = delta_ref.shape[1]
+    depth, half = delta_ref.shape
     flip = core() * half
     gradient = dst_gradient(
-        turned_ref[:half, :], 0, (qa, qb, qc, qd), column_ref[...], flip, negatives
+        turned_ref[:half, :], 0, (qa, qb, qc, qd), sent_counts(qa, depth), flip, negatives
     )
     _, size = step_size(state_ref[...], gradient)
     delta_out[...] = (delta_ref[...] + gradient * size).astype(BF)
 
 
-def query1_kernel(negatives, turned_ref, block_ref, q_ref, column_ref, out_ref):
-    rows = turned_ref.shape[0]
+def query1_kernel(negatives, turned_ref, block_ref, q_ref, out_ref):
+    rows, depth = turned_ref.shape
     weights = row_coefficients(
-        turned_ref[...], 0, q_ref, column_ref[...], core() * (rows // 2), negatives
+        turned_ref[...], 0, q_ref, sent_counts(q_ref, depth), core() * (rows // 2), negatives
     )
     out_ref[...] = dot(block_ref[...], weights).astype(BF)
 
@@ -299,7 +311,6 @@
     rows, depth = dst_emb.shape
     edges = src_emb.shape[0]
     half = rows // 2
-    relation_count = relations.shape[0]
     src_index, dst_index, rel_index, neg_index = (
         a[0] for a in (src_index, dst_index, rel_index, neg_index)
     )
@@ -312,18 +323,21 @@
         [((tall, half), BF)],
         [dst, dst_state.reshape(1, rows)],
         "cast_block",
-        scratch=[pltpu.VMEM((depth, half), F32), pltpu.SemaphoreType.DMA],
-        hbm=(0,),
-        limit=8,
+        scratch=[
+            pltpu.VMEM((depth, half), F32),
+            pltpu.VMEM((1, half), F32),
+            pltpu.SemaphoreType.DMA((2,)),
+        ],
+        hbm=(0, 1),
+        limit=60,
     )
     own = moved(payload, along=1)
-    negs_next = moved(neg_index[1:2, :], along=-1)
-
-    pieces = relation_count // (2 * LANES)
-    chunks = [(pieces // 4 + (i < pieces % 4)) * 2 * LANES for i in range(4)]
-    chunks[-1] += relation_count - sum(chunks)
-    query, query_t, target_at, rel0, rel1, count, column = call(
-        functools.partial(prep_kernel, tuple(chunks), rows),
+    rel, payload = lax.optimization_barrier((rel, payload))
+
+    src_state = src_state.reshape(1, edges)
+    blocks = rows // LANES
+    query, query_t, target_at, rel0, rel1, count, column, count1 = call(
+        functools.partial(prep_kernel, rows),
         [
             ((tall, edges), BF),
             ((edges, depth), BF),
@@ -331,68 +345,69 @@
             ((depth, edges), BF),
             ((depth, edges), BF),
             ((1, rows), F32),
-            ((LANES, rows // LANES), F32),
+            ((LANES, blocks), F32),
+            ((2 * blocks, LANES), F32),
         ],
         [rel, src, src_index, dst_index, rel_index, neg_index],
         "relation_rows",
-        flops=4 * depth * edges * relation_count,
-        scratch=[pltpu.VMEM((depth, relation_count), BF), pltpu.SemaphoreType.DMA((4,))],
-        hbm=(0,),
-        limit=40,
-    )
+        flops=4 * depth * edges * relations.shape[0],
+        limit=32,
+    )
+    query_c, query_y = moved(query, to=1), moved(query, to=2)
+    own, query_y, query_c = lax.optimization_barrier((own, query_y, query_c))
     other = moved(own, to=1)
-    query_y = moved(query, to=2)
-    query_c, query_cy = moved(query, to=1), moved(query_y, to=1)
+    query_cy = moved(query_y, to=1)
 
     matmul = 2 * edges * rows * depth
     query1, src1, src_state1 = call(
         functools.partial(src0_kernel, negatives),
         [((tall, edges), BF), ((depth, edges), F32), ((1, edges), F32)],
         [
-            own, other, query_t, target_at, count, src, src_state.reshape(1, edges),
-            rel0, rel1, src_index, dst_index,
+            own, other, query_t, target_at, count, src, src_state,
+            rel0, rel1, src_index, dst_index, count1,
         ],
         "source_step0",
         flops=2 * matmul,
         limit=24,
     )
     next_own, next_y = moved(query1, along=-1), moved(query1, along=-1, to=2)
-
-    block1, turned1, delta0, dst_state1, column1 = call(
+    own, query1 = lax.optimization_barrier((own, query1))
+
+    block1, turned1, delta0, dst_state1 = call(
         functools.partial(dst0_kernel, negatives),
         [
             ((depth, rows), BF),
             ((rows, depth), BF),
             ((depth, half), F32),
             ((1, half), F32),
-            ((LANES, rows // LANES), F32),
         ],
-        [own, other, query, query_y, query_c, query_cy, column, negs_next],
+        [own, other, query, query_y, query_c, query_cy, column],
         "destination_step0",
         flops=8 * matmul,
         limit=32,
     )
+    next_own, next_y, block1 = lax.optimization_barrier((next_own, next_y, block1))
     next_c, next_cy = moved(next_own, to=1), moved(next_y, to=1)
 
     delta = call(
         functools.partial(dst1_kernel, negatives),
         [((depth, half), BF)],
-        [turned1, next_own, next_y, next_c, next_cy, column1, delta0, dst_state1],
+        [turned1, next_own, next_y, next_c, next_cy, delta0, dst_state1],
         "destination_step1",
         flops=4 * matmul,
         limit=24,
     )
     home_own = moved(delta, along=-1)
+    block1, delta = lax.optimization_barrier((block1, delta))
     query_grad = call(
         functools.partial(query1_kernel, negatives),
         [((depth, edges), BF)],
-        [turned1, block1, next_own, column1],
+        [turned1, block1, next_own],
         "query_gradient_step1",
         flops=2 * matmul,
         limit=24,
     )
     home_grad = moved(query_grad, along=1)
-    home_other = moved(home_own, to=1)
     src_out = call(
         src1_kernel,
         [((depth, edges), F32)],
@@ -400,6 +415,8 @@
         "source_step1",
         limit=16,
     )
+    home_own, src_out = lax.optimization_barrier((home_own, src_out))
+    home_other = moved(home_own, to=1)
     dst_out = call(
         final_kernel,
         [((depth, rows), F32)],

time: 97.9 us -> 72.1 us (0.74)
  waiting for transfers between devices: 46.4 us -> 32.5 us
  starting transfers between devices: 27.9 us -> 17.4 us
  local copies, waits for them, and re-layouts: 4.83 us -> 2.71 us
    ppermute x13 -> x12, waiting for transfers between devices: 46.4 us -> 32.5 us  [moved(): return lax.ppermute(value, ('wide', 'narrow'), pairs)]
    ppermute x13 -> x12, starting transfers between devices: 27.9 us -> 17.4 us  [moved(): return lax.ppermute(value, ('wide', 'narrow'), pairs)]
    unnamed x20 -> x16, local copies, waits for them, and re-layouts: 4.82 us -> 2.71 us
  transfers between devices with their start and end apart: 13 -> 12, of which waited for: 7 -> 7; matrix products, arithmetic and copies ran while one was open for 0% -> 0% of each run, Pallas kernels for 14% -> 18%
where the time goes in v2:
time: 72.1 us; the launch traced here: 71.9 us
  waiting for transfers between devices  32.5 us (45%)
  Pallas kernels  18.6 us (26%)
  starting transfers between devices  17.4 us (24%)
  local copies, waits for them, and re-layouts  2.71 us (4%)
  between operations  0.77 us (1%)
    ppermute x12, waiting for transfers between devices, moved(): return lax.ppermute(value, ('wide', 'narrow'), pairs)  32.5 us
    pallas_call x8, Pallas kernels, call(): pl.pallas_call(kernel, out_shape=shapes, in_specs=[anywhere if i in hbm e...  18.6 us
    ppermute x12, starting transfers between devices, moved(): return lax.ppermute(value, ('wide', 'narrow'), pairs)  17.4 us
    unnamed x16, local copies, waits for them, and re-layouts  2.71 us
  transfers between devices with their start and end apart: 12, of which 7 were waited for; matrix products, arithmetic and copies ran while one was open for 0% of the time, Pallas kernels for 18%

profile of v2, /device:TPU:1, one launch (start us, length us, event | category | flops | bytes accessed | tf_op | source)
XLA Modules:
  0.0 71.9 jit_solution(508831162154270245)
XLA Ops:
  0.6 0.0 copy-start.2
  0.6 0.0 copy-start.1
  0.7 0.0 copy-start.3
  0.7 0.0 copy-start.7
  0.7 0.0 copy-start.6
  0.7 2.0 %cast_block.1 = bf16[416,512]{1,0:T(8,128)(2,1)} custom-call(f32[400,1024]{1,0:T(8,128)} %bitcast.11, f32[1,1024]{1,0:T(1,128)} %bitcast.26), custom_call_target="tpu_custom_call" | custom-call | bytes 2068480 | tf_op jit(solution)/shard_map/cast_block/pallas_call | solution.py:285
  2.7 2.5 %collective-permute-start = (bf16[416,512]{1,0:T(8,128)(2,1)}, bf16[416,512]{1,0:T(8,128)(2,1)S(1)}, u32[]{:S(2)}, u32[]{:S(2)}) collective-permute-start(bf16[416,512]{1,0:T(8,128)(2,1)} %cast_block.1), channel_id=1, source_target_pairs={{0,4},{1,5},{2,6},{3,7},{4,8},{5,9},{6,10},{7,11},{8,12},{9,13},{1... | collective-permute-start | bytes 1277960 | tf_op jit(solution)/shard_map/ppermute | solution.py:309
  5.2 0.0 copy-done.2
  5.2 0.0 copy-done.1
  5.3 0.0 copy-done.3
  5.3 0.0 copy-done.7
  5.3 0.0 copy-done.6
  5.3 0.0 copy-start.5
  5.3 2.7 %copy-done.5 = bf16[7424,400]{0,1:T(8,128)(2,1)S(1)} copy-done((bf16[7424,400]{0,1:T(8,128)(2,1)S(1)}, bf16[7424,400]{0,1:T(8,128)(2,1)}, u32[]{:S(2)}) %copy-start.5) | copy-done | bytes 5939224
  8.0 0.0 copy-start.4
  8.0 4.3 %relation_rows.1 = (bf16[416,256]{1,0:T(8,128)(2,1)S(1)}, bf16[256,400]{1,0:T(8,128)(2,1)S(1)}, s32[256,128]{1,0:T(8,128)S(1)}, bf16[400,256]{1,0:T(8,128)(2,1)S...) custom-call(bf16[400,7424]{1,0:T(8,128)(2,1)S(1)} %bitcast.21, ...), custom_call_target="tpu_custom_call" | custom-call | flops 3040870400 | bytes 7346176 | tf_op jit(solution)/shard_map/relation_rows/pallas_call | solution.py:285
  12.2 1.4 %collective-permute-start.1 = (bf16[416,256]{1,0:T(8,128)(2,1)S(1)}, bf16[416,256]{1,0:T(8,128)(2,1)S(1)}, u32[]{:S(2)}, u32[]{:S(2)}) collective-permute-start(bf16[416,256]{1,0:T(8,128)(2,1)S(1)} %get-tuple-element.29.qa), channel_id=1, source_target_pairs={{0,2},{1,3},{2,0},{3,1},{4,6},{5,7},{6,4},{7,5},{8,10},{9,11},{10,... | collective-permute-start | bytes 638984 | tf_op jit(solution)/shard_map/ppermute | solution.py:309
  13.6 1.2 %collective-permute-start.2 = (bf16[416,256]{1,0:T(8,128)(2,1)S(1)}, bf16[416,256]{1,0:T(8,128)(2,1)S(1)}, u32[]{:S(2)}, u32[]{:S(2)}) collective-permute-start(bf16[416,256]{1,0:T(8,128)(2,1)S(1)} %get-tuple-element.29.qa), channel_id=1, source_target_pairs={{0,1},{1,0},{2,3},{3,2},{4,5},{5,4},{6,7},{7,6},{8,9},{9,8},{10,11... | collective-permute-start | bytes 638984 | tf_op jit(solution)/shard_map/ppermute | solution.py:309
  14.9 12.6 %collective-permute-done.1.qb = bf16[416,256]{1,0:T(8,128)(2,1)S(1)} collective-permute-done((bf16[416,256]{1,0:T(8,128)(2,1)S(1)}, bf16[416,256]{1,0:T(8,128)(2,1)S(1)}, u32[]{:S(2)}, u32[]{:S(2)}) %collective-permute-start.1) | collective-permute-done | bytes 213024 | tf_op jit(solution)/shard_map/ppermute | solution.py:309
  27.4 0.0 collective-permute-done.2.qc
  27.4 0.0 collective-permute-done.own_ref
  27.5 0.5 collective-permute-start.3
  27.9 0.1 collective-permute-start.4
  28.0 1.3 %collective-permute-done.3.other_ref = bf16[416,512]{1,0:T(8,128)(2,1)S(1)} collective-permute-done((bf16[416,512]{1,0:T(8,128)(2,1)S(1)}, bf16[416,512]{1,0:T(8,128)(2,1)S(1)}, u32[]{:S(2)}, u32[]{:S(2)}) %collective-permute-start.3) | collective-permute-done | bytes 426016 | tf_op jit(solution)/shard_map/ppermute | solution.py:309
  29.3 0.0 copy-done.4
  29.3 1.7 %source_step0.1 = (bf16[416,256]{1,0:T(8,128)(2,1)S(1)}, f32[400,256]{1,0:T(8,128)S(1)}, f32[1,256]{1,0:T(1,128)S(1)}) custom-call(bf16[416,512]{1,0:T(8,128)(2,1)S(1)} %collective-permute-done.own_ref, bf16[416,512]{1,0:T(8,128)(2,1)S(1)} %collective-permute-done.3.other_ref, bf16[256,400]{1,0:T(8,128)(2,1)S(1)} %get-tuple-element.31.qt_ref, ...), custom_call_target="tpu_custom_call" | custom-call | flops 419430400 | bytes 2648064 | tf_op jit(solution)/shard_map/source_step0/pallas_call | solution.py:285
  31.1 0.9 %collective-permute-start.5 = (bf16[416,256]{1,0:T(8,128)(2,1)S(1)}, bf16[416,256]{1,0:T(8,128)(2,1)S(1)}, u32[]{:S(2)}, u32[]{:S(2)}) collective-permute-start(bf16[416,256]{1,0:T(8,128)(2,1)S(1)} %get-tuple-element.37), channel_id=1, source_target_pairs={{0,252},{1,253},{2,254},{3,255},{4,0},{5,1},{6,2},{7,3},{8,4},{9,5... | collective-permute-start | bytes 638984 | tf_op jit(solution)/shard_map/ppermute | solution.py:309
  32.0 1.2 %collective-permute-start.6 = (bf16[416,256]{1,0:T(8,128)(2,1)S(1)}, bf16[416,256]{1,0:T(8,128)(2,1)S(1)}, u32[]{:S(2)}, u32[]{:S(2)}) collective-permute-start(bf16[416,256]{1,0:T(8,128)(2,1)S(1)} %get-tuple-element.37), channel_id=1, source_target_pairs={{0,254},{1,255},{2,252},{3,253},{4,2},{5,3},{6,0},{7,1},{8,6},{9,7... | collective-permute-start | bytes 638984 | tf_op jit(solution)/shard_map/ppermute | solution.py:309
  33.2 0.0 collective-permute-done.4.qd
  33.2 4.8 %destination_step0.1 = (bf16[400,1024]{1,0:T(8,128)(2,1)S(1)}, bf16[1024,400]{1,0:T(8,128)(2,1)S(1)}, f32[400,512]{1,0:T(8,128)S(1)}, f32[1,512]{1,0:T(1,128)S(1)}) custom-call(bf16[416,512]{1,0:T(8,128)(2,1)S(1)} %collective-permute-done.own_ref, bf16[416,512]{1,0:T(8,128)(2,1)S(1)} %collective-permute-done.3.other_ref, ...), custom_call_target="tpu_custom_call" | custom-call | flops 1677721600 | bytes 4167680 | tf_op jit(solution)/shard_map/destination_step0/pallas_call | solution.py:285
  38.1 0.0 collective-permute-done.5.qa.q_ref
  38.1 4.0 %collective-permute-done.6.qb = bf16[416,256]{1,0:T(8,128)(2,1)S(1)} collective-permute-done((bf16[416,256]{1,0:T(8,128)(2,1)S(1)}, bf16[416,256]{1,0:T(8,128)(2,1)S(1)}, u32[]{:S(2)}, u32[]{:S(2)}) %collective-permute-start.6) | collective-permute-done | bytes 213024 | tf_op jit(solution)/shard_map/ppermute | solution.py:309
  42.1 1.2 %collective-permute-start.7 = (bf16[416,256]{1,0:T(8,128)(2,1)S(1)}, bf16[416,256]{1,0:T(8,128)(2,1)S(1)}, u32[]{:S(2)}, u32[]{:S(2)}) collective-permute-start(bf16[416,256]{1,0:T(8,128)(2,1)S(1)} %collective-permute-done.5.qa.q_ref), channel_id=1, source_target_pairs={{0,1},{1,0},{2,3},{3,2},{4,5},{5,4},{6,7},{7,6},{8,9},{9,8},{10,11... | collective-permute-start | bytes 638984 | tf_op jit(solution)/shard_map/ppermute | solution.py:309
  43.3 0.0 collective-permute-start.8
  43.3 1.1 %collective-permute-done.7.qc = bf16[416,256]{1,0:T(8,128)(2,1)S(1)} collective-permute-done((bf16[416,256]{1,0:T(8,128)(2,1)S(1)}, bf16[416,256]{1,0:T(8,128)(2,1)S(1)}, u32[]{:S(2)}, u32[]{:S(2)}) %collective-permute-start.7) | collective-permute-done | bytes 213024 | tf_op jit(solution)/shard_map/ppermute | solution.py:309
  44.4 0.4 collective-permute-done.8.qd
  44.7 2.1 %destination_step1.1 = bf16[400,512]{1,0:T(8,128)(2,1)S(1)} custom-call(bf16[1024,400]{1,0:T(8,128)(2,1)S(1)} %get-tuple-element.42.turned_ref, bf16[416,256]{1,0:T(8,128)(2,1)S(1)} %collective-permute-done.5.qa.q_ref, bf16[416,256]{1,0:T(8,128)(2,1)S(1)} %collective-permute-done.6.qb, bf16[416,256]{1,0:T(8,128)(2,1)S(1)} %collective-permute-done.7.qc, ...), custom_call_target="tpu_custom_call" | custom-call | flops 838860800 | bytes 2902016 | tf_op jit(solution)/shard_map/destination_step1/pallas_call | solution.py:285
  46.9 0.0 copy-start
  46.9 6.8 %collective-permute-start.9 = (bf16[400,512]{1,0:T(8,128)(2,1)S(1)}, bf16[400,512]{1,0:T(8,128)(2,1)S(1)}, u32[]{:S(2)}, u32[]{:S(2)}) collective-permute-start(bf16[400,512]{1,0:T(8,128)(2,1)S(1)} %destination_step1.1), channel_id=1, source_target_pairs={{0,252},{1,253},{2,254},{3,255},{4,0},{5,1},{6,2},{7,3},{8,4},{9,5... | collective-permute-start | bytes 1228808 | tf_op jit(solution)/shard_map/ppermute | solution.py:309
  53.6 1.1 %query_gradient_step1.1 = bf16[400,256]{1,0:T(8,128)(2,1)S(1)} custom-call(bf16[1024,400]{1,0:T(8,128)(2,1)S(1)} %get-tuple-element.42.turned_ref, bf16[400,1024]{1,0:T(8,128)(2,1)S(1)} %get-tuple-element.49.block_ref, bf16[416,256]{1,0:T(8,128)(2,1)S(1)} %collective-permute-done.5.qa.q_ref), custom_call_target="tpu_custom_call" | custom-call | flops 419430400 | bytes 2056192 | tf_op jit(solution)/shard_map/query_gradient_step1/pallas_call | solution.py:285
  54.8 0.1 collective-permute-start.10
  54.9 11.8 %collective-permute-done.10.grad_ref = bf16[400,256]{1,0:T(8,128)(2,1)S(1)} collective-permute-done((bf16[400,256]{1,0:T(8,128)(2,1)S(1)}, bf16[400,256]{1,0:T(8,128)(2,1)S(1)}, u32[]{:S(2)}, u32[]{:S(2)}) %collective-permute-start.10) | collective-permute-done | bytes 204832 | tf_op jit(solution)/shard_map/ppermute | solution.py:309
  66.6 1.2 %source_step1.1 = f32[400,256]{1,0:T(8,128)} custom-call(bf16[400,256]{1,0:T(8,128)(2,1)S(1)} %collective-permute-done.10.grad_ref, bf16[400,256]{1,0:T(8,128)(2,1)S(1)} %get-tuple-element.35.rel1_ref.rel_ref, f32[400,256]{1,0:T(8,128)S(1)} %get-tuple-element.50.src_ref, f32[1,256]{1,0:T(1,128)S(1)} %get-tuple-element.51.state_ref, s32[2,256]{1,0:T(2,128)S(1)} %bitcast.17), custom_call_target="tpu_custom_call" | custom-call | bytes 1231872 | tf_op jit(solution)/shard_map/source_step1/pallas_call | solution.py:285
  67.8 0.0 collective-permute-done.9.own_ref
  67.8 1.4 %collective-permute-start.11 = (bf16[400,512]{1,0:T(8,128)(2,1)S(1)}, bf16[400,512]{1,0:T(8,128)(2,1)S(1)}, u32[]{:S(2)}, u32[]{:S(2)}) collective-permute-start(bf16[400,512]{1,0:T(8,128)(2,1)S(1)} %collective-permute-done.9.own_ref), channel_id=1, source_target_pairs={{0,1},{1,0},{2,3},{3,2},{4,5},{5,4},{6,7},{7,6},{8,9},{9,8},{10,11... | collective-permute-start | bytes 1228808 | tf_op jit(solution)/shard_map/ppermute | solution.py:309
  69.2 1.4 %collective-permute-done.11.other_ref = bf16[400,512]{1,0:T(8,128)(2,1)S(1)} collective-permute-done((bf16[400,512]{1,0:T(8,128)(2,1)S(1)}, bf16[400,512]{1,0:T(8,128)(2,1)S(1)}, u32[]{:S(2)}, u32[]{:S(2)}) %collective-permute-start.11) | collective-permute-done | bytes 409632 | tf_op jit(solution)/shard_map/ppermute | solution.py:309
  70.6 0.0 copy-done
  70.6 1.3 %destination_out.1 = f32[400,1024]{1,0:T(8,128)} custom-call(f32[400,1024]{1,0:T(8,128)S(1)} %bitcast.12, bf16[400,512]{1,0:T(8,128)(2,1)S(1)} %collective-permute-done.9.own_ref, bf16[400,512]{1,0:T(8,128)(2,1)S(1)} %collective-permute-done.11.other_ref), custom_call_target="tpu_custom_call" | custom-call | bytes 4096000 | tf_op jit(solution)/shard_map/destination_out/pallas_call | solution.py:285
Async XLA Ops:
  0.6 4.6 %copy-start.2 = (s32[1,2,256]{2,1,0:T(2,128)S(1)}, s32[1,2,256]{2,1,0:T(2,128)}, u32[]{:S(2)}) copy-start(s32[1,2,256]{2,1,0:T(2,128)} %param.14) | copy-start | bytes 6148
  0.6 4.6 %copy-start.1 = (f32[256,400]{0,1:T(8,128)S(1)}, f32[256,400]{0,1:T(8,128)}, u32[]{:S(2)}) copy-start(f32[256,400]{0,1:T(8,128)} %param.9) | copy-start | bytes 1228804
  0.7 4.6 %copy-start.3 = (s32[1,2,256]{2,1,0:T(2,128)S(1)}, s32[1,2,256]{2,1,0:T(2,128)}, u32[]{:S(2)}) copy-start(s32[1,2,256]{2,1,0:T(2,128)} %param.15) | copy-start | bytes 6148
  0.7 4.6 %copy-start.7 = (s32[1,2,256]{2,1,0:T(2,128)S(1)}, s32[1,2,256]{2,1,0:T(2,128)}, u32[]{:S(2)}) copy-start(s32[1,2,256]{2,1,0:T(2,128)} %param.16) | copy-start | bytes 6148
  0.7 4.6 %copy-start.6 = (s32[1,2,2048]{2,1,0:T(2,128)S(1)}, s32[1,2,2048]{2,1,0:T(2,128)}, u32[]{:S(2)}) copy-start(s32[1,2,2048]{2,1,0:T(2,128)} %param.17) | copy-start | bytes 49156
  2.7 24.7 %collective-permute-start = (bf16[416,512]{1,0:T(8,128)(2,1)}, bf16[416,512]{1,0:T(8,128)(2,1)S(1)}, u32[]{:S(2)}, u32[]{:S(2)}) collective-permute-start(bf16[416,512]{1,0:T(8,128)(2,1)} %cast_block.1), channel_id=1, source_target_pairs={{0,4},{1,5},{2,6},{3,7},{4,8},{5,9},{6,10},{7,11},{8,12},{9,13},{1... | collective-permute-start | bytes 1277960 | tf_op jit(solution)/shard_map/ppermute | solution.py:309
  5.3 2.7 %copy-start.5 = (bf16[7424,400]{0,1:T(8,128)(2,1)S(1)}, bf16[7424,400]{0,1:T(8,128)(2,1)}, u32[]{:S(2)}) copy-start(bf16[7424,400]{0,1:T(8,128)(2,1)} %param.13) | copy-start | bytes 17817604
  8.0 21.4 %copy-start.4 = (f32[256]{0:T(256)S(1)}, f32[256]{0:T(256)}, u32[]{:S(2)}) copy-start(f32[256]{0:T(256)} %param.10) | copy-start | bytes 3076
  12.2 15.2 %collective-permute-start.1 = (bf16[416,256]{1,0:T(8,128)(2,1)S(1)}, bf16[416,256]{1,0:T(8,128)(2,1)S(1)}, u32[]{:S(2)}, u32[]{:S(2)}) collective-permute-start(bf16[416,256]{1,0:T(8,128)(2,1)S(1)} %get-tuple-element.29.qa), channel_id=1, source_target_pairs={{0,2},{1,3},{2,0},{3,1},{4,6},{5,7},{6,4},{7,5},{8,10},{9,11},{10,... | collective-permute-start | bytes 638984 | tf_op jit(solution)/shard_map/ppermute | solution.py:309
  13.6 13.8 %collective-permute-start.2 = (bf16[416,256]{1,0:T(8,128)(2,1)S(1)}, bf16[416,256]{1,0:T(8,128)(2,1)S(1)}, u32[]{:S(2)}, u32[]{:S(2)}) collective-permute-start(bf16[416,256]{1,0:T(8,128)(2,1)S(1)} %get-tuple-element.29.qa), channel_id=1, source_target_pairs={{0,1},{1,0},{2,3},{3,2},{4,5},{5,4},{6,7},{7,6},{8,9},{9,8},{10,11... | collective-permute-start | bytes 638984 | tf_op jit(solution)/shard_map/ppermute | solution.py:309
  27.5 1.9 %collective-permute-start.3 = (bf16[416,512]{1,0:T(8,128)(2,1)S(1)}, bf16[416,512]{1,0:T(8,128)(2,1)S(1)}, u32[]{:S(2)}, u32[]{:S(2)}) collective-permute-start(bf16[416,512]{1,0:T(8,128)(2,1)S(1)} %collective-permute-done.own_ref), channel_id=1, source_target_pairs={{0,1},{1,0},{2,3},{3,2},{4,5},{5,4},{6,7},{7,6},{8,9},{9,8},{10,11... | collective-permute-start | bytes 1277960 | tf_op jit(solution)/shard_map/ppermute | solution.py:309
  27.9 5.3 %collective-permute-start.4 = (bf16[416,256]{1,0:T(8,128)(2,1)S(1)}, bf16[416,256]{1,0:T(8,128)(2,1)S(1)}, u32[]{:S(2)}, u32[]{:S(2)}) collective-permute-start(bf16[416,256]{1,0:T(8,128)(2,1)S(1)} %collective-permute-done.1.qb), channel_id=1, source_target_pairs={{0,1},{1,0},{2,3},{3,2},{4,5},{5,4},{6,7},{7,6},{8,9},{9,8},{10,11... | collective-permute-start | bytes 638984 | tf_op jit(solution)/shard_map/ppermute | solution.py:309
  31.1 7.0 %collective-permute-start.5 = (bf16[416,256]{1,0:T(8,128)(2,1)S(1)}, bf16[416,256]{1,0:T(8,128)(2,1)S(1)}, u32[]{:S(2)}, u32[]{:S(2)}) collective-permute-start(bf16[416,256]{1,0:T(8,128)(2,1)S(1)} %get-tuple-element.37), channel_id=1, source_target_pairs={{0,252},{1,253},{2,254},{3,255},{4,0},{5,1},{6,2},{7,3},{8,4},{9,5... | collective-permute-start | bytes 638984 | tf_op jit(solution)/shard_map/ppermute | solution.py:309
  32.0 10.1 %collective-permute-start.6 = (bf16[416,256]{1,0:T(8,128)(2,1)S(1)}, bf16[416,256]{1,0:T(8,128)(2,1)S(1)}, u32[]{:S(2)}, u32[]{:S(2)}) collective-permute-start(bf16[416,256]{1,0:T(8,128)(2,1)S(1)} %get-tuple-element.37), channel_id=1, source_target_pairs={{0,254},{1,255},{2,252},{3,253},{4,2},{5,3},{6,0},{7,1},{8,6},{9,7... | collective-permute-start | bytes 638984 | tf_op jit(solution)/shard_map/ppermute | solution.py:309
  42.1 2.3 %collective-permute-start.7 = (bf16[416,256]{1,0:T(8,128)(2,1)S(1)}, bf16[416,256]{1,0:T(8,128)(2,1)S(1)}, u32[]{:S(2)}, u32[]{:S(2)}) collective-permute-start(bf16[416,256]{1,0:T(8,128)(2,1)S(1)} %collective-permute-done.5.qa.q_ref), channel_id=1, source_target_pairs={{0,1},{1,0},{2,3},{3,2},{4,5},{5,4},{6,7},{7,6},{8,9},{9,8},{10,11... | collective-permute-start | bytes 638984 | tf_op jit(solution)/shard_map/ppermute | solution.py:309
  43.3 1.5 %collective-permute-start.8 = (bf16[416,256]{1,0:T(8,128)(2,1)S(1)}, bf16[416,256]{1,0:T(8,128)(2,1)S(1)}, u32[]{:S(2)}, u32[]{:S(2)}) collective-permute-start(bf16[416,256]{1,0:T(8,128)(2,1)S(1)} %collective-permute-done.6.qb), channel_id=1, source_target_pairs={{0,1},{1,0},{2,3},{3,2},{4,5},{5,4},{6,7},{7,6},{8,9},{9,8},{10,11... | collective-permute-start | bytes 638984 | tf_op jit(solution)/shard_map/ppermute | solution.py:309
  46.9 23.8 %copy-start = (f32[1024,400]{0,1:T(8,128)S(1)}, f32[1024,400]{0,1:T(8,128)}, u32[]{:S(2)}) copy-start(f32[1024,400]{0,1:T(8,128)} %param.11) | copy-start | bytes 4915204
  46.9 20.9 %collective-permute-start.9 = (bf16[400,512]{1,0:T(8,128)(2,1)S(1)}, bf16[400,512]{1,0:T(8,128)(2,1)S(1)}, u32[]{:S(2)}, u32[]{:S(2)}) collective-permute-start(bf16[400,512]{1,0:T(8,128)(2,1)S(1)} %destination_step1.1), channel_id=1, source_target_pairs={{0,252},{1,253},{2,254},{3,255},{4,0},{5,1},{6,2},{7,3},{8,4},{9,5... | collective-permute-start | bytes 1228808 | tf_op jit(solution)/shard_map/ppermute | solution.py:309
  54.8 11.8 %collective-permute-start.10 = (bf16[400,256]{1,0:T(8,128)(2,1)S(1)}, bf16[400,256]{1,0:T(8,128)(2,1)S(1)}, u32[]{:S(2)}, u32[]{:S(2)}) collective-permute-start(bf16[400,256]{1,0:T(8,128)(2,1)S(1)} %query_gradient_step1.1), channel_id=1, source_target_pairs={{0,4},{1,5},{2,6},{3,7},{4,8},{5,9},{6,10},{7,11},{8,12},{9,13},{1... | collective-permute-start | bytes 614408 | tf_op jit(solution)/shard_map/ppermute | solution.py:309
  67.8 2.8 %collective-permute-start.11 = (bf16[400,512]{1,0:T(8,128)(2,1)S(1)}, bf16[400,512]{1,0:T(8,128)(2,1)S(1)}, u32[]{:S(2)}, u32[]{:S(2)}) collective-permute-start(bf16[400,512]{1,0:T(8,128)(2,1)S(1)} %collective-permute-done.9.own_ref), channel_id=1, source_target_pairs={{0,1},{1,0},{2,3},{3,2},{4,5},{5,4},{6,7},{7,6},{8,9},{9,8},{10,11... | collective-permute-start | bytes 1228808 | tf_op jit(solution)/shard_map/ppermute | solution.py:309

commit v3 on v2

v3 whole, which is shorter than its diff:
```python
import functools

import jax
import jax.numpy as jnp
from jax import lax
from jax.experimental import pallas as pl
from jax.experimental.pallas import tpu as pltpu
from jax.sharding import PartitionSpec as P

LEARNING_RATE = 0.1
BF = jnp.bfloat16
F32 = jnp.float32
I32 = jnp.int32
META = 16
FINE = 32
LANES = 128
PIECE = 1920


def dot(a, b):
    return lax.dot_general(a, b, (((1,), (0,)), ((), ())), preferred_element_type=F32)


def dot_nt(a, b):
    return lax.dot_general(a, b, (((1,), (1,)), ((), ())), preferred_element_type=F32)


def core():
    return lax.rem(lax.axis_index("narrow"), 2)


def iota(shape, dim):
    return lax.broadcasted_iota(I32, shape, dim)


def one_hot(rows, index):
    return (iota((rows, index.shape[1]), 0) == index).astype(F32).astype(BF)


def eye(n):
    return (iota((n, n), 0) == iota((n, n), 1)).astype(F32).astype(BF)


def two_rows(first, second, width):
    at = iota((META, width), 0)
    return jnp.where(at == 0, first, jnp.where(at == 1, second, 0.0)).astype(BF)


def index_rows(index):
    fine = lax.rem(index, FINE)
    coarse = lax.div(index, FINE)
    return two_rows(coarse.astype(F32), fine.astype(F32), index.shape[1])


def split(value):
    high = value.astype(BF)
    return high, (value - high.astype(F32)).astype(BF)


def picked(value, hot):
    high, low = split(value)
    return dot(high, hot) + dot(low, hot)


def summed(value, hot):
    high, low = split(value)
    return dot_nt(high, hot) + dot_nt(low, hot)


def coefficients(scores, count, is_target, negatives):
    tanh = jnp.tanh(0.5 * scores)
    scale = count * (0.5 / negatives)
    pull = jnp.where(is_target, 0.5 * tanh - 0.5, 0.0)
    return (scale * tanh + scale + pull).astype(BF)


def step_size(state, gradient):
    state = state + jnp.mean(gradient * gradient, axis=0, keepdims=True)
    return state, LEARNING_RATE / jnp.sqrt(state)


def cast_kernel(emb_ref, state_ref, out_ref, held, held_state, sems):
    depth, half = held.shape
    columns = pl.ds(pl.multiple_of(core() * half, half), half)
    copy_state = pltpu.make_async_copy(state_ref.at[:, columns], held_state, sems.at[0])
    copies = []
    for i, start in enumerate(range(0, depth, depth // 5)):
        part = pl.ds(start, depth // 5)
        copy = pltpu.make_async_copy(emb_ref.at[part, columns], held.at[part], sems.at[i + 1])
        copy.start()
        copies.append((copy, part))
    copy_state.start()
    for copy, part in copies:
        copy.wait()
        out_ref[part, :] = held[part, :].astype(BF)
    copy_state.wait()
    state = held_state[...]
    high = state.astype(BF).astype(F32)
    out_ref[depth:, :] = two_rows(high, state - high, half)


def count_grid(index, blocks):
    return one_hot(blocks, lax.div(index, LANES)), one_hot(LANES, lax.rem(index, LANES))


def relation_rows(rel_ref, index):
    depth, relations = rel_ref.shape
    block = lax.div(index, LANES)
    within = one_hot(LANES, lax.rem(index, LANES))
    found = jnp.zeros((depth, index.shape[1]), F32)
    for start in range(0, relations, PIECE):
        size = min(PIECE, relations - start)
        hot = jnp.concatenate(
            [
                within * (block == start // LANES + i).astype(F32).astype(BF)
                for i in range(size // LANES)
            ],
            axis=0,
        )
        found = found + dot(rel_ref[:, start : start + size], hot)
    return found


def lane_row(counts, out_ref):
    for i in range(counts.shape[0]):
        out_ref[:, i * LANES : (i + 1) * LANES] = counts[i : i + 1, :]


def query0_kernel(
    rel_ref, src_ref, src_index, dst_index, rel_index, q_ref, rel_out
):
    depth, edges = src_ref.shape
    found = relation_rows(rel_ref, rel_index[0:1, :])
    rel_out[...] = found.astype(BF)
    rows = picked(src_ref[...], one_hot(edges, src_index[0:1, :]))
    q_ref[:depth, :] = (rows * found).astype(BF)
    q_ref[depth:, :] = index_rows(dst_index[0:1, :])


def prep_kernel(
    rows, rel_ref, q_ref, rel_index, neg_index,
    qt_ref, at_ref, rel_out, count_ref, column_ref, next_ref, next_count_ref,
):
    depth, edges = rel_out.shape
    blocks = rows // LANES
    flip = core() * (rows // 2)
    coarse, fine = count_grid(neg_index[0:1, :] ^ flip, blocks)
    lane_row(dot_nt(coarse, fine), count_ref)
    column_ref[...] = dot_nt(fine, coarse)
    coarse, fine = count_grid(neg_index[1:2, :] ^ flip, blocks)
    counts = dot_nt(coarse, fine)
    high = jnp.floor(counts * (1.0 / FINE))
    next_ref[...] = jnp.concatenate([high, counts - high * FINE], axis=0)
    lane_row(counts, next_count_ref)
    rel_out[...] = relation_rows(rel_ref, rel_index[1:2, :]).astype(BF)
    query_t, target_at = turned_query(q_ref, depth, flip)
    qt_ref[...] = query_t
    at_ref[...] = jnp.broadcast_to(target_at, at_ref.shape)


def turned_query(q_ref, depth, flip):
    turn = eye(q_ref.shape[1])
    parts = dot_nt(turn, q_ref[depth:, :])
    target_at = (parts[:, 0:1] * FINE + parts[:, 1:2]).astype(I32) ^ flip
    return dot_nt(turn, q_ref[:depth, :]).astype(BF), target_at


def query_gradient(negatives, blocks, query_t, target_at, count_ref):
    total = 0.0
    start = 0
    for block in blocks:
        rows = block.shape[1]
        scores = dot(query_t, block)
        target = iota(scores.shape, 1) + start == target_at
        count = count_ref[:, start : start + rows]
        total += dot_nt(block, coefficients(scores, count, target, negatives))
        start += rows
    return total


def src0_kernel(
    negatives, own_ref, other_ref, qt_ref, at_ref, count_ref, src_ref, state_ref,
    rel0_ref, rel1_ref, src_index, dst_index, next_ref, q_ref, src_out, state_out,
):
    depth, edges = src_ref.shape
    blocks = own_ref[:depth, :], other_ref[:depth, :]
    grad = query_gradient(negatives, blocks, qt_ref[...], at_ref[:, 0:1], count_ref)
    gradient = summed(grad * rel0_ref[...].astype(F32), one_hot(edges, src_index[0:1, :]))
    state, size = step_size(state_ref[...], gradient)
    src = src_ref[...] - gradient * size
    src_out[...] = src
    state_out[...] = state
    rows = picked(src, one_hot(edges, src_index[1:2, :]))
    q_ref[:depth, :] = (rows * rel1_ref[...].astype(F32)).astype(BF)
    blocks = next_ref.shape[0] // 2
    counts = jnp.concatenate([next_ref[:blocks, :], next_ref[blocks:, :]], axis=1)
    gap = jnp.zeros((META // 2, edges), F32)
    meta = index_rows(dst_index[1:2, :]).astype(F32)
    q_ref[depth:, :] = (meta + jnp.concatenate([gap, counts], axis=0)).astype(BF)


def src1_kernel(
    negatives, own_ref, other_ref, last_ref, q_ref, count_ref, src_ref, state_ref, rel_ref,
    src_index, src_out,
):
    depth, edges = src_ref.shape
    half = own_ref.shape[1]
    query_t, target_at = turned_query(q_ref, depth, core() * half)
    blocks = own_ref[...], other_ref[...], last_ref[...]
    grad = query_gradient(negatives, blocks, query_t, target_at, count_ref)
    gradient = summed(grad * rel_ref[...].astype(F32), one_hot(edges, src_index[1:2, :]))
    _, size = step_size(state_ref[...], gradient)
    src_out[...] = src_ref[...] - gradient * size


def targets(q_ref, depth, flip):
    parts = q_ref[depth:, :].astype(F32)
    return (parts[0:1, :] * FINE + parts[1:2, :]).astype(I32) ^ flip


def sent_counts(q_ref, depth):
    parts = dot_nt(eye(LANES), q_ref[depth:, :LANES]) * FINE
    parts = parts + dot_nt(eye(LANES), q_ref[depth:, LANES : 2 * LANES])
    return parts[:, META // 2 :]


def row_coefficients(block_t, start, q_ref, column, flip, negatives):
    rows, depth = block_t.shape
    scores = dot(block_t, q_ref[:depth, :])
    target = iota(scores.shape, 0) + start == targets(q_ref, depth, flip)
    first = start // LANES
    count = jnp.concatenate(
        [column[:, first + i : first + i + 1] for i in range(rows // LANES)], axis=0
    )
    return coefficients(scores, count, target, negatives)


def dst_gradient(block_t, q_refs, column, flip, negatives):
    rows, depth = block_t.shape
    total = jnp.zeros((depth, rows), F32)
    for q_ref in q_refs:
        weights = row_coefficients(block_t, 0, q_ref, column, flip, negatives)
        total += dot_nt(q_ref[:depth, :], weights)
    return total


def turned(block):
    step = 2 * LANES
    turn = eye(step)
    return jnp.concatenate(
        [dot_nt(turn, block[:, k : k + step]).astype(BF) for k in range(0, block.shape[1], step)],
        axis=0,
    )


def dst0_kernel(
    negatives, own_ref, qa, qb, qc, qd, column_ref,
    block_out, turned_out, delta_out, state_out,
):
    depth, half = delta_out.shape
    block = own_ref[:depth, :]
    queries = qa, qb, qc, qd
    gradient = dst_gradient(
        turned(block), queries, column_ref[...], core() * half, negatives
    )
    parts = own_ref[depth:, :].astype(F32)
    state, size = step_size(parts[0:1, :] + parts[1:2, :], gradient)
    delta = gradient * size
    block = (block.astype(F32) - delta).astype(BF)
    block_out[...] = block
    turned_out[...] = turned(block)
    delta_out[...] = delta
    state_out[...] = state


def dst1_kernel(
    negatives, turned_ref, qa, qb, qc, qd, delta_ref, state_ref, delta_out
):
    depth, half = delta_ref.shape
    gradient = dst_gradient(
        turned_ref[...], (qa, qb, qc, qd), sent_counts(qa, depth), core() * half, negatives
    )
    _, size = step_size(state_ref[...], gradient)
    delta_out[:depth, :] = (delta_ref[...] + gradient * size).astype(BF)
    delta_out[depth:, :] = jnp.zeros((META, half), BF)


def final_kernel(emb_ref, own_ref, other_ref, out_ref):
    depth, half = emb_ref.shape[0], own_ref.shape[1]
    here = core()
    for place, delta_ref in ((here, own_ref), (1 - here, other_ref)):
        columns = pl.ds(pl.multiple_of(place * half, half), half)
        out_ref[:, columns] = emb_ref[:, columns] - delta_ref[:depth, :].astype(F32)


def call(kernel, outs, args, name, flops=None, scratch=(), hbm=(), limit=32):
    vmem = pl.BlockSpec(memory_space=pltpu.VMEM)
    anywhere = pl.BlockSpec(memory_space=pltpu.HBM)
    shapes = [jax.ShapeDtypeStruct(shape, dtype) for shape, dtype in outs]
    size = sum(a.size * a.dtype.itemsize for a in [*args, *shapes])
    result = pl.pallas_call(
        kernel,
        out_shape=shapes,
        in_specs=[anywhere if i in hbm else vmem for i in range(len(args))],
        out_specs=[vmem] * len(shapes),
        scratch_shapes=list(scratch),
        compiler_params=pltpu.CompilerParams(vmem_limit_bytes=int(limit * 2**20)),
        cost_estimate=pl.CostEstimate(
            flops=flops or 1, bytes_accessed=size if flops else 1, transcendentals=0
        ),
        name=name,
    )(*args)
    return result[0] if len(shapes) == 1 else result


def body(
    src_emb, src_state, dst_emb, dst_state, relations, src_index, dst_index, rel_index, neg_index
):
    wide, narrow = lax.axis_size("wide"), lax.axis_size("narrow")

    def moved(value, along=0, to=0):
        pairs = [
            (w * narrow + n, ((w + along) % wide) * narrow + (n ^ to))
            for w in range(wide)
            for n in range(narrow)
        ]
        return lax.ppermute(value, ("wide", "narrow"), pairs)

    rows, depth = dst_emb.shape
    edges = src_emb.shape[0]
    half = rows // 2
    src_index, dst_index, rel_index, neg_index = (
        a[0] for a in (src_index, dst_index, rel_index, neg_index)
    )
    negatives = neg_index.shape[1]
    dst, src, rel = dst_emb.T, src_emb.T, relations.T
    tall = depth + META

    payload = call(
        cast_kernel,
        [((tall, half), BF)],
        [dst, dst_state.reshape(1, rows)],
        "cast_block",
        scratch=[
            pltpu.VMEM((depth, half), F32),
            pltpu.VMEM((1, half), F32),
            pltpu.SemaphoreType.DMA((6,)),
        ],
        hbm=(0, 1),
        limit=8,
    )
    own = moved(payload, along=1)
    src_index, payload = lax.optimization_barrier((src_index, payload))

    src_state = src_state.reshape(1, edges)
    blocks = rows // LANES
    matmul = 2 * edges * rows * depth
    table = 2 * edges * relations.shape[0] * depth
    query, rel0 = call(
        query0_kernel,
        [((tall, edges), BF), ((depth, edges), BF)],
        [rel, src, src_index, dst_index, rel_index],
        "query_step0",
        flops=table,
        limit=32,
    )
    query_c, query_y = moved(query, to=1), moved(query, to=2)
    query_t, target_at, rel1, count0, column, counts_sent, count1 = call(
        functools.partial(prep_kernel, rows),
        [
            ((edges, depth), BF),
            ((edges, LANES), I32),
            ((depth, edges), BF),
            ((1, rows), F32),
            ((LANES, blocks), F32),
            ((2 * blocks, LANES), F32),
            ((1, rows), F32),
        ],
        [rel, query, rel_index, neg_index],
        "prepare",
        flops=table,
        limit=32,
    )
    own, query_y, query_c, rel1 = lax.optimization_barrier((own, query_y, query_c, rel1))
    other = moved(own, to=1)
    query_cy = moved(query_y, to=1)

    query1, src1, src_state1 = call(
        functools.partial(src0_kernel, negatives),
        [((tall, edges), BF), ((depth, edges), F32), ((1, edges), F32)],
        [
            own, other, query_t, target_at, count0, src, src_state,
            rel0, rel1, src_index, dst_index, counts_sent,
        ],
        "source_step0",
        flops=2 * matmul,
        limit=24,
    )
    next_own, next_y = moved(query1, along=-1), moved(query1, along=-1, to=2)
    own, query1 = lax.optimization_barrier((own, query1))

    block1, turned1, delta0, dst_state1 = call(
        functools.partial(dst0_kernel, negatives),
        [((depth, half), BF), ((half, depth), BF), ((depth, half), F32), ((1, half), F32)],
        [own, query, query_y, query_c, query_cy, column],
        "destination_step0",
        limit=24,
    )
    block1_own = moved(block1, along=1)
    next_own, next_y, block1 = lax.optimization_barrier((next_own, next_y, block1))
    next_c, next_cy = moved(next_own, to=1), moved(next_y, to=1)

    delta = call(
        functools.partial(dst1_kernel, negatives),
        [((tall, half), BF)],
        [turned1, next_own, next_y, next_c, next_cy, delta0, dst_state1],
        "destination_step1",
        flops=4 * matmul,
        limit=24,
    )
    home_own = moved(delta, along=-1)

    block1_own, delta = lax.optimization_barrier((block1_own, delta))
    block1_other = [moved(block1_own[:, k : k + half // 2], to=1) for k in (0, half // 2)]
    src_out = call(
        functools.partial(src1_kernel, negatives),
        [((depth, edges), F32)],
        [block1_own, *block1_other, query1, count1, src1, src_state1, rel1, src_index],
        "source_step1",
        limit=24,
    )
    home_own, src_out = lax.optimization_barrier((home_own, src_out))
    home_other = moved(home_own, to=1)
    dst_out = call(
        final_kernel,
        [((depth, rows), F32)],
        [dst, home_own, home_other],
        "destination_out",
        limit=16,
    )
    return src_out.T, dst_out.T


def solution(mesh):
    in_specs = (
        P(("wide", "narrow"), None),
        P(("wide", "narrow")),
        P("wide", None),
        P("wide"),
        P(),
        P(("wide", "narrow"), None, None),
        P(("wide", "narrow"), None, None),
        P(("wide", "narrow"), None, None),
        P("wide", None, None),
    )
    out_specs = (P(("wide", "narrow"), None), P("wide", None))
    return jax.shard_map(body, mesh=mesh, in_specs=in_specs, out_specs=out_specs, check_vma=False)
```

time: 72.1 us -> 65.2 us (0.904)
  waiting for transfers between devices: 32.5 us -> 26 us
  Pallas kernels: 18.6 us -> 14.5 us
  local copies, waits for them, and re-layouts: 2.71 us -> 4.85 us
  starting transfers between devices: 17.4 us -> 18.8 us
    ppermute x12 -> x14, waiting for transfers between devices: 32.5 us -> 26 us  [moved(): return lax.ppermute(value, ('wide', 'narrow'), pairs)]
    pallas_call x8, Pallas kernels: 18.6 us -> 14.5 us  [call(): pl.pallas_call(kernel, out_shape=shapes, in_specs=[anywhere if i in hbm e...]
    unnamed x16 -> x20, local copies, waits for them, and re-layouts: 2.71 us -> 4.82 us
    ppermute x12 -> x14, starting transfers between devices: 17.4 us -> 18.8 us  [moved(): return lax.ppermute(value, ('wide', 'narrow'), pairs)]
  transfers between devices with their start and end apart: 12 -> 14, of which waited for: 7 -> 10; matrix products, arithmetic and copies ran while one was open for 0% -> 0% of each run, Pallas kernels for 18% -> 20%
where the time goes in v3:
time: 65.2 us; the launch traced here: 65 us
  waiting for transfers between devices  26 us (40%)
  starting transfers between devices  18.8 us (29%)
  Pallas kernels  14.5 us (22%)
  local copies, waits for them, and re-layouts  4.85 us (7%)
  between operations  0.73 us (1%)
    ppermute x14, waiting for transfers between devices, moved(): return lax.ppermute(value, ('wide', 'narrow'), pairs)  26 us
    ppermute x14, starting transfers between devices, moved(): return lax.ppermute(value, ('wide', 'narrow'), pairs)  18.8 us
    pallas_call x8, Pallas kernels, call(): pl.pallas_call(kernel, out_shape=shapes, in_specs=[anywhere if i in hbm e...  14.5 us
    unnamed x20, local copies, waits for them, and re-layouts  4.82 us
  transfers between devices with their start and end apart: 14, of which 10 were waited for; matrix products, arithmetic and copies ran while one was open for 0% of the time, Pallas kernels for 20%

profile of v3, /device:TPU:1, one launch (start us, length us, event | category | flops | bytes accessed | tf_op | source)
XLA Modules:
  0.0 65.0 jit_solution(13225835803240506910)
XLA Ops:
  0.6 0.0 copy-start.4
  0.6 0.0 copy-start.1
  0.7 1.4 %copy-done.1 = f32[1024,400]{0,1:T(8,128)S(1)} copy-done((f32[1024,400]{0,1:T(8,128)S(1)}, f32[1024,400]{0,1:T(8,128)}, u32[]{:S(2)}) %copy-start.1) | copy-done | bytes 1638424
  2.1 0.7 %copy-done.8 = f32[1024]{0:T(1024)S(1)} copy-done((f32[1024]{0:T(1024)S(1)}, f32[1024]{0:T(1024)}, u32[]{:S(2)}) %copy-start.8) | copy-done | bytes 4120
  2.8 0.3 cast_block.1
  3.0 2.5 %collective-permute-start = (bf16[416,512]{1,0:T(8,128)(2,1)S(1)}, bf16[416,512]{1,0:T(8,128)(2,1)S(1)}, u32[]{:S(2)}, u32[]{:S(2)}) collective-permute-start(bf16[416,512]{1,0:T(8,128)(2,1)S(1)} %cast_block.1), channel_id=1, source_target_pairs={{0,4},{1,5},{2,6},{3,7},{4,8},{5,9},{6,10},{7,11},{8,12},{9,13},{1... | collective-permute-start | bytes 1277960 | tf_op jit(solution)/shard_map/ppermute | solution.py:327
  5.6 0.0 copy-done.4
  5.6 0.0 copy-done.3
  5.6 0.0 copy-done.6
  5.6 0.0 copy-done.7
  5.6 0.0 copy-start
  5.6 2.7 %copy-done = bf16[7424,400]{0,1:T(8,128)(2,1)S(1)} copy-done((bf16[7424,400]{0,1:T(8,128)(2,1)S(1)}, bf16[7424,400]{0,1:T(8,128)(2,1)}, u32[]{:S(2)}) %copy-start) | copy-done | bytes 5939224
  8.3 1.9 %query_step0.1 = (bf16[416,256]{1,0:T(8,128)(2,1)S(1)}, bf16[400,256]{1,0:T(8,128)(2,1)S(1)}) custom-call(bf16[400,7424]{1,0:T(8,128)(2,1)S(1)} %bitcast.11, f32[400,256]{1,0:T(8,128)S(1)} %bitcast.15, s32[2,256]{1,0:T(2,128)S(1)} %bitcast.17, s32[2,256]{1,0:T(2,128)S(1)} %bitcast.23, s32[2,256]{1,0:T(2,128)S(1)} %bitcast.21), custom_call_target="tpu_custom_call" | custom-call | flops 1520435200 | bytes 6772736 | tf_op jit(solution)/shard_map/query_step0/pallas_call | solution.py:301
  10.2 1.4 %collective-permute-start.1 = (bf16[416,256]{1,0:T(8,128)(2,1)S(1)}, bf16[416,256]{1,0:T(8,128)(2,1)S(1)}, u32[]{:S(2)}, u32[]{:S(2)}) collective-permute-start(bf16[416,256]{1,0:T(8,128)(2,1)S(1)} %get-tuple-element.31.q_ref.qa), channel_id=1, source_target_pairs={{0,2},{1,3},{2,0},{3,1},{4,6},{5,7},{6,4},{7,5},{8,10},{9,11},{10,... | collective-permute-start | bytes 638984 | tf_op jit(solution)/shard_map/ppermute | solution.py:327
  11.6 1.2 %collective-permute-start.2 = (bf16[416,256]{1,0:T(8,128)(2,1)S(1)}, bf16[416,256]{1,0:T(8,128)(2,1)S(1)}, u32[]{:S(2)}, u32[]{:S(2)}) collective-permute-start(bf16[416,256]{1,0:T(8,128)(2,1)S(1)} %get-tuple-element.31.q_ref.qa), channel_id=1, source_target_pairs={{0,1},{1,0},{2,3},{3,2},{4,5},{5,4},{6,7},{7,6},{8,9},{9,8},{10,11... | collective-permute-start | bytes 638984 | tf_op jit(solution)/shard_map/ppermute | solution.py:327
  12.8 0.0 copy-done.5
  12.8 2.3 %prepare.1 = (bf16[256,400]{1,0:T(8,128)(2,1)S(1)}, s32[256,128]{1,0:T(8,128)S(1)}, bf16[400,256]{1,0:T(8,128)(2,1)S(1)}, f32[1,1024]{1,0:T(1,128)S(1)}, f32[128...) custom-call(bf16[400,7424]{1,0:T(8,128)(2,1)S(1)} %bitcast.12, ...), custom_call_target="tpu_custom_call" | custom-call | flops 1520435200 | bytes 6731776 | tf_op jit(solution)/shard_map/prepare/pallas_call | solution.py:301
  15.1 10.4 %collective-permute-done.1.qb = bf16[416,256]{1,0:T(8,128)(2,1)S(1)} collective-permute-done((bf16[416,256]{1,0:T(8,128)(2,1)S(1)}, bf16[416,256]{1,0:T(8,128)(2,1)S(1)}, u32[]{:S(2)}, u32[]{:S(2)}) %collective-permute-start.1) | collective-permute-done | bytes 213024 | tf_op jit(solution)/shard_map/ppermute | solution.py:327
  25.6 0.0 collective-permute-done.2.qc
  25.6 0.0 collective-permute-done.own_ref
  25.6 1.5 %collective-permute-start.3 = (bf16[416,512]{1,0:T(8,128)(2,1)S(1)}, bf16[416,512]{1,0:T(8,128)(2,1)S(1)}, u32[]{:S(2)}, u32[]{:S(2)}) collective-permute-start(bf16[416,512]{1,0:T(8,128)(2,1)S(1)} %collective-permute-done.own_ref), channel_id=1, source_target_pairs={{0,1},{1,0},{2,3},{3,2},{4,5},{5,4},{6,7},{7,6},{8,9},{9,8},{10,11... | collective-permute-start | bytes 1277960 | tf_op jit(solution)/shard_map/ppermute | solution.py:327
  27.1 0.1 collective-permute-start.4
  27.2 1.3 %collective-permute-done.3.other_ref = bf16[416,512]{1,0:T(8,128)(2,1)S(1)} collective-permute-done((bf16[416,512]{1,0:T(8,128)(2,1)S(1)}, bf16[416,512]{1,0:T(8,128)(2,1)S(1)}, u32[]{:S(2)}, u32[]{:S(2)}) %collective-permute-start.3) | collective-permute-done | bytes 426016 | tf_op jit(solution)/shard_map/ppermute | solution.py:327
  28.5 1.7 %source_step0.1 = (bf16[416,256]{1,0:T(8,128)(2,1)S(1)}, f32[400,256]{1,0:T(8,128)S(1)}, f32[1,256]{1,0:T(1,128)S(1)}) custom-call(bf16[416,512]{1,0:T(8,128)(2,1)S(1)} %collective-permute-done.own_ref, bf16[416,512]{1,0:T(8,128)(2,1)S(1)} %collective-permute-done.3.other_ref, bf16[256,400]{1,0:T(8,128)(2,1)S(1)} %get-tuple-element.34.qt_ref, ...), custom_call_target="tpu_custom_call" | custom-call | flops 419430400 | bytes 2648064 | tf_op jit(solution)/shard_map/source_step0/pallas_call | solution.py:301
  30.2 0.3 collective-permute-start.5
  30.6 0.6 collective-permute-start.6
  31.2 0.0 collective-permute-done.4.qd
  31.2 2.6 %destination_step0.1 = (bf16[400,512]{1,0:T(8,128)(2,1)S(1)}, bf16[512,400]{1,0:T(8,128)(2,1)S(1)}, f32[400,512]{1,0:T(8,128)S(1)}, f32[1,512]{1,0:T(1,128)S(1)}) custom-call(bf16[416,512]{1,0:T(8,128)(2,1)S(1)} %collective-permute-done.own_ref, bf16[416,256]{1,0:T(8,128)(2,1)S(1)} %get-tuple-element.31.q_ref.qa, ...), custom_call_target="tpu_custom_call" | custom-call | flops 1 | bytes 1 | tf_op jit(solution)/shard_map/destination_step0/pallas_call | solution.py:301
  33.8 1.6 %collective-permute-start.10 = (bf16[400,512]{1,0:T(8,128)(2,1)S(1)}, bf16[400,512]{1,0:T(8,128)(2,1)S(1)}, u32[]{:S(2)}, u32[]{:S(2)}) collective-permute-start(bf16[400,512]{1,0:T(8,128)(2,1)S(1)} %get-tuple-element.46), channel_id=1, source_target_pairs={{0,4},{1,5},{2,6},{3,7},{4,8},{5,9},{6,10},{7,11},{8,12},{9,13},{1... | collective-permute-start | bytes 1228808 | tf_op jit(solution)/shard_map/ppermute | solution.py:327
  35.4 1.4 %collective-permute-done.5.qa = bf16[416,256]{1,0:T(8,128)(2,1)S(1)} collective-permute-done((bf16[416,256]{1,0:T(8,128)(2,1)S(1)}, bf16[416,256]{1,0:T(8,128)(2,1)S(1)}, u32[]{:S(2)}, u32[]{:S(2)}) %collective-permute-start.5) | collective-permute-done | bytes 213024 | tf_op jit(solution)/shard_map/ppermute | solution.py:327
  36.8 5.4 %collective-permute-done.6.qb = bf16[416,256]{1,0:T(8,128)(2,1)S(1)} collective-permute-done((bf16[416,256]{1,0:T(8,128)(2,1)S(1)}, bf16[416,256]{1,0:T(8,128)(2,1)S(1)}, u32[]{:S(2)}, u32[]{:S(2)}) %collective-permute-start.6) | collective-permute-done | bytes 213024 | tf_op jit(solution)/shard_map/ppermute | solution.py:327
  42.2 2.4 %collective-permute-start.7 = (bf16[416,256]{1,0:T(8,128)(2,1)S(1)}, bf16[416,256]{1,0:T(8,128)(2,1)S(1)}, u32[]{:S(2)}, u32[]{:S(2)}) collective-permute-start(bf16[416,256]{1,0:T(8,128)(2,1)S(1)} %collective-permute-done.5.qa), channel_id=1, source_target_pairs={{0,1},{1,0},{2,3},{3,2},{4,5},{5,4},{6,7},{7,6},{8,9},{9,8},{10,11... | collective-permute-start | bytes 638984 | tf_op jit(solution)/shard_map/ppermute | solution.py:327
  44.6 0.0 collective-permute-start.8
  44.6 1.1 %collective-permute-done.7.qc = bf16[416,256]{1,0:T(8,128)(2,1)S(1)} collective-permute-done((bf16[416,256]{1,0:T(8,128)(2,1)S(1)}, bf16[416,256]{1,0:T(8,128)(2,1)S(1)}, u32[]{:S(2)}, u32[]{:S(2)}) %collective-permute-start.7) | collective-permute-done | bytes 213024 | tf_op jit(solution)/shard_map/ppermute | solution.py:327
  45.7 0.4 collective-permute-done.8.qd
  46.1 2.1 %destination_step1.1 = bf16[416,512]{1,0:T(8,128)(2,1)S(1)} custom-call(bf16[512,400]{1,0:T(8,128)(2,1)S(1)} %get-tuple-element.45.turned_ref, bf16[416,256]{1,0:T(8,128)(2,1)S(1)} %collective-permute-done.5.qa, bf16[416,256]{1,0:T(8,128)(2,1)S(1)} %collective-permute-done.6.qb, bf16[416,256]{1,0:T(8,128)(2,1)S(1)} %collective-permute-done.7.qc, ...), custom_call_target="tpu_custom_call" | custom-call | flops 838860800 | bytes 2508800 | tf_op jit(solution)/shard_map/destination_step1/pallas_call | solution.py:301
  48.2 0.0 copy-start.2
  48.2 4.0 %collective-permute-start.9 = (bf16[416,512]{1,0:T(8,128)(2,1)S(1)}, bf16[416,512]{1,0:T(8,128)(2,1)S(1)}, u32[]{:S(2)}, u32[]{:S(2)}) collective-permute-start(bf16[416,512]{1,0:T(8,128)(2,1)S(1)} %destination_step1.1), channel_id=1, source_target_pairs={{0,252},{1,253},{2,254},{3,255},{4,0},{5,1},{6,2},{7,3},{8,4},{9,5... | collective-permute-start | bytes 1277960 | tf_op jit(solution)/shard_map/ppermute | solution.py:327
  52.2 0.0 collective-permute-done.10.own_ref
  52.2 1.8 %collective-permute-start.11 = (bf16[400,256]{1,0:T(8,128)(2,1)S(1)}, bf16[400,256]{1,0:T(8,128)(2,1)S(1)}, u32[]{:S(2)}, u32[]{:S(2)}) collective-permute-start(bf16[400,256]{1,0:T(8,128)(2,1)S(1)} %get-tuple-element.59), channel_id=1, source_target_pairs={{0,1},{1,0},{2,3},{3,2},{4,5},{5,4},{6,7},{7,6},{8,9},{9,8},{10,11... | collective-permute-start | bytes 614408 | tf_op jit(solution)/shard_map/ppermute | solution.py:327
  54.1 0.1 collective-permute-start.12
  54.2 1.0 %collective-permute-done.11.other_ref = bf16[400,256]{1,0:T(8,128)(2,1)S(1)} collective-permute-done((bf16[400,256]{1,0:T(8,128)(2,1)S(1)}, bf16[400,256]{1,0:T(8,128)(2,1)S(1)}, u32[]{:S(2)}, u32[]{:S(2)}) %collective-permute-start.11) | collective-permute-done | bytes 204832 | tf_op jit(solution)/shard_map/ppermute | solution.py:327
  55.1 0.4 collective-permute-done.12.last_ref
  55.5 2.3 %source_step1.1 = f32[400,256]{1,0:T(8,128)} custom-call(bf16[400,512]{1,0:T(8,128)(2,1)S(1)} %collective-permute-done.10.own_ref, bf16[400,256]{1,0:T(8,128)(2,1)S(1)} %collective-permute-done.11.other_ref, bf16[400,256]{1,0:T(8,128)(2,1)S(1)} %collective-permute-done.12.last_ref, bf16[416,256]{1,0:T(8,128)(2,1)S(1)} %get-tuple-element.52.q_ref, ...), custom_call_target="tpu_custom_call" | custom-call | flops 1 | bytes 1 | tf_op jit(solution)/shard_map/source_step1/pallas_call | solution.py:301
  57.8 3.3 %collective-permute-done.9.own_ref = bf16[416,512]{1,0:T(8,128)(2,1)S(1)} collective-permute-done((bf16[416,512]{1,0:T(8,128)(2,1)S(1)}, bf16[416,512]{1,0:T(8,128)(2,1)S(1)}, u32[]{:S(2)}, u32[]{:S(2)}) %collective-permute-start.9) | collective-permute-done | bytes 426016 | tf_op jit(solution)/shard_map/ppermute | solution.py:327
  61.1 1.1 %collective-permute-start.13 = (bf16[416,512]{1,0:T(8,128)(2,1)S(1)}, bf16[416,512]{1,0:T(8,128)(2,1)S(1)}, u32[]{:S(2)}, u32[]{:S(2)}) collective-permute-start(bf16[416,512]{1,0:T(8,128)(2,1)S(1)} %collective-permute-done.9.own_ref), channel_id=1, source_target_pairs={{0,1},{1,0},{2,3},{3,2},{4,5},{5,4},{6,7},{7,6},{8,9},{9,8},{10,11... | collective-permute-start | bytes 1277960 | tf_op jit(solution)/shard_map/ppermute | solution.py:327
  62.2 1.4 %collective-permute-done.13.other_ref = bf16[416,512]{1,0:T(8,128)(2,1)S(1)} collective-permute-done((bf16[416,512]{1,0:T(8,128)(2,1)S(1)}, bf16[416,512]{1,0:T(8,128)(2,1)S(1)}, u32[]{:S(2)}, u32[]{:S(2)}) %collective-permute-start.13) | collective-permute-done | bytes 426016 | tf_op jit(solution)/shard_map/ppermute | solution.py:327
  63.6 1.3 %destination_out.1 = f32[400,1024]{1,0:T(8,128)} custom-call(f32[400,1024]{1,0:T(8,128)S(1)} %bitcast.14, bf16[416,512]{1,0:T(8,128)(2,1)S(1)} %collective-permute-done.9.own_ref, bf16[416,512]{1,0:T(8,128)(2,1)S(1)} %collective-permute-done.13.other_ref), custom_call_target="tpu_custom_call" | custom-call | flops 1 | bytes 1 | tf_op jit(solution)/shard_map/destination_out/pallas_call | solution.py:301
  (9 shorter events, 0.0 us)
Async XLA Ops:
  0.6 5.0 %copy-start.4 = (s32[1,2,256]{2,1,0:T(2,128)S(1)}, s32[1,2,256]{2,1,0:T(2,128)}, u32[]{:S(2)}) copy-start(s32[1,2,256]{2,1,0:T(2,128)} %param.14) | copy-start | bytes 6148
  0.6 1.4 %copy-start.1 = (f32[1024,400]{0,1:T(8,128)S(1)}, f32[1024,400]{0,1:T(8,128)}, u32[]{:S(2)}) copy-start(f32[1024,400]{0,1:T(8,128)} %param.11) | copy-start | bytes 4915204
  2.1 0.7 %copy-start.8 = (f32[1024]{0:T(1024)S(1)}, f32[1024]{0:T(1024)}, u32[]{:S(2)}) copy-start(f32[1024]{0:T(1024)} %param.12) | copy-start | bytes 12292
  2.8 2.8 %copy-start.3 = (f32[256,400]{0,1:T(8,128)S(1)}, f32[256,400]{0,1:T(8,128)}, u32[]{:S(2)}) copy-start(f32[256,400]{0,1:T(8,128)} %param.9) | copy-start | bytes 1228804
  2.8 2.8 %copy-start.6 = (s32[1,2,256]{2,1,0:T(2,128)S(1)}, s32[1,2,256]{2,1,0:T(2,128)}, u32[]{:S(2)}) copy-start(s32[1,2,256]{2,1,0:T(2,128)} %param.16) | copy-start | bytes 6148
  2.8 2.8 %copy-start.7 = (s32[1,2,256]{2,1,0:T(2,128)S(1)}, s32[1,2,256]{2,1,0:T(2,128)}, u32[]{:S(2)}) copy-start(s32[1,2,256]{2,1,0:T(2,128)} %param.15) | copy-start | bytes 6148
  3.0 22.5 %collective-permute-start = (bf16[416,512]{1,0:T(8,128)(2,1)S(1)}, bf16[416,512]{1,0:T(8,128)(2,1)S(1)}, u32[]{:S(2)}, u32[]{:S(2)}) collective-permute-start(bf16[416,512]{1,0:T(8,128)(2,1)S(1)} %cast_block.1), channel_id=1, source_target_pairs={{0,4},{1,5},{2,6},{3,7},{4,8},{5,9},{6,10},{7,11},{8,12},{9,13},{1... | collective-permute-start | bytes 1277960 | tf_op jit(solution)/shard_map/ppermute | solution.py:327
  5.6 2.7 %copy-start = (bf16[7424,400]{0,1:T(8,128)(2,1)S(1)}, bf16[7424,400]{0,1:T(8,128)(2,1)}, u32[]{:S(2)}) copy-start(bf16[7424,400]{0,1:T(8,128)(2,1)} %param.13) | copy-start | bytes 17817604
  8.3 4.6 %copy-start.5 = (s32[1,2,2048]{2,1,0:T(2,128)S(1)}, s32[1,2,2048]{2,1,0:T(2,128)}, u32[]{:S(2)}) copy-start(s32[1,2,2048]{2,1,0:T(2,128)} %param.17) | copy-start | bytes 49156
  10.2 15.4 %collective-permute-start.1 = (bf16[416,256]{1,0:T(8,128)(2,1)S(1)}, bf16[416,256]{1,0:T(8,128)(2,1)S(1)}, u32[]{:S(2)}, u32[]{:S(2)}) collective-permute-start(bf16[416,256]{1,0:T(8,128)(2,1)S(1)} %get-tuple-element.31.q_ref.qa), channel_id=1, source_target_pairs={{0,2},{1,3},{2,0},{3,1},{4,6},{5,7},{6,4},{7,5},{8,10},{9,11},{10,... | collective-permute-start | bytes 638984 | tf_op jit(solution)/shard_map/ppermute | solution.py:327
  11.6 14.0 %collective-permute-start.2 = (bf16[416,256]{1,0:T(8,128)(2,1)S(1)}, bf16[416,256]{1,0:T(8,128)(2,1)S(1)}, u32[]{:S(2)}, u32[]{:S(2)}) collective-permute-start(bf16[416,256]{1,0:T(8,128)(2,1)S(1)} %get-tuple-element.31.q_ref.qa), channel_id=1, source_target_pairs={{0,1},{1,0},{2,3},{3,2},{4,5},{5,4},{6,7},{7,6},{8,9},{9,8},{10,11... | collective-permute-start | bytes 638984 | tf_op jit(solution)/shard_map/ppermute | solution.py:327
  12.8 15.7 %copy-start.9 = (f32[256]{0:T(256)S(1)}, f32[256]{0:T(256)}, u32[]{:S(2)}) copy-start(f32[256]{0:T(256)} %param.10) | copy-start | bytes 3076
  25.6 2.9 %collective-permute-start.3 = (bf16[416,512]{1,0:T(8,128)(2,1)S(1)}, bf16[416,512]{1,0:T(8,128)(2,1)S(1)}, u32[]{:S(2)}, u32[]{:S(2)}) collective-permute-start(bf16[416,512]{1,0:T(8,128)(2,1)S(1)} %collective-permute-done.own_ref), channel_id=1, source_target_pairs={{0,1},{1,0},{2,3},{3,2},{4,5},{5,4},{6,7},{7,6},{8,9},{9,8},{10,11... | collective-permute-start | bytes 1277960 | tf_op jit(solution)/shard_map/ppermute | solution.py:327
  27.1 4.1 %collective-permute-start.4 = (bf16[416,256]{1,0:T(8,128)(2,1)S(1)}, bf16[416,256]{1,0:T(8,128)(2,1)S(1)}, u32[]{:S(2)}, u32[]{:S(2)}) collective-permute-start(bf16[416,256]{1,0:T(8,128)(2,1)S(1)} %collective-permute-done.1.qb), channel_id=1, source_target_pairs={{0,1},{1,0},{2,3},{3,2},{4,5},{5,4},{6,7},{7,6},{8,9},{9,8},{10,11... | collective-permute-start | bytes 638984 | tf_op jit(solution)/shard_map/ppermute | solution.py:327
  30.2 6.5 %collective-permute-start.5 = (bf16[416,256]{1,0:T(8,128)(2,1)S(1)}, bf16[416,256]{1,0:T(8,128)(2,1)S(1)}, u32[]{:S(2)}, u32[]{:S(2)}) collective-permute-start(bf16[416,256]{1,0:T(8,128)(2,1)S(1)} %get-tuple-element.52.q_ref), channel_id=1, source_target_pairs={{0,252},{1,253},{2,254},{3,255},{4,0},{5,1},{6,2},{7,3},{8,4},{9,5... | collective-permute-start | bytes 638984 | tf_op jit(solution)/shard_map/ppermute | solution.py:327
  30.6 11.6 %collective-permute-start.6 = (bf16[416,256]{1,0:T(8,128)(2,1)S(1)}, bf16[416,256]{1,0:T(8,128)(2,1)S(1)}, u32[]{:S(2)}, u32[]{:S(2)}) collective-permute-start(bf16[416,256]{1,0:T(8,128)(2,1)S(1)} %get-tuple-element.52.q_ref), channel_id=1, source_target_pairs={{0,254},{1,255},{2,252},{3,253},{4,2},{5,3},{6,0},{7,1},{8,6},{9,7... | collective-permute-start | bytes 638984 | tf_op jit(solution)/shard_map/ppermute | solution.py:327
  33.8 18.4 %collective-permute-start.10 = (bf16[400,512]{1,0:T(8,128)(2,1)S(1)}, bf16[400,512]{1,0:T(8,128)(2,1)S(1)}, u32[]{:S(2)}, u32[]{:S(2)}) collective-permute-start(bf16[400,512]{1,0:T(8,128)(2,1)S(1)} %get-tuple-element.46), channel_id=1, source_target_pairs={{0,4},{1,5},{2,6},{3,7},{4,8},{5,9},{6,10},{7,11},{8,12},{9,13},{1... | collective-permute-start | bytes 1228808 | tf_op jit(solution)/shard_map/ppermute | solution.py:327
  42.2 3.5 %collective-permute-start.7 = (bf16[416,256]{1,0:T(8,128)(2,1)S(1)}, bf16[416,256]{1,0:T(8,128)(2,1)S(1)}, u32[]{:S(2)}, u32[]{:S(2)}) collective-permute-start(bf16[416,256]{1,0:T(8,128)(2,1)S(1)} %collective-permute-done.5.qa), channel_id=1, source_target_pairs={{0,1},{1,0},{2,3},{3,2},{4,5},{5,4},{6,7},{7,6},{8,9},{9,8},{10,11... | collective-permute-start | bytes 638984 | tf_op jit(solution)/shard_map/ppermute | solution.py:327
  44.6 1.5 %collective-permute-start.8 = (bf16[416,256]{1,0:T(8,128)(2,1)S(1)}, bf16[416,256]{1,0:T(8,128)(2,1)S(1)}, u32[]{:S(2)}, u32[]{:S(2)}) collective-permute-start(bf16[416,256]{1,0:T(8,128)(2,1)S(1)} %collective-permute-done.6.qb), channel_id=1, source_target_pairs={{0,1},{1,0},{2,3},{3,2},{4,5},{5,4},{6,7},{7,6},{8,9},{9,8},{10,11... | collective-permute-start | bytes 638984 | tf_op jit(solution)/shard_map/ppermute | solution.py:327
  48.2 15.5 %copy-start.2 = (f32[1024,400]{0,1:T(8,128)S(1)}, f32[1024,400]{0,1:T(8,128)}, u32[]{:S(2)}) copy-start(f32[1024,400]{0,1:T(8,128)} %param.11) | copy-start | bytes 4915204
  48.2 12.9 %collective-permute-start.9 = (bf16[416,512]{1,0:T(8,128)(2,1)S(1)}, bf16[416,512]{1,0:T(8,128)(2,1)S(1)}, u32[]{:S(2)}, u32[]{:S(2)}) collective-permute-start(bf16[416,512]{1,0:T(8,128)(2,1)S(1)} %destination_step1.1), channel_id=1, source_target_pairs={{0,252},{1,253},{2,254},{3,255},{4,0},{5,1},{6,2},{7,3},{8,4},{9,5... | collective-permute-start | bytes 1277960 | tf_op jit(solution)/shard_map/ppermute | solution.py:327
  52.2 2.9 %collective-permute-start.11 = (bf16[400,256]{1,0:T(8,128)(2,1)S(1)}, bf16[400,256]{1,0:T(8,128)(2,1)S(1)}, u32[]{:S(2)}, u32[]{:S(2)}) collective-permute-start(bf16[400,256]{1,0:T(8,128)(2,1)S(1)} %get-tuple-element.59), channel_id=1, source_target_pairs={{0,1},{1,0},{2,3},{3,2},{4,5},{5,4},{6,7},{7,6},{8,9},{9,8},{10,11... | collective-permute-start | bytes 614408 | tf_op jit(solution)/shard_map/ppermute | solution.py:327
  54.1 1.5 %collective-permute-start.12 = (bf16[400,256]{1,0:T(8,128)(2,1)S(1)}, bf16[400,256]{1,0:T(8,128)(2,1)S(1)}, u32[]{:S(2)}, u32[]{:S(2)}) collective-permute-start(bf16[400,256]{1,0:T(8,128)(2,1)S(1)} %get-tuple-element.58), channel_id=1, source_target_pairs={{0,1},{1,0},{2,3},{3,2},{4,5},{5,4},{6,7},{7,6},{8,9},{9,8},{10,11... | collective-permute-start | bytes 614408 | tf_op jit(solution)/shard_map/ppermute | solution.py:327
  61.1 2.5 %collective-permute-start.13 = (bf16[416,512]{1,0:T(8,128)(2,1)S(1)}, bf16[416,512]{1,0:T(8,128)(2,1)S(1)}, u32[]{:S(2)}, u32[]{:S(2)}) collective-permute-start(bf16[416,512]{1,0:T(8,128)(2,1)S(1)} %collective-permute-done.9.own_ref), channel_id=1, source_target_pairs={{0,1},{1,0},{2,3},{3,2},{4,5},{5,4},{6,7},{7,6},{8,9},{9,8},{10,11... | collective-permute-start | bytes 1277960 | tf_op jit(solution)/shard_map/ppermute | solution.py:327

commit v4 on v3

--- a/solution.py
+++ b/solution.py
@@ -41,15 +41,12 @@
     return (iota((n, n), 0) == iota((n, n), 1)).astype(F32).astype(BF)
 
 
-def two_rows(first, second, width):
-    at = iota((META, width), 0)
-    return jnp.where(at == 0, first, jnp.where(at == 1, second, 0.0)).astype(BF)
-
-
 def index_rows(index):
     fine = lax.rem(index, FINE)
     coarse = lax.div(index, FINE)
-    return two_rows(coarse.astype(F32), fine.astype(F32), index.shape[1])
+    at = iota((META, index.shape[1]), 0)
+    parts = jnp.where(at == 0, coarse, jnp.where(at == 1, fine, 0))
+    return parts.astype(F32).astype(BF)
 
 
 def split(value):
@@ -77,26 +74,6 @@
 def step_size(state, gradient):
     state = state + jnp.mean(gradient * gradient, axis=0, keepdims=True)
     return state, LEARNING_RATE / jnp.sqrt(state)
-
-
-def cast_kernel(emb_ref, state_ref, out_ref, held, held_state, sems):
-    depth, half = held.shape
-    columns = pl.ds(pl.multiple_of(core() * half, half), half)
-    copy_state = pltpu.make_async_copy(state_ref.at[:, columns], held_state, sems.at[0])
-    copies = []
-    for i, start in enumerate(range(0, depth, depth // 5)):
-        part = pl.ds(start, depth // 5)
-        copy = pltpu.make_async_copy(emb_ref.at[part, columns], held.at[part], sems.at[i + 1])
-        copy.start()
-        copies.append((copy, part))
-    copy_state.start()
-    for copy, part in copies:
-        copy.wait()
-        out_ref[part, :] = held[part, :].astype(BF)
-    copy_state.wait()
-    state = held_state[...]
-    high = state.astype(BF).astype(F32)
-    out_ref[depth:, :] = two_rows(high, state - high, half)
 
 
 def count_grid(index, blocks):
@@ -127,21 +104,27 @@
 
 
 def query0_kernel(
-    rel_ref, src_ref, src_index, dst_index, rel_index, q_ref, rel_out
+    rel_ref, src_ref, index, q_ref, rel_out
 ):
     depth, edges = src_ref.shape
-    found = relation_rows(rel_ref, rel_index[0:1, :])
+    src_index, dst_index, rel_index = index[0:1, :], index[2:3, :], index[4:5, :]
+    found = relation_rows(rel_ref, rel_index)
     rel_out[...] = found.astype(BF)
-    rows = picked(src_ref[...], one_hot(edges, src_index[0:1, :]))
+    rows = picked(src_ref[...], one_hot(edges, src_index))
     q_ref[:depth, :] = (rows * found).astype(BF)
-    q_ref[depth:, :] = index_rows(dst_index[0:1, :])
+    q_ref[depth:, :] = index_rows(dst_index)
 
 
 def prep_kernel(
-    rows, rel_ref, q_ref, rel_index, neg_index,
+    rows, rel_ref, q_ref, rel_index, neg_index, src_ref, state_ref, src_index, dst_index,
     qt_ref, at_ref, rel_out, count_ref, column_ref, next_ref, next_count_ref,
+    src_out, state_out, src_index_out, dst_index_out,
 ):
     depth, edges = rel_out.shape
+    src_out[...] = src_ref[...]
+    state_out[...] = state_ref[...]
+    src_index_out[...] = src_index[...]
+    dst_index_out[...] = dst_index[...]
     blocks = rows // LANES
     flip = core() * (rows // 2)
     coarse, fine = count_grid(neg_index[0:1, :] ^ flip, blocks)
@@ -179,11 +162,11 @@
 
 
 def src0_kernel(
-    negatives, own_ref, other_ref, qt_ref, at_ref, count_ref, src_ref, state_ref,
+    negatives, own_ref, other_a, other_b, qt_ref, at_ref, count_ref, src_ref, state_ref,
     rel0_ref, rel1_ref, src_index, dst_index, next_ref, q_ref, src_out, state_out,
 ):
     depth, edges = src_ref.shape
-    blocks = own_ref[:depth, :], other_ref[:depth, :]
+    blocks = own_ref[...], jnp.concatenate([other_a[...], other_b[...]], axis=1)
     grad = query_gradient(negatives, blocks, qt_ref[...], at_ref[:, 0:1], count_ref)
     gradient = summed(grad * rel0_ref[...].astype(F32), one_hot(edges, src_index[0:1, :]))
     state, size = step_size(state_ref[...], gradient)
@@ -254,17 +237,17 @@
 
 
 def dst0_kernel(
-    negatives, own_ref, qa, qb, qc, qd, column_ref,
+    negatives, own_ref, old_ref, qa, qb, qc, qd, column_ref,
     block_out, turned_out, delta_out, state_out,
 ):
     depth, half = delta_out.shape
-    block = own_ref[:depth, :]
+    block = own_ref[...]
+    columns = pl.ds(pl.multiple_of(core() * half, half), half)
     queries = qa, qb, qc, qd
     gradient = dst_gradient(
         turned(block), queries, column_ref[...], core() * half, negatives
     )
-    parts = own_ref[depth:, :].astype(F32)
-    state, size = step_size(parts[0:1, :] + parts[1:2, :], gradient)
+    state, size = step_size(old_ref[:, columns], gradient)
     delta = gradient * size
     block = (block.astype(F32) - delta).astype(BF)
     block_out[...] = block
@@ -273,27 +256,44 @@
     state_out[...] = state
 
 
+def dst1_first_kernel(negatives, turned_ref, qa, qb, grad_out):
+    depth, half = grad_out.shape
+    grad_out[...] = dst_gradient(
+        turned_ref[...], (qa, qb), sent_counts(qa, depth), core() * half, negatives
+    )
+
+
 def dst1_kernel(
-    negatives, turned_ref, qa, qb, qc, qd, delta_ref, state_ref, delta_out
+    negatives, turned_ref, first_ref, qa, qc, qd, delta_ref, state_ref, delta_out
 ):
     depth, half = delta_ref.shape
-    gradient = dst_gradient(
-        turned_ref[...], (qa, qb, qc, qd), sent_counts(qa, depth), core() * half, negatives
+    gradient = first_ref[...] + dst_gradient(
+        turned_ref[...], (qc, qd), sent_counts(qa, depth), core() * half, negatives
     )
     _, size = step_size(state_ref[...], gradient)
     delta_out[:depth, :] = (delta_ref[...] + gradient * size).astype(BF)
     delta_out[depth:, :] = jnp.zeros((META, half), BF)
 
 
-def final_kernel(emb_ref, own_ref, other_ref, out_ref):
-    depth, half = emb_ref.shape[0], own_ref.shape[1]
-    here = core()
-    for place, delta_ref in ((here, own_ref), (1 - here, other_ref)):
-        columns = pl.ds(pl.multiple_of(place * half, half), half)
-        out_ref[:, columns] = emb_ref[:, columns] - delta_ref[:depth, :].astype(F32)
-
-
-def call(kernel, outs, args, name, flops=None, scratch=(), hbm=(), limit=32):
+def final_kernel(mine, emb_ref, delta_ref, *refs):
+    out_ref, held, sems = refs[-3:]
+    depth, half = held.shape
+    place = core() if mine else 1 - core()
+    copies = []
+    for i in range(2):
+        size = half // 2
+        columns = pl.ds(pl.multiple_of(place * half + i * size, size), size)
+        part = slice(i * size, (i + 1) * size)
+        held[:, part] = emb_ref[:, columns] - delta_ref[:depth, part].astype(F32)
+        copies.append(
+            pltpu.make_async_copy(held.at[:, part], out_ref.at[:, columns], sems.at[i])
+        )
+        copies[-1].start()
+    for copy in copies:
+        copy.wait()
+
+
+def call(kernel, outs, args, name, flops=None, scratch=(), hbm=(), limit=32, out=None):
     vmem = pl.BlockSpec(memory_space=pltpu.VMEM)
     anywhere = pl.BlockSpec(memory_space=pltpu.HBM)
     shapes = [jax.ShapeDtypeStruct(shape, dtype) for shape, dtype in outs]
@@ -302,7 +302,8 @@
         kernel,
         out_shape=shapes,
         in_specs=[anywhere if i in hbm else vmem for i in range(len(args))],
-        out_specs=[vmem] * len(shapes),
+        out_specs=[vmem if out is None else anywhere] * len(shapes),
+        input_output_aliases={out: 0} if out else {},
         scratch_shapes=list(scratch),
         compiler_params=pltpu.CompilerParams(vmem_limit_bytes=int(limit * 2**20)),
         cost_estimate=pl.CostEstimate(
@@ -318,12 +319,13 @@
 ):
     wide, narrow = lax.axis_size("wide"), lax.axis_size("narrow")
 
-    def moved(value, along=0, to=0):
-        pairs = [
-            (w * narrow + n, ((w + along) % wide) * narrow + (n ^ to))
-            for w in range(wide)
-            for n in range(narrow)
-        ]
+    def moved(value, along=0, to=0, copies=False):
+        pairs = []
+        for w in range(wide):
+            target = (w + along) % wide
+            other_half = copies and w // (wide // 2) != target // (wide // 2)
+            turn = to ^ 2 if other_half else to
+            pairs += [(w * narrow + n, target * narrow + (n ^ turn)) for n in range(narrow)]
         return lax.ppermute(value, ("wide", "narrow"), pairs)
 
     rows, depth = dst_emb.shape
@@ -336,21 +338,11 @@
     dst, src, rel = dst_emb.T, src_emb.T, relations.T
     tall = depth + META
 
-    payload = call(
-        cast_kernel,
-        [((tall, half), BF)],
-        [dst, dst_state.reshape(1, rows)],
-        "cast_block",
-        scratch=[
-            pltpu.VMEM((depth, half), F32),
-            pltpu.VMEM((1, half), F32),
-            pltpu.SemaphoreType.DMA((6,)),
-        ],
-        hbm=(0, 1),
-        limit=8,
-    )
-    own = moved(payload, along=1)
-    src_index, payload = lax.optimization_barrier((src_index, payload))
+    here = lax.rem(lax.axis_index("narrow"), 2)
+    payload = lax.dynamic_slice(dst, (0, here * half), (depth, half)).astype(BF)
+    own = moved(payload, along=1, copies=True)
+    edges_index = jnp.concatenate([src_index, dst_index, rel_index], axis=0)
+    edges_index, payload = lax.optimization_barrier((edges_index, payload))
 
     src_state = src_state.reshape(1, edges)
     blocks = rows // LANES
@@ -359,13 +351,18 @@
     query, rel0 = call(
         query0_kernel,
         [((tall, edges), BF), ((depth, edges), BF)],
-        [rel, src, src_index, dst_index, rel_index],
+        [rel, src, edges_index],
         "query_step0",
         flops=table,
         limit=32,
     )
     query_c, query_y = moved(query, to=1), moved(query, to=2)
-    query_t, target_at, rel1, count0, column, counts_sent, count1 = call(
+    query, dst_state = lax.optimization_barrier((query, dst_state))
+    state = moved(dst_state.reshape(1, rows), along=1, copies=True)
+    (
+        query_t, target_at, rel1, count0, column, counts_sent, count1,
+        src, src_state, src_index, dst_index,
+    ) = call(
         functools.partial(prep_kernel, rows),
         [
             ((edges, depth), BF),
@@ -375,50 +372,60 @@
             ((LANES, blocks), F32),
             ((2 * blocks, LANES), F32),
             ((1, rows), F32),
+            (src.shape, F32),
+            (src_state.shape, F32),
+            (src_index.shape, I32),
+            (dst_index.shape, I32),
         ],
-        [rel, query, rel_index, neg_index],
+        [rel, query, rel_index, neg_index, src, src_state, src_index, dst_index],
         "prepare",
         flops=table,
         limit=32,
     )
-    own, query_y, query_c, rel1 = lax.optimization_barrier((own, query_y, query_c, rel1))
-    other = moved(own, to=1)
-    query_cy = moved(query_y, to=1)
+    own, query_c, rel1, state = lax.optimization_barrier((own, query_c, rel1, state))
+    other = [moved(own[:, k : k + half // 2], to=1) for k in (0, half // 2)]
 
     query1, src1, src_state1 = call(
         functools.partial(src0_kernel, negatives),
         [((tall, edges), BF), ((depth, edges), F32), ((1, edges), F32)],
         [
-            own, other, query_t, target_at, count0, src, src_state,
+            own, *other, query_t, target_at, count0, src, src_state,
             rel0, rel1, src_index, dst_index, counts_sent,
         ],
         "source_step0",
-        flops=2 * matmul,
         limit=24,
     )
     next_own, next_y = moved(query1, along=-1), moved(query1, along=-1, to=2)
-    own, query1 = lax.optimization_barrier((own, query1))
+    query_y, query1 = lax.optimization_barrier((query_y, query1))
+    query_cy = moved(query_y, to=1)
 
     block1, turned1, delta0, dst_state1 = call(
         functools.partial(dst0_kernel, negatives),
         [((depth, half), BF), ((half, depth), BF), ((depth, half), F32), ((1, half), F32)],
-        [own, query, query_y, query_c, query_cy, column],
+        [own, state, query, query_y, query_c, query_cy, column],
         "destination_step0",
         limit=24,
     )
-    block1_own = moved(block1, along=1)
-    next_own, next_y, block1 = lax.optimization_barrier((next_own, next_y, block1))
-    next_c, next_cy = moved(next_own, to=1), moved(next_y, to=1)
-
+    block1_own = moved(block1, along=1, copies=True)
+    next_c = moved(next_own, to=1)
+
+    first = call(
+        functools.partial(dst1_first_kernel, negatives),
+        [((depth, half), F32)],
+        [turned1, next_own, next_c],
+        "destination_step1_first",
+        limit=24,
+    )
+    next_cy = moved(next_y, to=1)
     delta = call(
         functools.partial(dst1_kernel, negatives),
         [((tall, half), BF)],
-        [turned1, next_own, next_y, next_c, next_cy, delta0, dst_state1],
+        [turned1, first, next_own, next_y, next_cy, delta0, dst_state1],
         "destination_step1",
-        flops=4 * matmul,
+        flops=2 * matmul,
         limit=24,
     )
-    home_own = moved(delta, along=-1)
+    home_own = moved(delta, along=-1, copies=True)
 
     block1_own, delta = lax.optimization_barrier((block1_own, delta))
     block1_other = [moved(block1_own[:, k : k + half // 2], to=1) for k in (0, half // 2)]
@@ -431,13 +438,21 @@
     )
     home_own, src_out = lax.optimization_barrier((home_own, src_out))
     home_other = moved(home_own, to=1)
-    dst_out = call(
-        final_kernel,
-        [((depth, rows), F32)],
-        [dst, home_own, home_other],
-        "destination_out",
-        limit=16,
-    )
+    dst_out = ()
+    for mine, home in ((True, home_own), (False, home_other)):
+        dst_out = (
+            call(
+                functools.partial(final_kernel, mine),
+                [((depth, rows), F32)],
+                [dst, home, *dst_out],
+                "destination_out",
+                scratch=[pltpu.VMEM((depth, half), F32), pltpu.SemaphoreType.DMA((2,))],
+                hbm=(2,),
+                limit=16,
+                out=0 if mine else 2,
+            ),
+        )
+    dst_out = dst_out[0]
     return src_out.T, dst_out.T
 
 

time: 65.2 us -> 61.8 us (0.948)
  waiting for transfers between devices: 26 us -> 15.5 us
  starting transfers between devices: 18.8 us -> 24.5 us
  other arithmetic: 0 us -> 0.72 us
    ppermute x14 -> x16, waiting for transfers between devices: 26 us -> 15.5 us  [moved(): return lax.ppermute(value, ('wide', 'narrow'), pairs)]
    ppermute x14 -> x16, starting transfers between devices: 18.8 us -> 24.5 us  [moved(): return lax.ppermute(value, ('wide', 'narrow'), pairs)]
    convert_element_type x0 -> x1, local copies, waits for them, and re-layouts: none -> 1.2 us  [body(): payload = lax.dynamic_slice(dst, (0, here * half), (depth, half)).astype(BF)]
    unnamed x20 -> x18, local copies, waits for them, and re-layouts: 4.82 us -> 3.72 us
    concatenate x0 -> x1, other arithmetic: none -> 0.72 us  [body(): edges_index = jnp.concatenate([src_index, dst_index, rel_index], axis=0)]
    pallas_call x8 -> x9, Pallas kernels: 14.5 us -> 15 us  [call(): pl.pallas_call(kernel, out_shape=shapes, in_specs=[anywhere if i in hbm e...]
  transfers between devices with their start and end apart: 14 -> 16, of which waited for: 10 -> 10; matrix products, arithmetic and copies ran while one was open for 0% -> 1% of each run, Pallas kernels for 20% -> 23%
where the time goes in v4:
time: 61.8 us; the launch traced here: 61.6 us
  starting transfers between devices  24.5 us (40%)
  waiting for transfers between devices  15.5 us (25%)
  Pallas kernels  15 us (24%)
  local copies, waits for them, and re-layouts  4.97 us (8%)
  between operations  0.92 us (1%)
  other arithmetic  0.72 us (1%)
    ppermute x16, starting transfers between devices, moved(): return lax.ppermute(value, ('wide', 'narrow'), pairs)  24.5 us
    ppermute x16, waiting for transfers between devices, moved(): return lax.ppermute(value, ('wide', 'narrow'), pairs)  15.5 us
    pallas_call x9, Pallas kernels, call(): pl.pallas_call(kernel, out_shape=shapes, in_specs=[anywhere if i in hbm e...  15 us
    unnamed x18, local copies, waits for them, and re-layouts  3.72 us
  transfers between devices with their start and end apart: 16, of which 10 were waited for; matrix products, arithmetic and copies ran while one was open for 1% of the time, Pallas kernels for 23%

profile of v4, /device:TPU:1, one launch (start us, length us, event | category | flops | bytes accessed | tf_op | source)
XLA Modules:
  0.0 61.6 jit_solution(6971566200113751332)
XLA Ops:
  0.6 1.2 %fusion = bf16[400,512]{1,0:T(8,128)(2,1)S(1)} fusion(f32[1024,400]{0,1:T(8,128)} %param.11, s32[]{:T(128)S(6)} %select_n.3), kind=kLoop, calls=%fused_computation.1 | loop fusion | bytes 819204 | tf_op jit(solution)/shard_map/convert_element_type | solution.py:342
  1.8 2.5 %collective-permute-start = (bf16[400,512]{1,0:T(8,128)(2,1)S(1)}, bf16[400,512]{1,0:T(8,128)(2,1)S(1)}, u32[]{:S(2)}, u32[]{:S(2)}) collective-permute-start(bf16[400,512]{1,0:T(8,128)(2,1)S(1)} %fusion), channel_id=1, source_target_pairs={{0,4},{1,5},{2,6},{3,7},{4,8},{5,9},{6,10},{7,11},{8,12},{9,13},{1... | collective-permute-start | bytes 1228808 | tf_op jit(solution)/shard_map/ppermute | solution.py:329
  4.4 0.7 %pad_add_fusion.index = s32[6,256]{1,0:T(8,128)S(1)} fusion(s32[2,256]{1,0:T(2,128)} %bitcast.20, s32[2,256]{1,0:T(2,128)} %bitcast.22, s32[2,256]{1,0:T(2,128)} %bitcast.24), kind=kLoop, calls=%fused_computation.2 | loop fusion | flops 3072 | bytes 12288 | tf_op jit(solution)/shard_map/concatenate | solution.py:344
  5.1 2.7 %copy-done = bf16[7424,400]{0,1:T(8,128)(2,1)S(1)} copy-done((bf16[7424,400]{0,1:T(8,128)(2,1)S(1)}, bf16[7424,400]{0,1:T(8,128)(2,1)}, u32[]{:S(2)}) %copy-start) | copy-done | bytes 5939224
  7.8 1.0 %copy-done.2 = f32[256,400]{0,1:T(8,128)S(1)} copy-done((f32[256,400]{0,1:T(8,128)S(1)}, f32[256,400]{0,1:T(8,128)}, u32[]{:S(2)}) %copy-start.2) | copy-done | bytes 409624
  8.8 0.0 copy-start.6
  8.8 0.0 copy-start.7
  8.8 1.9 %query_step0.1 = (bf16[416,256]{1,0:T(8,128)(2,1)S(1)}, bf16[400,256]{1,0:T(8,128)(2,1)S(1)}) custom-call(bf16[400,7424]{1,0:T(8,128)(2,1)S(1)} %bitcast.13, f32[400,256]{1,0:T(8,128)S(1)} %bitcast.17, s32[6,256]{1,0:T(8,128)S(1)} %pad_add_fusion.index), custom_call_target="tpu_custom_call" | custom-call | flops 1520435200 | bytes 6772736 | tf_op jit(solution)/shard_map/query_step0/pallas_call | solution.py:301
  10.8 1.0 %collective-permute-start.1 = (bf16[416,256]{1,0:T(8,128)(2,1)S(1)}, bf16[416,256]{1,0:T(8,128)(2,1)S(1)}, u32[]{:S(2)}, u32[]{:S(2)}) collective-permute-start(bf16[416,256]{1,0:T(8,128)(2,1)S(1)} %get-tuple-element.36.q_ref.qa), channel_id=1, source_target_pairs={{0,1},{1,0},{2,3},{3,2},{4,5},{5,4},{6,7},{7,6},{8,9},{9,8},{10,11... | collective-permute-start | bytes 638984 | tf_op jit(solution)/shard_map/ppermute | solution.py:329
  11.8 1.3 %collective-permute-start.3 = (bf16[416,256]{1,0:T(8,128)(2,1)S(1)}, bf16[416,256]{1,0:T(8,128)(2,1)S(1)}, u32[]{:S(2)}, u32[]{:S(2)}) collective-permute-start(bf16[416,256]{1,0:T(8,128)(2,1)S(1)} %get-tuple-element.36.q_ref.qa), channel_id=1, source_target_pairs={{0,2},{1,3},{2,0},{3,1},{4,6},{5,7},{6,4},{7,5},{8,10},{9,11},{10,... | collective-permute-start | bytes 638984 | tf_op jit(solution)/shard_map/ppermute | solution.py:329
  13.1 1.6 %collective-permute-start.2 = (f32[1,1024]{1,0:T(1,128)S(1)}, f32[1,1024]{1,0:T(1,128)S(1)}, u32[]{:S(2)}, u32[]{:S(2)}) collective-permute-start(f32[1,1024]{1,0:T(1,128)S(1)} %bitcast.29), channel_id=1, source_target_pairs={{0,4},{1,5},{2,6},{3,7},{4,8},{5,9},{6,10},{7,11},{8,12},{9,13},{1... | collective-permute-start | bytes 12296 | tf_op jit(solution)/shard_map/ppermute | solution.py:329
  14.8 2.3 %prepare.1 = (bf16[256,400]{1,0:T(8,128)(2,1)S(1)}, s32[256,128]{1,0:T(8,128)S(1)}, bf16[400,256]{1,0:T(8,128)(2,1)S(1)}, f32[1,1024]{1,0:T(1,128)S(1)}, f32[128...) custom-call(bf16[400,7424]{1,0:T(8,128)(2,1)S(1)} %bitcast.14, ...), custom_call_target="tpu_custom_call" | custom-call | flops 1520435200 | bytes 7561216 | tf_op jit(solution)/shard_map/prepare/pallas_call | solution.py:301
  17.1 5.1 %collective-permute-done.2.old_ref = f32[1,1024]{1,0:T(1,128)S(1)} collective-permute-done((f32[1,1024]{1,0:T(1,128)S(1)}, f32[1,1024]{1,0:T(1,128)S(1)}, u32[]{:S(2)}, u32[]{:S(2)}) %collective-permute-start.2) | collective-permute-done | bytes 4128 | tf_op jit(solution)/shard_map/ppermute | solution.py:329
  22.2 0.0 collective-permute-done.1.qc
  22.3 0.0 collective-permute-done.own_ref
  22.3 1.3 %collective-permute-start.4 = (bf16[400,256]{1,0:T(8,128)(2,1)S(1)}, bf16[400,256]{1,0:T(8,128)(2,1)S(1)}, u32[]{:S(2)}, u32[]{:S(2)}) collective-permute-start(bf16[400,256]{1,0:T(8,128)(2,1)S(1)} %get-tuple-element.69), channel_id=1, source_target_pairs={{0,1},{1,0},{2,3},{3,2},{4,5},{5,4},{6,7},{7,6},{8,9},{9,8},{10,11... | collective-permute-start | bytes 614408 | tf_op jit(solution)/shard_map/ppermute | solution.py:329
  23.6 0.1 collective-permute-start.5
  23.7 1.0 %collective-permute-done.4.other_a = bf16[400,256]{1,0:T(8,128)(2,1)S(1)} collective-permute-done((bf16[400,256]{1,0:T(8,128)(2,1)S(1)}, bf16[400,256]{1,0:T(8,128)(2,1)S(1)}, u32[]{:S(2)}, u32[]{:S(2)}) %collective-permute-start.4) | collective-permute-done | bytes 204832 | tf_op jit(solution)/shard_map/ppermute | solution.py:329
  24.7 0.4 collective-permute-done.5.other_b
  25.1 1.7 %source_step0.1 = (bf16[416,256]{1,0:T(8,128)(2,1)S(1)}, f32[400,256]{1,0:T(8,128)S(1)}, f32[1,256]{1,0:T(1,128)S(1)}) custom-call(bf16[400,512]{1,0:T(8,128)(2,1)S(1)} %collective-permute-done.own_ref, bf16[400,256]{1,0:T(8,128)(2,1)S(1)} %collective-permute-done.4.other_a, bf16[400,256]{1,0:T(8,128)(2,1)S(1)} %collective-permute-done.5.other_b, ...), custom_call_target="tpu_custom_call" | custom-call | flops 1 | bytes 1 | tf_op jit(solution)/shard_map/source_step0/pallas_call | solution.py:301
  26.8 0.0 collective-permute-done.3.qb
  26.8 0.4 collective-permute-start.6
  27.2 1.8 %collective-permute-start.7 = (bf16[416,256]{1,0:T(8,128)(2,1)S(1)}, bf16[416,256]{1,0:T(8,128)(2,1)S(1)}, u32[]{:S(2)}, u32[]{:S(2)}) collective-permute-start(bf16[416,256]{1,0:T(8,128)(2,1)S(1)} %get-tuple-element.60.q_ref), channel_id=1, source_target_pairs={{0,252},{1,253},{2,254},{3,255},{4,0},{5,1},{6,2},{7,3},{8,4},{9,5... | collective-permute-start | bytes 638984 | tf_op jit(solution)/shard_map/ppermute | solution.py:329
  29.0 1.0 %collective-permute-start.9 = (bf16[416,256]{1,0:T(8,128)(2,1)S(1)}, bf16[416,256]{1,0:T(8,128)(2,1)S(1)}, u32[]{:S(2)}, u32[]{:S(2)}) collective-permute-start(bf16[416,256]{1,0:T(8,128)(2,1)S(1)} %get-tuple-element.60.q_ref), channel_id=1, source_target_pairs={{0,254},{1,255},{2,252},{3,253},{4,2},{5,3},{6,0},{7,1},{8,6},{9,7... | collective-permute-start | bytes 638984 | tf_op jit(solution)/shard_map/ppermute | solution.py:329
  30.0 0.0 collective-permute-done.6.qd
  30.0 2.7 %destination_step0.1 = (bf16[400,512]{1,0:T(8,128)(2,1)S(1)}, bf16[512,400]{1,0:T(8,128)(2,1)S(1)}, f32[400,512]{1,0:T(8,128)S(1)}, f32[1,512]{1,0:T(1,128)S(1)}) custom-call(bf16[400,512]{1,0:T(8,128)(2,1)S(1)} %collective-permute-done.own_ref, f32[1,1024]{1,0:T(1,128)S(1)} %collective-permute-done.2.old_ref, ...), custom_call_target="tpu_custom_call" | custom-call | flops 1 | bytes 1 | tf_op jit(solution)/shard_map/destination_step0/pallas_call | solution.py:301
  32.7 0.5 collective-permute-start.12
  33.1 0.7 %collective-permute-done.7.qa = bf16[416,256]{1,0:T(8,128)(2,1)S(1)} collective-permute-done((bf16[416,256]{1,0:T(8,128)(2,1)S(1)}, bf16[416,256]{1,0:T(8,128)(2,1)S(1)}, u32[]{:S(2)}, u32[]{:S(2)}) %collective-permute-start.7) | collective-permute-done | bytes 213024 | tf_op jit(solution)/shard_map/ppermute | solution.py:329
  33.8 1.7 %collective-permute-start.8 = (bf16[416,256]{1,0:T(8,128)(2,1)S(1)}, bf16[416,256]{1,0:T(8,128)(2,1)S(1)}, u32[]{:S(2)}, u32[]{:S(2)}) collective-permute-start(bf16[416,256]{1,0:T(8,128)(2,1)S(1)} %collective-permute-done.7.qa), channel_id=1, source_target_pairs={{0,1},{1,0},{2,3},{3,2},{4,5},{5,4},{6,7},{7,6},{8,9},{9,8},{10,11... | collective-permute-start | bytes 638984 | tf_op jit(solution)/shard_map/ppermute | solution.py:329
  35.5 2.5 %collective-permute-done.9.qc = bf16[416,256]{1,0:T(8,128)(2,1)S(1)} collective-permute-done((bf16[416,256]{1,0:T(8,128)(2,1)S(1)}, bf16[416,256]{1,0:T(8,128)(2,1)S(1)}, u32[]{:S(2)}, u32[]{:S(2)}) %collective-permute-start.9) | collective-permute-done | bytes 213024 | tf_op jit(solution)/shard_map/ppermute | solution.py:329
  38.0 1.0 %collective-permute-start.10 = (bf16[416,256]{1,0:T(8,128)(2,1)S(1)}, bf16[416,256]{1,0:T(8,128)(2,1)S(1)}, u32[]{:S(2)}, u32[]{:S(2)}) collective-permute-start(bf16[416,256]{1,0:T(8,128)(2,1)S(1)} %collective-permute-done.9.qc), channel_id=1, source_target_pairs={{0,1},{1,0},{2,3},{3,2},{4,5},{5,4},{6,7},{7,6},{8,9},{9,8},{10,11... | collective-permute-start | bytes 638984 | tf_op jit(solution)/shard_map/ppermute | solution.py:329
  39.0 0.0 collective-permute-done.8.qb
  39.0 0.9 %destination_step1_first.1.first_ref = f32[400,512]{1,0:T(8,128)S(1)} custom-call(bf16[512,400]{1,0:T(8,128)(2,1)S(1)} %get-tuple-element.55.turned_ref, bf16[416,256]{1,0:T(8,128)(2,1)S(1)} %collective-permute-done.7.qa, bf16[416,256]{1,0:T(8,128)(2,1)S(1)} %collective-permute-done.8.qb), custom_call_target="tpu_custom_call" | custom-call | flops 1 | bytes 1 | tf_op jit(solution)/shard_map/destination_step1_first/pallas_call | solution.py:301
  40.0 0.1 collective-permute-done.10.qd
  40.1 1.2 %destination_step1.1 = bf16[416,512]{1,0:T(8,128)(2,1)S(1)} custom-call(bf16[512,400]{1,0:T(8,128)(2,1)S(1)} %get-tuple-element.55.turned_ref, f32[400,512]{1,0:T(8,128)S(1)} %destination_step1_first.1.first_ref, bf16[416,256]{1,0:T(8,128)(2,1)S(1)} %collective-permute-done.7.qa, bf16[416,256]{1,0:T(8,128)(2,1)S(1)} %collective-permute-done.9.qc, ...), custom_call_target="tpu_custom_call" | custom-call | flops 419430400 | bytes 3115008 | tf_op jit(solution)/shard_map/destination_step1/pallas_call | solution.py:301
  41.3 0.0 copy-start.1
  41.3 7.7 %collective-permute-start.11 = (bf16[416,512]{1,0:T(8,128)(2,1)S(1)}, bf16[416,512]{1,0:T(8,128)(2,1)S(1)}, u32[]{:S(2)}, u32[]{:S(2)}) collective-permute-start(bf16[416,512]{1,0:T(8,128)(2,1)S(1)} %destination_step1.1), channel_id=1, source_target_pairs={{0,254},{1,255},{2,252},{3,253},{4,0},{5,1},{6,2},{7,3},{8,4},{9,5... | collective-permute-start | bytes 1277960 | tf_op jit(solution)/shard_map/ppermute | solution.py:329
  49.0 0.0 collective-permute-done.12.own_ref
  49.1 1.1 %collective-permute-start.13 = (bf16[400,256]{1,0:T(8,128)(2,1)S(1)}, bf16[400,256]{1,0:T(8,128)(2,1)S(1)}, u32[]{:S(2)}, u32[]{:S(2)}) collective-permute-start(bf16[400,256]{1,0:T(8,128)(2,1)S(1)} %get-tuple-element.67), channel_id=1, source_target_pairs={{0,1},{1,0},{2,3},{3,2},{4,5},{5,4},{6,7},{7,6},{8,9},{9,8},{10,11... | collective-permute-start | bytes 614408 | tf_op jit(solution)/shard_map/ppermute | solution.py:329
  50.2 0.1 collective-permute-start.14
  50.3 1.0 %collective-permute-done.13.other_ref = bf16[400,256]{1,0:T(8,128)(2,1)S(1)} collective-permute-done((bf16[400,256]{1,0:T(8,128)(2,1)S(1)}, bf16[400,256]{1,0:T(8,128)(2,1)S(1)}, u32[]{:S(2)}, u32[]{:S(2)}) %collective-permute-start.13) | collective-permute-done | bytes 204832 | tf_op jit(solution)/shard_map/ppermute | solution.py:329
  51.3 0.4 collective-permute-done.14.last_ref
  51.6 2.3 %source_step1.1 = f32[400,256]{1,0:T(8,128)} custom-call(bf16[400,512]{1,0:T(8,128)(2,1)S(1)} %collective-permute-done.12.own_ref, bf16[400,256]{1,0:T(8,128)(2,1)S(1)} %collective-permute-done.13.other_ref, bf16[400,256]{1,0:T(8,128)(2,1)S(1)} %collective-permute-done.14.last_ref, bf16[416,256]{1,0:T(8,128)(2,1)S(1)} %get-tuple-element.60.q_ref, ...), custom_call_target="tpu_custom_call" | custom-call | flops 1 | bytes 1 | tf_op jit(solution)/shard_map/source_step1/pallas_call | solution.py:301
  53.9 3.9 %collective-permute-done.11.delta_ref = bf16[416,512]{1,0:T(8,128)(2,1)S(1)} collective-permute-done((bf16[416,512]{1,0:T(8,128)(2,1)S(1)}, bf16[416,512]{1,0:T(8,128)(2,1)S(1)}, u32[]{:S(2)}, u32[]{:S(2)}) %collective-permute-start.11) | collective-permute-done | bytes 426016 | tf_op jit(solution)/shard_map/ppermute | solution.py:329
  57.8 1.2 %collective-permute-start.15 = (bf16[416,512]{1,0:T(8,128)(2,1)S(1)}, bf16[416,512]{1,0:T(8,128)(2,1)S(1)}, u32[]{:S(2)}, u32[]{:S(2)}) collective-permute-start(bf16[416,512]{1,0:T(8,128)(2,1)S(1)} %collective-permute-done.11.delta_ref), channel_id=1, source_target_pairs={{0,1},{1,0},{2,3},{3,2},{4,5},{5,4},{6,7},{7,6},{8,9},{9,8},{10,11... | collective-permute-start | bytes 1277960 | tf_op jit(solution)/shard_map/ppermute | solution.py:329
  59.1 1.0 %destination_out.2.refs_0_ = f32[400,1024]{1,0:T(8,128)} custom-call(f32[400,1024]{1,0:T(8,128)S(1)} %bitcast.15, bf16[416,512]{1,0:T(8,128)(2,1)S(1)} %collective-permute-done.11.delta_ref), custom_call_target="tpu_custom_call" | custom-call | flops 1 | bytes 1 | tf_op jit(solution)/shard_map/destination_out/pallas_call | solution.py:301
  60.0 0.4 collective-permute-done.15.delta_ref
  60.4 1.0 %destination_out.3 = f32[400,1024]{1,0:T(8,128)} custom-call(f32[400,1024]{1,0:T(8,128)S(1)} %bitcast.16, bf16[416,512]{1,0:T(8,128)(2,1)S(1)} %collective-permute-done.15.delta_ref, f32[400,1024]{1,0:T(8,128)} %destination_out.2.refs_0_), custom_call_target="tpu_custom_call", output_to_operand_aliasing={{}: (2, {})} | custom-call | flops 1 | bytes 1 | tf_op jit(solution)/shard_map/destination_out/pallas_call | solution.py:301
  (15 shorter events, 0.1 us)
Async XLA Ops:
  1.8 20.4 %collective-permute-start = (bf16[400,512]{1,0:T(8,128)(2,1)S(1)}, bf16[400,512]{1,0:T(8,128)(2,1)S(1)}, u32[]{:S(2)}, u32[]{:S(2)}) collective-permute-start(bf16[400,512]{1,0:T(8,128)(2,1)S(1)} %fusion), channel_id=1, source_target_pairs={{0,4},{1,5},{2,6},{3,7},{4,8},{5,9},{6,10},{7,11},{8,12},{9,13},{1... | collective-permute-start | bytes 1228808 | tf_op jit(solution)/shard_map/ppermute | solution.py:329
  5.1 2.7 %copy-start = (bf16[7424,400]{0,1:T(8,128)(2,1)S(1)}, bf16[7424,400]{0,1:T(8,128)(2,1)}, u32[]{:S(2)}) copy-start(bf16[7424,400]{0,1:T(8,128)(2,1)} %param.13) | copy-start | bytes 17817604
  7.8 1.0 %copy-start.2 = (f32[256,400]{0,1:T(8,128)S(1)}, f32[256,400]{0,1:T(8,128)}, u32[]{:S(2)}) copy-start(f32[256,400]{0,1:T(8,128)} %param.9) | copy-start | bytes 1228804
  8.8 4.3 %copy-start.8 = (f32[1024]{0:T(1024)S(1)}, f32[1024]{0:T(1024)}, u32[]{:S(2)}) copy-start(f32[1024]{0:T(1024)} %param.12) | copy-start | bytes 12292
  8.8 6.0 %copy-start.3 = (s32[1,2,2048]{2,1,0:T(2,128)S(1)}, s32[1,2,2048]{2,1,0:T(2,128)}, u32[]{:S(2)}) copy-start(s32[1,2,2048]{2,1,0:T(2,128)} %param.17) | copy-start | bytes 49156
  8.8 6.0 %copy-start.4 = (s32[1,2,256]{2,1,0:T(2,128)S(1)}, s32[1,2,256]{2,1,0:T(2,128)}, u32[]{:S(2)}) copy-start(s32[1,2,256]{2,1,0:T(2,128)} %param.16) | copy-start | bytes 6148
  8.8 6.0 %copy-start.5 = (s32[1,2,256]{2,1,0:T(2,128)S(1)}, s32[1,2,256]{2,1,0:T(2,128)}, u32[]{:S(2)}) copy-start(s32[1,2,256]{2,1,0:T(2,128)} %param.15) | copy-start | bytes 6148
  8.8 6.0 %copy-start.6 = (s32[1,2,256]{2,1,0:T(2,128)S(1)}, s32[1,2,256]{2,1,0:T(2,128)}, u32[]{:S(2)}) copy-start(s32[1,2,256]{2,1,0:T(2,128)} %param.14) | copy-start | bytes 6148
  8.8 6.0 %copy-start.7 = (f32[256]{0:T(256)S(1)}, f32[256]{0:T(256)}, u32[]{:S(2)}) copy-start(f32[256]{0:T(256)} %param.10) | copy-start | bytes 3076
  10.8 11.5 %collective-permute-start.1 = (bf16[416,256]{1,0:T(8,128)(2,1)S(1)}, bf16[416,256]{1,0:T(8,128)(2,1)S(1)}, u32[]{:S(2)}, u32[]{:S(2)}) collective-permute-start(bf16[416,256]{1,0:T(8,128)(2,1)S(1)} %get-tuple-element.36.q_ref.qa), channel_id=1, source_target_pairs={{0,1},{1,0},{2,3},{3,2},{4,5},{5,4},{6,7},{7,6},{8,9},{9,8},{10,11... | collective-permute-start | bytes 638984 | tf_op jit(solution)/shard_map/ppermute | solution.py:329
  11.8 15.0 %collective-permute-start.3 = (bf16[416,256]{1,0:T(8,128)(2,1)S(1)}, bf16[416,256]{1,0:T(8,128)(2,1)S(1)}, u32[]{:S(2)}, u32[]{:S(2)}) collective-permute-start(bf16[416,256]{1,0:T(8,128)(2,1)S(1)} %get-tuple-element.36.q_ref.qa), channel_id=1, source_target_pairs={{0,2},{1,3},{2,0},{3,1},{4,6},{5,7},{6,4},{7,5},{8,10},{9,11},{10,... | collective-permute-start | bytes 638984 | tf_op jit(solution)/shard_map/ppermute | solution.py:329
  13.1 9.1 %collective-permute-start.2 = (f32[1,1024]{1,0:T(1,128)S(1)}, f32[1,1024]{1,0:T(1,128)S(1)}, u32[]{:S(2)}, u32[]{:S(2)}) collective-permute-start(f32[1,1024]{1,0:T(1,128)S(1)} %bitcast.29), channel_id=1, source_target_pairs={{0,4},{1,5},{2,6},{3,7},{4,8},{5,9},{6,10},{7,11},{8,12},{9,13},{1... | collective-permute-start | bytes 12296 | tf_op jit(solution)/shard_map/ppermute | solution.py:329
  22.3 2.4 %collective-permute-start.4 = (bf16[400,256]{1,0:T(8,128)(2,1)S(1)}, bf16[400,256]{1,0:T(8,128)(2,1)S(1)}, u32[]{:S(2)}, u32[]{:S(2)}) collective-permute-start(bf16[400,256]{1,0:T(8,128)(2,1)S(1)} %get-tuple-element.69), channel_id=1, source_target_pairs={{0,1},{1,0},{2,3},{3,2},{4,5},{5,4},{6,7},{7,6},{8,9},{9,8},{10,11... | collective-permute-start | bytes 614408 | tf_op jit(solution)/shard_map/ppermute | solution.py:329
  23.6 1.5 %collective-permute-start.5 = (bf16[400,256]{1,0:T(8,128)(2,1)S(1)}, bf16[400,256]{1,0:T(8,128)(2,1)S(1)}, u32[]{:S(2)}, u32[]{:S(2)}) collective-permute-start(bf16[400,256]{1,0:T(8,128)(2,1)S(1)} %get-tuple-element.68), channel_id=1, source_target_pairs={{0,1},{1,0},{2,3},{3,2},{4,5},{5,4},{6,7},{7,6},{8,9},{9,8},{10,11... | collective-permute-start | bytes 614408 | tf_op jit(solution)/shard_map/ppermute | solution.py:329
  26.8 3.2 %collective-permute-start.6 = (bf16[416,256]{1,0:T(8,128)(2,1)S(1)}, bf16[416,256]{1,0:T(8,128)(2,1)S(1)}, u32[]{:S(2)}, u32[]{:S(2)}) collective-permute-start(bf16[416,256]{1,0:T(8,128)(2,1)S(1)} %collective-permute-done.3.qb), channel_id=1, source_target_pairs={{0,1},{1,0},{2,3},{3,2},{4,5},{5,4},{6,7},{7,6},{8,9},{9,8},{10,11... | collective-permute-start | bytes 638984 | tf_op jit(solution)/shard_map/ppermute | solution.py:329
  27.2 6.6 %collective-permute-start.7 = (bf16[416,256]{1,0:T(8,128)(2,1)S(1)}, bf16[416,256]{1,0:T(8,128)(2,1)S(1)}, u32[]{:S(2)}, u32[]{:S(2)}) collective-permute-start(bf16[416,256]{1,0:T(8,128)(2,1)S(1)} %get-tuple-element.60.q_ref), channel_id=1, source_target_pairs={{0,252},{1,253},{2,254},{3,255},{4,0},{5,1},{6,2},{7,3},{8,4},{9,5... | collective-permute-start | bytes 638984 | tf_op jit(solution)/shard_map/ppermute | solution.py:329
  29.0 9.0 %collective-permute-start.9 = (bf16[416,256]{1,0:T(8,128)(2,1)S(1)}, bf16[416,256]{1,0:T(8,128)(2,1)S(1)}, u32[]{:S(2)}, u32[]{:S(2)}) collective-permute-start(bf16[416,256]{1,0:T(8,128)(2,1)S(1)} %get-tuple-element.60.q_ref), channel_id=1, source_target_pairs={{0,254},{1,255},{2,252},{3,253},{4,2},{5,3},{6,0},{7,1},{8,6},{9,7... | collective-permute-start | bytes 638984 | tf_op jit(solution)/shard_map/ppermute | solution.py:329
  32.7 16.4 %collective-permute-start.12 = (bf16[400,512]{1,0:T(8,128)(2,1)S(1)}, bf16[400,512]{1,0:T(8,128)(2,1)S(1)}, u32[]{:S(2)}, u32[]{:S(2)}) collective-permute-start(bf16[400,512]{1,0:T(8,128)(2,1)S(1)} %get-tuple-element.58), channel_id=1, source_target_pairs={{0,4},{1,5},{2,6},{3,7},{4,8},{5,9},{6,10},{7,11},{8,12},{9,13},{1... | collective-permute-start | bytes 1228808 | tf_op jit(solution)/shard_map/ppermute | solution.py:329
  33.8 5.2 %collective-permute-start.8 = (bf16[416,256]{1,0:T(8,128)(2,1)S(1)}, bf16[416,256]{1,0:T(8,128)(2,1)S(1)}, u32[]{:S(2)}, u32[]{:S(2)}) collective-permute-start(bf16[416,256]{1,0:T(8,128)(2,1)S(1)} %collective-permute-done.7.qa), channel_id=1, source_target_pairs={{0,1},{1,0},{2,3},{3,2},{4,5},{5,4},{6,7},{7,6},{8,9},{9,8},{10,11... | collective-permute-start | bytes 638984 | tf_op jit(solution)/shard_map/ppermute | solution.py:329
  38.0 2.1 %collective-permute-start.10 = (bf16[416,256]{1,0:T(8,128)(2,1)S(1)}, bf16[416,256]{1,0:T(8,128)(2,1)S(1)}, u32[]{:S(2)}, u32[]{:S(2)}) collective-permute-start(bf16[416,256]{1,0:T(8,128)(2,1)S(1)} %collective-permute-done.9.qc), channel_id=1, source_target_pairs={{0,1},{1,0},{2,3},{3,2},{4,5},{5,4},{6,7},{7,6},{8,9},{9,8},{10,11... | collective-permute-start | bytes 638984 | tf_op jit(solution)/shard_map/ppermute | solution.py:329
  41.3 17.8 %copy-start.1 = (f32[1024,400]{0,1:T(8,128)S(1)}, f32[1024,400]{0,1:T(8,128)}, u32[]{:S(2)}) copy-start(f32[1024,400]{0,1:T(8,128)} %param.11) | copy-start | bytes 4915204
  41.3 16.5 %collective-permute-start.11 = (bf16[416,512]{1,0:T(8,128)(2,1)S(1)}, bf16[416,512]{1,0:T(8,128)(2,1)S(1)}, u32[]{:S(2)}, u32[]{:S(2)}) collective-permute-start(bf16[416,512]{1,0:T(8,128)(2,1)S(1)} %destination_step1.1), channel_id=1, source_target_pairs={{0,254},{1,255},{2,252},{3,253},{4,0},{5,1},{6,2},{7,3},{8,4},{9,5... | collective-permute-start | bytes 1277960 | tf_op jit(solution)/shard_map/ppermute | solution.py:329
  49.1 2.2 %collective-permute-start.13 = (bf16[400,256]{1,0:T(8,128)(2,1)S(1)}, bf16[400,256]{1,0:T(8,128)(2,1)S(1)}, u32[]{:S(2)}, u32[]{:S(2)}) collective-permute-start(bf16[400,256]{1,0:T(8,128)(2,1)S(1)} %get-tuple-element.67), channel_id=1, source_target_pairs={{0,1},{1,0},{2,3},{3,2},{4,5},{5,4},{6,7},{7,6},{8,9},{9,8},{10,11... | collective-permute-start | bytes 614408 | tf_op jit(solution)/shard_map/ppermute | solution.py:329
  50.2 1.5 %collective-permute-start.14 = (bf16[400,256]{1,0:T(8,128)(2,1)S(1)}, bf16[400,256]{1,0:T(8,128)(2,1)S(1)}, u32[]{:S(2)}, u32[]{:S(2)}) collective-permute-start(bf16[400,256]{1,0:T(8,128)(2,1)S(1)} %get-tuple-element.66), channel_id=1, source_target_pairs={{0,1},{1,0},{2,3},{3,2},{4,5},{5,4},{6,7},{7,6},{8,9},{9,8},{10,11... | collective-permute-start | bytes 614408 | tf_op jit(solution)/shard_map/ppermute | solution.py:329
  57.8 2.6 %collective-permute-start.15 = (bf16[416,512]{1,0:T(8,128)(2,1)S(1)}, bf16[416,512]{1,0:T(8,128)(2,1)S(1)}, u32[]{:S(2)}, u32[]{:S(2)}) collective-permute-start(bf16[416,512]{1,0:T(8,128)(2,1)S(1)} %collective-permute-done.11.delta_ref), channel_id=1, source_target_pairs={{0,1},{1,0},{2,3},{3,2},{4,5},{5,4},{6,7},{7,6},{8,9},{9,8},{10,11... | collective-permute-start | bytes 1277960 | tf_op jit(solution)/shard_map/ppermute | solution.py:329

commit v5 on v4

--- a/solution.py
+++ b/solution.py
@@ -14,6 +14,7 @@
 META = 16
 FINE = 32
 LANES = 128
+ROW_CUTS = 0, 144, 272
 PIECE = 1920
 
 
@@ -161,13 +162,23 @@
     return total
 
 
+def src0_first_kernel(negatives, own_ref, qt_ref, at_ref, count_ref, grad_out):
+    half = own_ref.shape[1]
+    grad_out[...] = query_gradient(
+        negatives, [own_ref[...]], qt_ref[...], at_ref[:, 0:1], count_ref[:, :half]
+    )
+
+
 def src0_kernel(
-    negatives, own_ref, other_a, other_b, qt_ref, at_ref, count_ref, src_ref, state_ref,
+    negatives, first_ref, other_a, other_b, qt_ref, at_ref, count_ref, src_ref, state_ref,
     rel0_ref, rel1_ref, src_index, dst_index, next_ref, q_ref, src_out, state_out,
 ):
     depth, edges = src_ref.shape
-    blocks = own_ref[...], jnp.concatenate([other_a[...], other_b[...]], axis=1)
-    grad = query_gradient(negatives, blocks, qt_ref[...], at_ref[:, 0:1], count_ref)
+    block = jnp.concatenate([other_a[...], other_b[...]], axis=1)
+    half = block.shape[1]
+    grad = first_ref[...] + query_gradient(
+        negatives, [block], qt_ref[...], at_ref[:, 0:1] - half, count_ref[:, half:]
+    )
     gradient = summed(grad * rel0_ref[...].astype(F32), one_hot(edges, src_index[0:1, :]))
     state, size = step_size(state_ref[...], gradient)
     src = src_ref[...] - gradient * size
@@ -183,13 +194,13 @@
 
 
 def src1_kernel(
-    negatives, own_ref, other_ref, last_ref, q_ref, count_ref, src_ref, state_ref, rel_ref,
+    negatives, own_ref, other_a, other_b, other_c, q_ref, count_ref, src_ref, state_ref, rel_ref,
     src_index, src_out,
 ):
     depth, edges = src_ref.shape
     half = own_ref.shape[1]
     query_t, target_at = turned_query(q_ref, depth, core() * half)
-    blocks = own_ref[...], other_ref[...], last_ref[...]
+    blocks = own_ref[...], jnp.concatenate([other_a[...], other_b[...], other_c[...]], axis=0)
     grad = query_gradient(negatives, blocks, query_t, target_at, count_ref)
     gradient = summed(grad * rel_ref[...].astype(F32), one_hot(edges, src_index[1:2, :]))
     _, size = step_size(state_ref[...], gradient)
@@ -218,11 +229,11 @@
     return coefficients(scores, count, target, negatives)
 
 
-def dst_gradient(block_t, q_refs, column, flip, negatives):
+def dst_gradient(block_t, q_refs, column, flip, negatives, start=0):
     rows, depth = block_t.shape
     total = jnp.zeros((depth, rows), F32)
     for q_ref in q_refs:
-        weights = row_coefficients(block_t, 0, q_ref, column, flip, negatives)
+        weights = row_coefficients(block_t, start, q_ref, column, flip, negatives)
         total += dot_nt(q_ref[:depth, :], weights)
     return total
 
@@ -256,38 +267,37 @@
     state_out[...] = state
 
 
-def dst1_first_kernel(negatives, turned_ref, qa, qb, grad_out):
+def dst1_first_kernel(negatives, turned_ref, qa, qb, qc, grad_out):
     depth, half = grad_out.shape
     grad_out[...] = dst_gradient(
-        turned_ref[...], (qa, qb), sent_counts(qa, depth), core() * half, negatives
+        turned_ref[...], (qa, qb, qc), sent_counts(qa, depth), core() * half, negatives
     )
 
 
 def dst1_kernel(
-    negatives, turned_ref, first_ref, qa, qc, qd, delta_ref, state_ref, delta_out
-):
+    negatives, start, turned_ref, first_ref, qa, qd, delta_ref, state_ref, *refs
+):
+    delta_out = refs[-1]
     depth, half = delta_ref.shape
-    gradient = first_ref[...] + dst_gradient(
-        turned_ref[...], (qc, qd), sent_counts(qa, depth), core() * half, negatives
-    )
-    _, size = step_size(state_ref[...], gradient)
-    delta_out[:depth, :] = (delta_ref[...] + gradient * size).astype(BF)
-    delta_out[depth:, :] = jnp.zeros((META, half), BF)
-
-
-def final_kernel(mine, emb_ref, delta_ref, *refs):
+    part = slice(start, start + delta_out.shape[1])
+    gradient = first_ref[:, part] + dst_gradient(
+        turned_ref[part, :], (qd,), sent_counts(qa, depth), core() * half, negatives, start
+    )
+    _, size = step_size(state_ref[:, part], gradient)
+    delta_out[...] = (delta_ref[:, part] + gradient * size).astype(BF)
+
+
+def final_kernel(start, parts, emb_ref, own_ref, *refs):
     out_ref, held, sems = refs[-3:]
-    depth, half = held.shape
-    place = core() if mine else 1 - core()
+    size = own_ref.shape[1]
+    other = jnp.concatenate([ref[...] for ref in refs[:parts]], axis=1)
+    half = emb_ref.shape[1] // 2
+    here = core()
     copies = []
-    for i in range(2):
-        size = half // 2
-        columns = pl.ds(pl.multiple_of(place * half + i * size, size), size)
-        part = slice(i * size, (i + 1) * size)
-        held[:, part] = emb_ref[:, columns] - delta_ref[:depth, part].astype(F32)
-        copies.append(
-            pltpu.make_async_copy(held.at[:, part], out_ref.at[:, columns], sems.at[i])
-        )
+    for i, (place, delta) in enumerate(((here, own_ref[...]), (1 - here, other))):
+        columns = pl.ds(pl.multiple_of(place * half + start, size), size)
+        held[i] = emb_ref[:, columns] - delta.astype(F32)
+        copies.append(pltpu.make_async_copy(held.at[i], out_ref.at[:, columns], sems.at[i]))
         copies[-1].start()
     for copy in copies:
         copy.wait()
@@ -385,11 +395,18 @@
     own, query_c, rel1, state = lax.optimization_barrier((own, query_c, rel1, state))
     other = [moved(own[:, k : k + half // 2], to=1) for k in (0, half // 2)]
 
+    first = call(
+        functools.partial(src0_first_kernel, negatives),
+        [((depth, edges), F32)],
+        [own, query_t, target_at, count0],
+        "source_step0_first",
+        limit=24,
+    )
     query1, src1, src_state1 = call(
         functools.partial(src0_kernel, negatives),
         [((tall, edges), BF), ((depth, edges), F32), ((1, edges), F32)],
         [
-            own, *other, query_t, target_at, count0, src, src_state,
+            first, *other, query_t, target_at, count0, src, src_state,
             rel0, rel1, src_index, dst_index, counts_sent,
         ],
         "source_step0",
@@ -412,23 +429,29 @@
     first = call(
         functools.partial(dst1_first_kernel, negatives),
         [((depth, half), F32)],
-        [turned1, next_own, next_c],
+        [turned1, next_own, next_c, next_y],
         "destination_step1_first",
         limit=24,
     )
     next_cy = moved(next_y, to=1)
-    delta = call(
-        functools.partial(dst1_kernel, negatives),
-        [((tall, half), BF)],
-        [turned1, first, next_own, next_y, next_cy, delta0, dst_state1],
-        "destination_step1",
-        flops=2 * matmul,
-        limit=24,
-    )
-    home_own = moved(delta, along=-1, copies=True)
-
-    block1_own, delta = lax.optimization_barrier((block1_own, delta))
-    block1_other = [moved(block1_own[:, k : k + half // 2], to=1) for k in (0, half // 2)]
+    piece = half // 2
+    deltas = []
+    for start in range(0, half, piece):
+        deltas.append(
+            call(
+                functools.partial(dst1_kernel, negatives, start),
+                [((depth, piece), BF)],
+                [turned1, first, next_own, next_cy, delta0, dst_state1, *deltas],
+                "destination_step1",
+                limit=24,
+            )
+        )
+    homes = [moved(delta, along=-1, copies=True) for delta in deltas]
+
+    block1_own, *_ = lax.optimization_barrier((block1_own, *deltas))
+    block1_other = [
+        moved(block1_own[a:b], to=1) for a, b in zip(ROW_CUTS, (*ROW_CUTS[1:], depth))
+    ]
     src_out = call(
         functools.partial(src1_kernel, negatives),
         [((depth, edges), F32)],
@@ -436,20 +459,26 @@
         "source_step1",
         limit=24,
     )
-    home_own, src_out = lax.optimization_barrier((home_own, src_out))
-    home_other = moved(home_own, to=1)
+    homes[0], src_out = lax.optimization_barrier((homes[0], src_out))
+    def exchanged(home, parts):
+        size = piece // parts
+        return [moved(home[:, k * size : (k + 1) * size], to=1) for k in range(parts)]
+
     dst_out = ()
-    for mine, home in ((True, home_own), (False, home_other)):
+    for i, home in enumerate(homes):
+        if i:
+            home, *dst_out = lax.optimization_barrier((home, *dst_out))
         dst_out = (
             call(
-                functools.partial(final_kernel, mine),
+                functools.partial(final_kernel, i * piece, 2 - i),
                 [((depth, rows), F32)],
-                [dst, home, *dst_out],
+                [dst, home, *exchanged(home, 2 - i), *dst_out],
                 "destination_out",
-                scratch=[pltpu.VMEM((depth, half), F32), pltpu.SemaphoreType.DMA((2,))],
-                hbm=(2,),
+                flops=i * matmul // 4,
+                scratch=[pltpu.VMEM((2, depth, piece), F32), pltpu.SemaphoreType.DMA((2,))],
+                hbm=(3,) if i else (),
                 limit=16,
-                out=0 if mine else 2,
+                out=3 * i,
             ),
         )
     dst_out = dst_out[0]

time: 61.8 us -> 60.6 us (0.981)
  waiting for transfers between devices: 15.5 us -> 13.2 us
  Pallas kernels: 15 us -> 15.8 us
    ppermute x16 -> x20, waiting for transfers between devices: 15.5 us -> 13.2 us  [moved(): return lax.ppermute(value, ('wide', 'narrow'), pairs)]
    pallas_call x9 -> x11, Pallas kernels: 15 us -> 15.8 us  [call(): pl.pallas_call(kernel, out_shape=shapes, in_specs=[anywhere if i in hbm e...]
    ppermute x16 -> x20, starting transfers between devices: 24.5 us -> 24.7 us  [moved(): return lax.ppermute(value, ('wide', 'narrow'), pairs)]
  transfers between devices with their start and end apart: 16 -> 20, of which waited for: 10 -> 11; matrix products, arithmetic and copies ran while one was open for 1% -> 1% of each run, Pallas kernels for 23% -> 25%
where the time goes in v5:
time: 60.6 us; the launch traced here: 60.3 us
  starting transfers between devices  24.7 us (41%)
  Pallas kernels  15.8 us (26%)
  waiting for transfers between devices  13.2 us (22%)
  local copies, waits for them, and re-layouts  4.99 us (8%)
  between operations  0.97 us (2%)
  other arithmetic  0.72 us (1%)
    ppermute x20, starting transfers between devices, moved(): return lax.ppermute(value, ('wide', 'narrow'), pairs)  24.7 us
    pallas_call x11, Pallas kernels, call(): pl.pallas_call(kernel, out_shape=shapes, in_specs=[anywhere if i in hbm e...  15.8 us
    ppermute x20, waiting for transfers between devices, moved(): return lax.ppermute(value, ('wide', 'narrow'), pairs)  13.2 us
    unnamed x18, local copies, waits for them, and re-layouts  3.72 us
  transfers between devices with their start and end apart: 20, of which 11 were waited for; matrix products, arithmetic and copies ran while one was open for 1% of the time, Pallas kernels for 25%

profile of v5, /device:TPU:1, one launch (start us, length us, event | category | flops | bytes accessed | tf_op | source)
XLA Modules:
  0.0 60.3 jit_solution(7671334595207172010)
XLA Ops:
  0.6 1.2 %fusion = bf16[400,512]{1,0:T(8,128)(2,1)S(1)} fusion(f32[1024,400]{0,1:T(8,128)} %param.11, s32[]{:T(128)S(6)} %select_n.3), kind=kLoop, calls=%fused_computation.1 | loop fusion | bytes 819204 | tf_op jit(solution)/shard_map/convert_element_type | solution.py:352
  1.8 2.5 %collective-permute-start = (bf16[400,512]{1,0:T(8,128)(2,1)S(1)}, bf16[400,512]{1,0:T(8,128)(2,1)S(1)}, u32[]{:S(2)}, u32[]{:S(2)}) collective-permute-start(bf16[400,512]{1,0:T(8,128)(2,1)S(1)} %fusion), channel_id=1, source_target_pairs={{0,4},{1,5},{2,6},{3,7},{4,8},{5,9},{6,10},{7,11},{8,12},{9,13},{1... | collective-permute-start | bytes 1228808 | tf_op jit(solution)/shard_map/ppermute | solution.py:339
  4.4 0.7 %pad_add_fusion.index = s32[6,256]{1,0:T(8,128)S(1)} fusion(s32[2,256]{1,0:T(2,128)} %bitcast.20, s32[2,256]{1,0:T(2,128)} %bitcast.22, s32[2,256]{1,0:T(2,128)} %bitcast.24), kind=kLoop, calls=%fused_computation.2 | loop fusion | flops 3072 | bytes 12288 | tf_op jit(solution)/shard_map/concatenate | solution.py:354
  5.1 2.7 %copy-done = bf16[7424,400]{0,1:T(8,128)(2,1)S(1)} copy-done((bf16[7424,400]{0,1:T(8,128)(2,1)S(1)}, bf16[7424,400]{0,1:T(8,128)(2,1)}, u32[]{:S(2)}) %copy-start) | copy-done | bytes 5939224
  7.8 1.0 %copy-done.2 = f32[256,400]{0,1:T(8,128)S(1)} copy-done((f32[256,400]{0,1:T(8,128)S(1)}, f32[256,400]{0,1:T(8,128)}, u32[]{:S(2)}) %copy-start.2) | copy-done | bytes 409624
  8.8 0.0 copy-start.6
  8.8 0.0 copy-start.7
  8.8 1.9 %query_step0.1 = (bf16[416,256]{1,0:T(8,128)(2,1)S(1)}, bf16[400,256]{1,0:T(8,128)(2,1)S(1)}) custom-call(bf16[400,7424]{1,0:T(8,128)(2,1)S(1)} %bitcast.13, f32[400,256]{1,0:T(8,128)S(1)} %bitcast.17, s32[6,256]{1,0:T(8,128)S(1)} %pad_add_fusion.index), custom_call_target="tpu_custom_call" | custom-call | flops 1520435200 | bytes 6772736 | tf_op jit(solution)/shard_map/query_step0/pallas_call | solution.py:311
  10.8 1.0 %collective-permute-start.1 = (bf16[416,256]{1,0:T(8,128)(2,1)S(1)}, bf16[416,256]{1,0:T(8,128)(2,1)S(1)}, u32[]{:S(2)}, u32[]{:S(2)}) collective-permute-start(bf16[416,256]{1,0:T(8,128)(2,1)S(1)} %get-tuple-element.38.q_ref.qa), channel_id=1, source_target_pairs={{0,1},{1,0},{2,3},{3,2},{4,5},{5,4},{6,7},{7,6},{8,9},{9,8},{10,11... | collective-permute-start | bytes 638984 | tf_op jit(solution)/shard_map/ppermute | solution.py:339
  11.8 1.3 %collective-permute-start.3 = (bf16[416,256]{1,0:T(8,128)(2,1)S(1)}, bf16[416,256]{1,0:T(8,128)(2,1)S(1)}, u32[]{:S(2)}, u32[]{:S(2)}) collective-permute-start(bf16[416,256]{1,0:T(8,128)(2,1)S(1)} %get-tuple-element.38.q_ref.qa), channel_id=1, source_target_pairs={{0,2},{1,3},{2,0},{3,1},{4,6},{5,7},{6,4},{7,5},{8,10},{9,11},{10,... | collective-permute-start | bytes 638984 | tf_op jit(solution)/shard_map/ppermute | solution.py:339
  13.1 1.6 %collective-permute-start.2 = (f32[1,1024]{1,0:T(1,128)S(1)}, f32[1,1024]{1,0:T(1,128)S(1)}, u32[]{:S(2)}, u32[]{:S(2)}) collective-permute-start(f32[1,1024]{1,0:T(1,128)S(1)} %bitcast.29), channel_id=1, source_target_pairs={{0,4},{1,5},{2,6},{3,7},{4,8},{5,9},{6,10},{7,11},{8,12},{9,13},{1... | collective-permute-start | bytes 12296 | tf_op jit(solution)/shard_map/ppermute | solution.py:339
  14.8 2.3 %prepare.1 = (bf16[256,400]{1,0:T(8,128)(2,1)S(1)}, s32[256,128]{1,0:T(8,128)S(1)}, bf16[400,256]{1,0:T(8,128)(2,1)S(1)}, f32[1,1024]{1,0:T(1,128)S(1)}, f32[128...) custom-call(bf16[400,7424]{1,0:T(8,128)(2,1)S(1)} %bitcast.14, ...), custom_call_target="tpu_custom_call" | custom-call | flops 1520435200 | bytes 7561216 | tf_op jit(solution)/shard_map/prepare/pallas_call | solution.py:311
  17.1 5.1 %collective-permute-done.2.old_ref = f32[1,1024]{1,0:T(1,128)S(1)} collective-permute-done((f32[1,1024]{1,0:T(1,128)S(1)}, f32[1,1024]{1,0:T(1,128)S(1)}, u32[]{:S(2)}, u32[]{:S(2)}) %collective-permute-start.2) | collective-permute-done | bytes 4128 | tf_op jit(solution)/shard_map/ppermute | solution.py:339
  22.3 1.3 %collective-permute-start.4 = (bf16[400,256]{1,0:T(8,128)(2,1)S(1)}, bf16[400,256]{1,0:T(8,128)(2,1)S(1)}, u32[]{:S(2)}, u32[]{:S(2)}) collective-permute-start(bf16[400,256]{1,0:T(8,128)(2,1)S(1)} %get-tuple-element.73), channel_id=1, source_target_pairs={{0,1},{1,0},{2,3},{3,2},{4,5},{5,4},{6,7},{7,6},{8,9},{9,8},{10,11... | collective-permute-start | bytes 614408 | tf_op jit(solution)/shard_map/ppermute | solution.py:339
  23.6 0.1 collective-permute-start.5
  23.7 0.6 %source_step0_first.1.first_ref = f32[400,256]{1,0:T(8,128)S(1)} custom-call(bf16[400,512]{1,0:T(8,128)(2,1)S(1)} %collective-permute-done.own_ref, bf16[256,400]{1,0:T(8,128)(2,1)S(1)} %get-tuple-element.43.qt_ref, s32[256,128]{1,0:T(8,128)S(1)} %get-tuple-element.44.at_ref, f32[1,1024]{1,0:T(1,128)S(1)} %get-tuple-element.45.count_ref), custom_call_target="tpu_custom_call" | custom-call | flops 1 | bytes 1 | tf_op jit(solution)/shard_map/source_step0_first/pallas_call | solution.py:311
  24.4 0.3 collective-permute-done.4.other_a
  24.7 0.4 collective-permute-done.5.other_b
  25.1 1.3 %source_step0.1 = (bf16[416,256]{1,0:T(8,128)(2,1)S(1)}, f32[400,256]{1,0:T(8,128)S(1)}, f32[1,256]{1,0:T(1,128)S(1)}) custom-call(f32[400,256]{1,0:T(8,128)S(1)} %source_step0_first.1.first_ref, bf16[400,256]{1,0:T(8,128)(2,1)S(1)} %collective-permute-done.4.other_a, bf16[400,256]{1,0:T(8,128)(2,1)S(1)} %collective-permute-done.5.other_b, ...), custom_call_target="tpu_custom_call" | custom-call | flops 1 | bytes 1 | tf_op jit(solution)/shard_map/source_step0/pallas_call | solution.py:311
  26.4 0.4 collective-permute-start.6
  26.8 1.8 %collective-permute-start.7 = (bf16[416,256]{1,0:T(8,128)(2,1)S(1)}, bf16[416,256]{1,0:T(8,128)(2,1)S(1)}, u32[]{:S(2)}, u32[]{:S(2)}) collective-permute-start(bf16[416,256]{1,0:T(8,128)(2,1)S(1)} %get-tuple-element.62.q_ref), channel_id=1, source_target_pairs={{0,252},{1,253},{2,254},{3,255},{4,0},{5,1},{6,2},{7,3},{8,4},{9,5... | collective-permute-start | bytes 638984 | tf_op jit(solution)/shard_map/ppermute | solution.py:339
  28.6 1.0 %collective-permute-start.9 = (bf16[416,256]{1,0:T(8,128)(2,1)S(1)}, bf16[416,256]{1,0:T(8,128)(2,1)S(1)}, u32[]{:S(2)}, u32[]{:S(2)}) collective-permute-start(bf16[416,256]{1,0:T(8,128)(2,1)S(1)} %get-tuple-element.62.q_ref), channel_id=1, source_target_pairs={{0,254},{1,255},{2,252},{3,253},{4,2},{5,3},{6,0},{7,1},{8,6},{9,7... | collective-permute-start | bytes 638984 | tf_op jit(solution)/shard_map/ppermute | solution.py:339
  29.6 2.7 %destination_step0.1 = (bf16[400,512]{1,0:T(8,128)(2,1)S(1)}, bf16[512,400]{1,0:T(8,128)(2,1)S(1)}, f32[400,512]{1,0:T(8,128)S(1)}, f32[1,512]{1,0:T(1,128)S(1)}) custom-call(bf16[400,512]{1,0:T(8,128)(2,1)S(1)} %collective-permute-done.own_ref, f32[1,1024]{1,0:T(1,128)S(1)} %collective-permute-done.2.old_ref, ...), custom_call_target="tpu_custom_call" | custom-call | flops 1 | bytes 1 | tf_op jit(solution)/shard_map/destination_step0/pallas_call | solution.py:311
  32.3 0.5 collective-permute-start.12
  32.7 0.7 %collective-permute-done.7.qa = bf16[416,256]{1,0:T(8,128)(2,1)S(1)} collective-permute-done((bf16[416,256]{1,0:T(8,128)(2,1)S(1)}, bf16[416,256]{1,0:T(8,128)(2,1)S(1)}, u32[]{:S(2)}, u32[]{:S(2)}) %collective-permute-start.7) | collective-permute-done | bytes 213024 | tf_op jit(solution)/shard_map/ppermute | solution.py:339
  33.4 1.7 %collective-permute-start.8 = (bf16[416,256]{1,0:T(8,128)(2,1)S(1)}, bf16[416,256]{1,0:T(8,128)(2,1)S(1)}, u32[]{:S(2)}, u32[]{:S(2)}) collective-permute-start(bf16[416,256]{1,0:T(8,128)(2,1)S(1)} %collective-permute-done.7.qa), channel_id=1, source_target_pairs={{0,1},{1,0},{2,3},{3,2},{4,5},{5,4},{6,7},{7,6},{8,9},{9,8},{10,11... | collective-permute-start | bytes 638984 | tf_op jit(solution)/shard_map/ppermute | solution.py:339
  35.1 2.5 %collective-permute-done.9.qc = bf16[416,256]{1,0:T(8,128)(2,1)S(1)} collective-permute-done((bf16[416,256]{1,0:T(8,128)(2,1)S(1)}, bf16[416,256]{1,0:T(8,128)(2,1)S(1)}, u32[]{:S(2)}, u32[]{:S(2)}) %collective-permute-start.9) | collective-permute-done | bytes 213024 | tf_op jit(solution)/shard_map/ppermute | solution.py:339
  37.6 1.0 %collective-permute-start.10 = (bf16[416,256]{1,0:T(8,128)(2,1)S(1)}, bf16[416,256]{1,0:T(8,128)(2,1)S(1)}, u32[]{:S(2)}, u32[]{:S(2)}) collective-permute-start(bf16[416,256]{1,0:T(8,128)(2,1)S(1)} %collective-permute-done.9.qc), channel_id=1, source_target_pairs={{0,1},{1,0},{2,3},{3,2},{4,5},{5,4},{6,7},{7,6},{8,9},{9,8},{10,11... | collective-permute-start | bytes 638984 | tf_op jit(solution)/shard_map/ppermute | solution.py:339
  38.6 1.5 %destination_step1_first.1.first_ref = f32[400,512]{1,0:T(8,128)S(1)} custom-call(bf16[512,400]{1,0:T(8,128)(2,1)S(1)} %get-tuple-element.57.turned_ref, bf16[416,256]{1,0:T(8,128)(2,1)S(1)} %collective-permute-done.7.qa, bf16[416,256]{1,0:T(8,128)(2,1)S(1)} %collective-permute-done.8.qb, bf16[416,256]{1,0:T(8,128)(2,1)S(1)} %collective-permute-done.9.qc), custom_call_target="tpu_custom_call" | custom-call | flops 1 | bytes 1 | tf_op jit(solution)/shard_map/destination_step1_first/pallas_call | solution.py:311
  40.1 0.7 %destination_step1.2.refs_0_ = bf16[400,256]{1,0:T(8,128)(2,1)S(1)} custom-call(bf16[512,400]{1,0:T(8,128)(2,1)S(1)} %get-tuple-element.57.turned_ref, f32[400,512]{1,0:T(8,128)S(1)} %destination_step1_first.1.first_ref, bf16[416,256]{1,0:T(8,128)(2,1)S(1)} %collective-permute-done.7.qa, bf16[416,256]{1,0:T(8,128)(2,1)S(1)} %collective-permute-done.10.qd, ...), custom_call_target="tpu_custom_call" | custom-call | flops 1 | bytes 1 | tf_op jit(solution)/shard_map/destination_step1/pallas_call | solution.py:311
  40.8 7.7 %collective-permute-start.11 = (bf16[400,256]{1,0:T(8,128)(2,1)S(1)}, bf16[400,256]{1,0:T(8,128)(2,1)S(1)}, u32[]{:S(2)}, u32[]{:S(2)}) collective-permute-start(bf16[400,256]{1,0:T(8,128)(2,1)S(1)} %destination_step1.2.refs_0_), channel_id=1, source_target_pairs={{0,254},{1,255},{2,252},{3,253},{4,0},{5,1},{6,2},{7,3},{8,4},{9,5... | collective-permute-start | bytes 614408 | tf_op jit(solution)/shard_map/ppermute | solution.py:339
  48.5 0.7 %destination_step1.3 = bf16[400,256]{1,0:T(8,128)(2,1)S(1)} custom-call(bf16[512,400]{1,0:T(8,128)(2,1)S(1)} %get-tuple-element.57.turned_ref, f32[400,512]{1,0:T(8,128)S(1)} %destination_step1_first.1.first_ref, bf16[416,256]{1,0:T(8,128)(2,1)S(1)} %collective-permute-done.7.qa, bf16[416,256]{1,0:T(8,128)(2,1)S(1)} %collective-permute-done.10.qd, ...), custom_call_target="tpu_custom_call" | custom-call | flops 1 | bytes 1 | tf_op jit(solution)/shard_map/destination_step1/pallas_call | solution.py:311
  49.1 0.0 copy-start.1
  49.2 0.6 collective-permute-start.13
  49.8 0.1 collective-permute-start.14
  49.9 0.5 collective-permute-start.15
  50.4 0.8 %collective-permute-done.14.other_b = bf16[128,512]{1,0:T(8,128)(2,1)S(1)} collective-permute-done((bf16[128,512]{1,0:T(8,128)(2,1)S(1)}, bf16[128,512]{1,0:T(8,128)(2,1)S(1)}, u32[]{:S(2)}, u32[]{:S(2)}) %collective-permute-start.14) | collective-permute-done | bytes 131104 | tf_op jit(solution)/shard_map/ppermute | solution.py:339
  51.2 0.2 collective-permute-done.15.other_c
  51.4 2.2 %source_step1.1 = f32[400,256]{1,0:T(8,128)} custom-call(bf16[400,512]{1,0:T(8,128)(2,1)S(1)} %collective-permute-done.12.own_ref, bf16[144,512]{1,0:T(8,128)(2,1)S(1)} %collective-permute-done.13.other_a, bf16[128,512]{1,0:T(8,128)(2,1)S(1)} %collective-permute-done.14.other_b, bf16[128,512]{1,0:T(8,128)(2,1)S(1)} %collective-permute-done.15.other_c, ...), custom_call_target="tpu_custom_call" | custom-call | flops 1 | bytes 1 | tf_op jit(solution)/shard_map/source_step1/pallas_call | solution.py:311
  53.7 0.6 collective-permute-start.17
  54.3 0.1 collective-permute-start.18
  54.4 0.8 %collective-permute-done.17.refs_0_ = bf16[400,128]{1,0:T(8,128)(2,1)S(1)} collective-permute-done((bf16[400,128]{1,0:T(8,128)(2,1)S(1)}, bf16[400,128]{1,0:T(8,128)(2,1)S(1)}, u32[]{:S(2)}, u32[]{:S(2)}) %collective-permute-start.17) | collective-permute-done | bytes 102432 | tf_op jit(solution)/shard_map/ppermute | solution.py:339
  55.2 0.4 collective-permute-done.18.refs_1_
  55.6 0.9 %destination_out.2.refs_1_ = f32[400,1024]{1,0:T(8,128)} custom-call(f32[400,1024]{1,0:T(8,128)S(1)} %bitcast.15, bf16[400,256]{1,0:T(8,128)(2,1)S(1)} %collective-permute-done.11.own_ref, bf16[400,128]{1,0:T(8,128)(2,1)S(1)} %collective-permute-done.17.refs_0_, bf16[400,128]{1,0:T(8,128)(2,1)S(1)} %collective-permute-done.18.refs_1_), custom_call_target="tpu_custom_call" | custom-call | flops 1 | bytes 1 | tf_op jit(solution)/shard_map/destination_out/pallas_call | solution.py:311
  56.5 0.8 %collective-permute-done.16.own_ref = bf16[400,256]{1,0:T(8,128)(2,1)S(1)} collective-permute-done((bf16[400,256]{1,0:T(8,128)(2,1)S(1)}, bf16[400,256]{1,0:T(8,128)(2,1)S(1)}, u32[]{:S(2)}, u32[]{:S(2)}) %collective-permute-start.16) | collective-permute-done | bytes 204832 | tf_op jit(solution)/shard_map/ppermute | solution.py:339
  57.4 0.8 %collective-permute-start.19 = (bf16[400,256]{1,0:T(8,128)(2,1)S(1)}, bf16[400,256]{1,0:T(8,128)(2,1)S(1)}, u32[]{:S(2)}, u32[]{:S(2)}) collective-permute-start(bf16[400,256]{1,0:T(8,128)(2,1)S(1)} %collective-permute-done.16.own_ref), channel_id=1, source_target_pairs={{0,1},{1,0},{2,3},{3,2},{4,5},{5,4},{6,7},{7,6},{8,9},{9,8},{10,11... | collective-permute-start | bytes 614408 | tf_op jit(solution)/shard_map/ppermute | solution.py:339
  58.2 1.1 %collective-permute-done.19.refs_0_ = bf16[400,256]{1,0:T(8,128)(2,1)S(1)} collective-permute-done((bf16[400,256]{1,0:T(8,128)(2,1)S(1)}, bf16[400,256]{1,0:T(8,128)(2,1)S(1)}, u32[]{:S(2)}, u32[]{:S(2)}) %collective-permute-start.19) | collective-permute-done | bytes 204832 | tf_op jit(solution)/shard_map/ppermute | solution.py:339
  59.2 1.0 %destination_out.3 = f32[400,1024]{1,0:T(8,128)} custom-call(f32[400,1024]{1,0:T(8,128)S(1)} %bitcast.16, bf16[400,256]{1,0:T(8,128)(2,1)S(1)} %collective-permute-done.16.own_ref, bf16[400,256]{1,0:T(8,128)(2,1)S(1)} %collective-permute-done.19.refs_0_, f32[400,1024]{1,0:T(8,128)} %destination_out.2.refs_1_), custom_call_target="tpu_custom_call", output_to_operand_aliasing={{}: (3, {})} | custom-call | flops 52428800 | bytes 5324800 | tf_op jit(solution)/shard_map/destination_out/pallas_call | solution.py:311
  (27 shorter events, 0.1 us)
Async XLA Ops:
  1.8 20.4 %collective-permute-start = (bf16[400,512]{1,0:T(8,128)(2,1)S(1)}, bf16[400,512]{1,0:T(8,128)(2,1)S(1)}, u32[]{:S(2)}, u32[]{:S(2)}) collective-permute-start(bf16[400,512]{1,0:T(8,128)(2,1)S(1)} %fusion), channel_id=1, source_target_pairs={{0,4},{1,5},{2,6},{3,7},{4,8},{5,9},{6,10},{7,11},{8,12},{9,13},{1... | collective-permute-start | bytes 1228808 | tf_op jit(solution)/shard_map/ppermute | solution.py:339
  5.1 2.7 %copy-start = (bf16[7424,400]{0,1:T(8,128)(2,1)S(1)}, bf16[7424,400]{0,1:T(8,128)(2,1)}, u32[]{:S(2)}) copy-start(bf16[7424,400]{0,1:T(8,128)(2,1)} %param.13) | copy-start | bytes 17817604
  7.8 1.0 %copy-start.2 = (f32[256,400]{0,1:T(8,128)S(1)}, f32[256,400]{0,1:T(8,128)}, u32[]{:S(2)}) copy-start(f32[256,400]{0,1:T(8,128)} %param.9) | copy-start | bytes 1228804
  8.8 4.3 %copy-start.8 = (f32[1024]{0:T(1024)S(1)}, f32[1024]{0:T(1024)}, u32[]{:S(2)}) copy-start(f32[1024]{0:T(1024)} %param.12) | copy-start | bytes 12292
  8.8 6.0 %copy-start.3 = (s32[1,2,2048]{2,1,0:T(2,128)S(1)}, s32[1,2,2048]{2,1,0:T(2,128)}, u32[]{:S(2)}) copy-start(s32[1,2,2048]{2,1,0:T(2,128)} %param.17) | copy-start | bytes 49156
  8.8 6.0 %copy-start.4 = (s32[1,2,256]{2,1,0:T(2,128)S(1)}, s32[1,2,256]{2,1,0:T(2,128)}, u32[]{:S(2)}) copy-start(s32[1,2,256]{2,1,0:T(2,128)} %param.16) | copy-start | bytes 6148
  8.8 6.0 %copy-start.5 = (s32[1,2,256]{2,1,0:T(2,128)S(1)}, s32[1,2,256]{2,1,0:T(2,128)}, u32[]{:S(2)}) copy-start(s32[1,2,256]{2,1,0:T(2,128)} %param.15) | copy-start | bytes 6148
  8.8 6.0 %copy-start.6 = (s32[1,2,256]{2,1,0:T(2,128)S(1)}, s32[1,2,256]{2,1,0:T(2,128)}, u32[]{:S(2)}) copy-start(s32[1,2,256]{2,1,0:T(2,128)} %param.14) | copy-start | bytes 6148
  8.8 6.0 %copy-start.7 = (f32[256]{0:T(256)S(1)}, f32[256]{0:T(256)}, u32[]{:S(2)}) copy-start(f32[256]{0:T(256)} %param.10) | copy-start | bytes 3076
  10.8 11.5 %collective-permute-start.1 = (bf16[416,256]{1,0:T(8,128)(2,1)S(1)}, bf16[416,256]{1,0:T(8,128)(2,1)S(1)}, u32[]{:S(2)}, u32[]{:S(2)}) collective-permute-start(bf16[416,256]{1,0:T(8,128)(2,1)S(1)} %get-tuple-element.38.q_ref.qa), channel_id=1, source_target_pairs={{0,1},{1,0},{2,3},{3,2},{4,5},{5,4},{6,7},{7,6},{8,9},{9,8},{10,11... | collective-permute-start | bytes 638984 | tf_op jit(solution)/shard_map/ppermute | solution.py:339
  11.8 14.6 %collective-permute-start.3 = (bf16[416,256]{1,0:T(8,128)(2,1)S(1)}, bf16[416,256]{1,0:T(8,128)(2,1)S(1)}, u32[]{:S(2)}, u32[]{:S(2)}) collective-permute-start(bf16[416,256]{1,0:T(8,128)(2,1)S(1)} %get-tuple-element.38.q_ref.qa), channel_id=1, source_target_pairs={{0,2},{1,3},{2,0},{3,1},{4,6},{5,7},{6,4},{7,5},{8,10},{9,11},{10,... | collective-permute-start | bytes 638984 | tf_op jit(solution)/shard_map/ppermute | solution.py:339
  13.1 9.1 %collective-permute-start.2 = (f32[1,1024]{1,0:T(1,128)S(1)}, f32[1,1024]{1,0:T(1,128)S(1)}, u32[]{:S(2)}, u32[]{:S(2)}) collective-permute-start(f32[1,1024]{1,0:T(1,128)S(1)} %bitcast.29), channel_id=1, source_target_pairs={{0,4},{1,5},{2,6},{3,7},{4,8},{5,9},{6,10},{7,11},{8,12},{9,13},{1... | collective-permute-start | bytes 12296 | tf_op jit(solution)/shard_map/ppermute | solution.py:339
  22.3 2.4 %collective-permute-start.4 = (bf16[400,256]{1,0:T(8,128)(2,1)S(1)}, bf16[400,256]{1,0:T(8,128)(2,1)S(1)}, u32[]{:S(2)}, u32[]{:S(2)}) collective-permute-start(bf16[400,256]{1,0:T(8,128)(2,1)S(1)} %get-tuple-element.73), channel_id=1, source_target_pairs={{0,1},{1,0},{2,3},{3,2},{4,5},{5,4},{6,7},{7,6},{8,9},{9,8},{10,11... | collective-permute-start | bytes 614408 | tf_op jit(solution)/shard_map/ppermute | solution.py:339
  23.6 1.5 %collective-permute-start.5 = (bf16[400,256]{1,0:T(8,128)(2,1)S(1)}, bf16[400,256]{1,0:T(8,128)(2,1)S(1)}, u32[]{:S(2)}, u32[]{:S(2)}) collective-permute-start(bf16[400,256]{1,0:T(8,128)(2,1)S(1)} %get-tuple-element.72), channel_id=1, source_target_pairs={{0,1},{1,0},{2,3},{3,2},{4,5},{5,4},{6,7},{7,6},{8,9},{9,8},{10,11... | collective-permute-start | bytes 614408 | tf_op jit(solution)/shard_map/ppermute | solution.py:339
  26.4 3.2 %collective-permute-start.6 = (bf16[416,256]{1,0:T(8,128)(2,1)S(1)}, bf16[416,256]{1,0:T(8,128)(2,1)S(1)}, u32[]{:S(2)}, u32[]{:S(2)}) collective-permute-start(bf16[416,256]{1,0:T(8,128)(2,1)S(1)} %collective-permute-done.3.qb), channel_id=1, source_target_pairs={{0,1},{1,0},{2,3},{3,2},{4,5},{5,4},{6,7},{7,6},{8,9},{9,8},{10,11... | collective-permute-start | bytes 638984 | tf_op jit(solution)/shard_map/ppermute | solution.py:339
  26.8 6.6 %collective-permute-start.7 = (bf16[416,256]{1,0:T(8,128)(2,1)S(1)}, bf16[416,256]{1,0:T(8,128)(2,1)S(1)}, u32[]{:S(2)}, u32[]{:S(2)}) collective-permute-start(bf16[416,256]{1,0:T(8,128)(2,1)S(1)} %get-tuple-element.62.q_ref), channel_id=1, source_target_pairs={{0,252},{1,253},{2,254},{3,255},{4,0},{5,1},{6,2},{7,3},{8,4},{9,5... | collective-permute-start | bytes 638984 | tf_op jit(solution)/shard_map/ppermute | solution.py:339
  28.6 9.0 %collective-permute-start.9 = (bf16[416,256]{1,0:T(8,128)(2,1)S(1)}, bf16[416,256]{1,0:T(8,128)(2,1)S(1)}, u32[]{:S(2)}, u32[]{:S(2)}) collective-permute-start(bf16[416,256]{1,0:T(8,128)(2,1)S(1)} %get-tuple-element.62.q_ref), channel_id=1, source_target_pairs={{0,254},{1,255},{2,252},{3,253},{4,2},{5,3},{6,0},{7,1},{8,6},{9,7... | collective-permute-start | bytes 638984 | tf_op jit(solution)/shard_map/ppermute | solution.py:339
  32.3 16.9 %collective-permute-start.12 = (bf16[400,512]{1,0:T(8,128)(2,1)S(1)}, bf16[400,512]{1,0:T(8,128)(2,1)S(1)}, u32[]{:S(2)}, u32[]{:S(2)}) collective-permute-start(bf16[400,512]{1,0:T(8,128)(2,1)S(1)} %get-tuple-element.60), channel_id=1, source_target_pairs={{0,4},{1,5},{2,6},{3,7},{4,8},{5,9},{6,10},{7,11},{8,12},{9,13},{1... | collective-permute-start | bytes 1228808 | tf_op jit(solution)/shard_map/ppermute | solution.py:339
  33.4 5.2 %collective-permute-start.8 = (bf16[416,256]{1,0:T(8,128)(2,1)S(1)}, bf16[416,256]{1,0:T(8,128)(2,1)S(1)}, u32[]{:S(2)}, u32[]{:S(2)}) collective-permute-start(bf16[416,256]{1,0:T(8,128)(2,1)S(1)} %collective-permute-done.7.qa), channel_id=1, source_target_pairs={{0,1},{1,0},{2,3},{3,2},{4,5},{5,4},{6,7},{7,6},{8,9},{9,8},{10,11... | collective-permute-start | bytes 638984 | tf_op jit(solution)/shard_map/ppermute | solution.py:339
  37.6 2.5 %collective-permute-start.10 = (bf16[416,256]{1,0:T(8,128)(2,1)S(1)}, bf16[416,256]{1,0:T(8,128)(2,1)S(1)}, u32[]{:S(2)}, u32[]{:S(2)}) collective-permute-start(bf16[416,256]{1,0:T(8,128)(2,1)S(1)} %collective-permute-done.9.qc), channel_id=1, source_target_pairs={{0,1},{1,0},{2,3},{3,2},{4,5},{5,4},{6,7},{7,6},{8,9},{9,8},{10,11... | collective-permute-start | bytes 638984 | tf_op jit(solution)/shard_map/ppermute | solution.py:339
  40.8 12.9 %collective-permute-start.11 = (bf16[400,256]{1,0:T(8,128)(2,1)S(1)}, bf16[400,256]{1,0:T(8,128)(2,1)S(1)}, u32[]{:S(2)}, u32[]{:S(2)}) collective-permute-start(bf16[400,256]{1,0:T(8,128)(2,1)S(1)} %destination_step1.2.refs_0_), channel_id=1, source_target_pairs={{0,254},{1,255},{2,252},{3,253},{4,0},{5,1},{6,2},{7,3},{8,4},{9,5... | collective-permute-start | bytes 614408 | tf_op jit(solution)/shard_map/ppermute | solution.py:339
  49.1 6.4 %copy-start.1 = (f32[1024,400]{0,1:T(8,128)S(1)}, f32[1024,400]{0,1:T(8,128)}, u32[]{:S(2)}) copy-start(f32[1024,400]{0,1:T(8,128)} %param.11) | copy-start | bytes 4915204
  49.2 2.2 %collective-permute-start.13 = (bf16[144,512]{1,0:T(8,128)(2,1)S(1)}, bf16[144,512]{1,0:T(8,128)(2,1)S(1)}, u32[]{:S(2)}, u32[]{:S(2)}) collective-permute-start(bf16[144,512]{1,0:T(8,128)(2,1)S(1)} %slice.23), channel_id=1, source_target_pairs={{0,1},{1,0},{2,3},{3,2},{4,5},{5,4},{6,7},{7,6},{8,9},{9,8},{10,11... | collective-permute-start | bytes 442376 | tf_op jit(solution)/shard_map/ppermute | solution.py:339
  49.8 1.4 %collective-permute-start.14 = (bf16[128,512]{1,0:T(8,128)(2,1)S(1)}, bf16[128,512]{1,0:T(8,128)(2,1)S(1)}, u32[]{:S(2)}, u32[]{:S(2)}) collective-permute-start(bf16[128,512]{1,0:T(8,128)(2,1)S(1)} %get-tuple-element.71), channel_id=1, source_target_pairs={{0,1},{1,0},{2,3},{3,2},{4,5},{5,4},{6,7},{7,6},{8,9},{9,8},{10,11... | collective-permute-start | bytes 393224 | tf_op jit(solution)/shard_map/ppermute | solution.py:339
  49.9 1.5 %collective-permute-start.15 = (bf16[128,512]{1,0:T(8,128)(2,1)S(1)}, bf16[128,512]{1,0:T(8,128)(2,1)S(1)}, u32[]{:S(2)}, u32[]{:S(2)}) collective-permute-start(bf16[128,512]{1,0:T(8,128)(2,1)S(1)} %get-tuple-element.70), channel_id=1, source_target_pairs={{0,1},{1,0},{2,3},{3,2},{4,5},{5,4},{6,7},{7,6},{8,9},{9,8},{10,11... | collective-permute-start | bytes 393224 | tf_op jit(solution)/shard_map/ppermute | solution.py:339
  50.4 7.0 %collective-permute-start.16 = (bf16[400,256]{1,0:T(8,128)(2,1)S(1)}, bf16[400,256]{1,0:T(8,128)(2,1)S(1)}, u32[]{:S(2)}, u32[]{:S(2)}) collective-permute-start(bf16[400,256]{1,0:T(8,128)(2,1)S(1)} %destination_step1.3), channel_id=1, source_target_pairs={{0,254},{1,255},{2,252},{3,253},{4,0},{5,1},{6,2},{7,3},{8,4},{9,5... | collective-permute-start | bytes 614408 | tf_op jit(solution)/shard_map/ppermute | solution.py:339
  53.7 1.5 %collective-permute-start.17 = (bf16[400,128]{1,0:T(8,128)(2,1)S(1)}, bf16[400,128]{1,0:T(8,128)(2,1)S(1)}, u32[]{:S(2)}, u32[]{:S(2)}) collective-permute-start(bf16[400,128]{1,0:T(8,128)(2,1)S(1)} %get-tuple-element.75), channel_id=1, source_target_pairs={{0,1},{1,0},{2,3},{3,2},{4,5},{5,4},{6,7},{7,6},{8,9},{9,8},{10,11... | collective-permute-start | bytes 307208 | tf_op jit(solution)/shard_map/ppermute | solution.py:339
  54.3 1.3 %collective-permute-start.18 = (bf16[400,128]{1,0:T(8,128)(2,1)S(1)}, bf16[400,128]{1,0:T(8,128)(2,1)S(1)}, u32[]{:S(2)}, u32[]{:S(2)}) collective-permute-start(bf16[400,128]{1,0:T(8,128)(2,1)S(1)} %get-tuple-element.74), channel_id=1, source_target_pairs={{0,1},{1,0},{2,3},{3,2},{4,5},{5,4},{6,7},{7,6},{8,9},{9,8},{10,11... | collective-permute-start | bytes 307208 | tf_op jit(solution)/shard_map/ppermute | solution.py:339
  57.4 1.9 %collective-permute-start.19 = (bf16[400,256]{1,0:T(8,128)(2,1)S(1)}, bf16[400,256]{1,0:T(8,128)(2,1)S(1)}, u32[]{:S(2)}, u32[]{:S(2)}) collective-permute-start(bf16[400,256]{1,0:T(8,128)(2,1)S(1)} %collective-permute-done.16.own_ref), channel_id=1, source_target_pairs={{0,1},{1,0},{2,3},{3,2},{4,5},{5,4},{6,7},{7,6},{8,9},{9,8},{10,11... | collective-permute-start | bytes 614408 | tf_op jit(solution)/shard_map/ppermute | solution.py:339

commit v6 on v5

--- a/solution.py
+++ b/solution.py
@@ -287,14 +287,15 @@
     delta_out[...] = (delta_ref[:, part] + gradient * size).astype(BF)
 
 
-def final_kernel(start, parts, emb_ref, own_ref, *refs):
+def final_kernel(start, sides, emb_ref, *refs):
     out_ref, held, sems = refs[-3:]
-    size = own_ref.shape[1]
-    other = jnp.concatenate([ref[...] for ref in refs[:parts]], axis=1)
     half = emb_ref.shape[1] // 2
-    here = core()
     copies = []
-    for i, (place, delta) in enumerate(((here, own_ref[...]), (1 - here, other))):
+    for i, (side, count) in enumerate(sides):
+        delta = jnp.concatenate([ref[...] for ref in refs[:count]], axis=1)
+        refs = refs[count:]
+        size = delta.shape[1]
+        place = core() if side == 0 else 1 - core()
         columns = pl.ds(pl.multiple_of(place * half + start, size), size)
         held[i] = emb_ref[:, columns] - delta.astype(F32)
         copies.append(pltpu.make_async_copy(held.at[i], out_ref.at[:, columns], sems.at[i]))
@@ -460,28 +461,28 @@
         limit=24,
     )
     homes[0], src_out = lax.optimization_barrier((homes[0], src_out))
-    def exchanged(home, parts):
-        size = piece // parts
-        return [moved(home[:, k * size : (k + 1) * size], to=1) for k in range(parts)]
-
-    dst_out = ()
-    for i, home in enumerate(homes):
-        if i:
-            home, *dst_out = lax.optimization_barrier((home, *dst_out))
-        dst_out = (
-            call(
-                functools.partial(final_kernel, i * piece, 2 - i),
-                [((depth, rows), F32)],
-                [dst, home, *exchanged(home, 2 - i), *dst_out],
-                "destination_out",
-                flops=i * matmul // 4,
-                scratch=[pltpu.VMEM((2, depth, piece), F32), pltpu.SemaphoreType.DMA((2,))],
-                hbm=(3,) if i else (),
-                limit=16,
-                out=3 * i,
-            ),
+    def final(start, sides, changes, done):
+        return call(
+            functools.partial(final_kernel, start, sides),
+            [((depth, rows), F32)],
+            [dst, *changes, *done],
+            "destination_out",
+            scratch=[
+                pltpu.VMEM((len(sides), depth, piece), F32),
+                pltpu.SemaphoreType.DMA((len(sides),)),
+            ],
+            hbm=(1 + len(changes),),
+            limit=16,
+            out=1 + len(changes) if done else 0,
         )
-    dst_out = dst_out[0]
+
+    cuts = range(0, piece, LANES)
+    other = [moved(homes[0][:, k : k + LANES], to=1) for k in cuts]
+    dst_out = final(0, ((0, 1), (1, len(other))), [homes[0], *other], ())
+    home, dst_out = lax.optimization_barrier((homes[1], dst_out))
+    other = moved(home, to=1)
+    dst_out = final(piece, ((0, 1),), [home], (dst_out,))
+    dst_out = final(piece, ((1, 1),), [other], (dst_out,))
     return src_out.T, dst_out.T
 
 

time: 60.6 us -> 60.4 us (level)
  waiting for transfers between devices: 13.2 us -> 12.4 us
    ppermute x20, waiting for transfers between devices: 13.2 us -> 12.4 us  [moved(): return lax.ppermute(value, ('wide', 'narrow'), pairs)]
    pallas_call x11 -> x12, Pallas kernels: 15.8 us -> 16.4 us  [call(): pl.pallas_call(kernel, out_shape=shapes, in_specs=[anywhere if i in hbm e...]
  transfers between devices with their start and end apart: 20 -> 20, of which waited for: 11 -> 11; matrix products, arithmetic and copies ran while one was open for 1% -> 1% of each run, Pallas kernels for 25% -> 26%
where the time goes in v6:
time: 60.4 us; the launch traced here: 60.2 us
  starting transfers between devices  24.7 us (41%)
  Pallas kernels  16.4 us (27%)
  waiting for transfers between devices  12.4 us (21%)
  local copies, waits for them, and re-layouts  4.99 us (8%)
  between operations  0.98 us (2%)
  other arithmetic  0.72 us (1%)
    ppermute x20, starting transfers between devices, moved(): return lax.ppermute(value, ('wide', 'narrow'), pairs)  24.7 us
    pallas_call x12, Pallas kernels, call(): pl.pallas_call(kernel, out_shape=shapes, in_specs=[anywhere if i in hbm e...  16.4 us
    ppermute x20, waiting for transfers between devices, moved(): return lax.ppermute(value, ('wide', 'narrow'), pairs)  12.4 us
    unnamed x18, local copies, waits for them, and re-layouts  3.72 us
  transfers between devices with their start and end apart: 20, of which 11 were waited for; matrix products, arithmetic and copies ran while one was open for 1% of the time, Pallas kernels for 26%

profile of v6, /device:TPU:1, one launch (start us, length us, event | category | flops | bytes accessed | tf_op | source)
XLA Modules:
  0.0 60.2 jit_solution(9335660621836617579)
XLA Ops:
  0.6 1.2 %fusion = bf16[400,512]{1,0:T(8,128)(2,1)S(1)} fusion(f32[1024,400]{0,1:T(8,128)} %param.11, s32[]{:T(128)S(6)} %select_n.3), kind=kLoop, calls=%fused_computation.1 | loop fusion | bytes 819204 | tf_op jit(solution)/shard_map/convert_element_type | solution.py:353
  1.8 2.5 %collective-permute-start = (bf16[400,512]{1,0:T(8,128)(2,1)S(1)}, bf16[400,512]{1,0:T(8,128)(2,1)S(1)}, u32[]{:S(2)}, u32[]{:S(2)}) collective-permute-start(bf16[400,512]{1,0:T(8,128)(2,1)S(1)} %fusion), channel_id=1, source_target_pairs={{0,4},{1,5},{2,6},{3,7},{4,8},{5,9},{6,10},{7,11},{8,12},{9,13},{1... | collective-permute-start | bytes 1228808 | tf_op jit(solution)/shard_map/ppermute | solution.py:340
  4.4 0.7 %pad_add_fusion.index = s32[6,256]{1,0:T(8,128)S(1)} fusion(s32[2,256]{1,0:T(2,128)} %bitcast.21, s32[2,256]{1,0:T(2,128)} %bitcast.23, s32[2,256]{1,0:T(2,128)} %bitcast.25), kind=kLoop, calls=%fused_computation.2 | loop fusion | flops 3072 | bytes 12288 | tf_op jit(solution)/shard_map/concatenate | solution.py:355
  5.1 2.7 %copy-done = bf16[7424,400]{0,1:T(8,128)(2,1)S(1)} copy-done((bf16[7424,400]{0,1:T(8,128)(2,1)S(1)}, bf16[7424,400]{0,1:T(8,128)(2,1)}, u32[]{:S(2)}) %copy-start) | copy-done | bytes 5939224
  7.8 1.0 %copy-done.2 = f32[256,400]{0,1:T(8,128)S(1)} copy-done((f32[256,400]{0,1:T(8,128)S(1)}, f32[256,400]{0,1:T(8,128)}, u32[]{:S(2)}) %copy-start.2) | copy-done | bytes 409624
  8.8 0.0 copy-start.6
  8.8 1.9 %query_step0.1 = (bf16[416,256]{1,0:T(8,128)(2,1)S(1)}, bf16[400,256]{1,0:T(8,128)(2,1)S(1)}) custom-call(bf16[400,7424]{1,0:T(8,128)(2,1)S(1)} %bitcast.13, f32[400,256]{1,0:T(8,128)S(1)} %bitcast.18, s32[6,256]{1,0:T(8,128)S(1)} %pad_add_fusion.index), custom_call_target="tpu_custom_call" | custom-call | flops 1520435200 | bytes 6772736 | tf_op jit(solution)/shard_map/query_step0/pallas_call | solution.py:312
  10.8 1.0 %collective-permute-start.1 = (bf16[416,256]{1,0:T(8,128)(2,1)S(1)}, bf16[416,256]{1,0:T(8,128)(2,1)S(1)}, u32[]{:S(2)}, u32[]{:S(2)}) collective-permute-start(bf16[416,256]{1,0:T(8,128)(2,1)S(1)} %get-tuple-element.38.q_ref.qa), channel_id=1, source_target_pairs={{0,1},{1,0},{2,3},{3,2},{4,5},{5,4},{6,7},{7,6},{8,9},{9,8},{10,11... | collective-permute-start | bytes 638984 | tf_op jit(solution)/shard_map/ppermute | solution.py:340
  11.8 1.3 %collective-permute-start.3 = (bf16[416,256]{1,0:T(8,128)(2,1)S(1)}, bf16[416,256]{1,0:T(8,128)(2,1)S(1)}, u32[]{:S(2)}, u32[]{:S(2)}) collective-permute-start(bf16[416,256]{1,0:T(8,128)(2,1)S(1)} %get-tuple-element.38.q_ref.qa), channel_id=1, source_target_pairs={{0,2},{1,3},{2,0},{3,1},{4,6},{5,7},{6,4},{7,5},{8,10},{9,11},{10,... | collective-permute-start | bytes 638984 | tf_op jit(solution)/shard_map/ppermute | solution.py:340
  13.1 1.6 %collective-permute-start.2 = (f32[1,1024]{1,0:T(1,128)S(1)}, f32[1,1024]{1,0:T(1,128)S(1)}, u32[]{:S(2)}, u32[]{:S(2)}) collective-permute-start(f32[1,1024]{1,0:T(1,128)S(1)} %bitcast.30), channel_id=1, source_target_pairs={{0,4},{1,5},{2,6},{3,7},{4,8},{5,9},{6,10},{7,11},{8,12},{9,13},{1... | collective-permute-start | bytes 12296 | tf_op jit(solution)/shard_map/ppermute | solution.py:340
  14.8 2.3 %prepare.1 = (bf16[256,400]{1,0:T(8,128)(2,1)S(1)}, s32[256,128]{1,0:T(8,128)S(1)}, bf16[400,256]{1,0:T(8,128)(2,1)S(1)}, f32[1,1024]{1,0:T(1,128)S(1)}, f32[128...) custom-call(bf16[400,7424]{1,0:T(8,128)(2,1)S(1)} %bitcast.14, ...), custom_call_target="tpu_custom_call" | custom-call | flops 1520435200 | bytes 7561216 | tf_op jit(solution)/shard_map/prepare/pallas_call | solution.py:312
  17.1 5.1 %collective-permute-done.2.old_ref = f32[1,1024]{1,0:T(1,128)S(1)} collective-permute-done((f32[1,1024]{1,0:T(1,128)S(1)}, f32[1,1024]{1,0:T(1,128)S(1)}, u32[]{:S(2)}, u32[]{:S(2)}) %collective-permute-start.2) | collective-permute-done | bytes 4128 | tf_op jit(solution)/shard_map/ppermute | solution.py:340
  22.3 1.3 %collective-permute-start.4 = (bf16[400,256]{1,0:T(8,128)(2,1)S(1)}, bf16[400,256]{1,0:T(8,128)(2,1)S(1)}, u32[]{:S(2)}, u32[]{:S(2)}) collective-permute-start(bf16[400,256]{1,0:T(8,128)(2,1)S(1)} %get-tuple-element.73), channel_id=1, source_target_pairs={{0,1},{1,0},{2,3},{3,2},{4,5},{5,4},{6,7},{7,6},{8,9},{9,8},{10,11... | collective-permute-start | bytes 614408 | tf_op jit(solution)/shard_map/ppermute | solution.py:340
  23.6 0.1 collective-permute-start.5
  23.7 0.6 %source_step0_first.1.first_ref = f32[400,256]{1,0:T(8,128)S(1)} custom-call(bf16[400,512]{1,0:T(8,128)(2,1)S(1)} %collective-permute-done.own_ref, bf16[256,400]{1,0:T(8,128)(2,1)S(1)} %get-tuple-element.43.qt_ref, s32[256,128]{1,0:T(8,128)S(1)} %get-tuple-element.44.at_ref, f32[1,1024]{1,0:T(1,128)S(1)} %get-tuple-element.45.count_ref), custom_call_target="tpu_custom_call" | custom-call | flops 1 | bytes 1 | tf_op jit(solution)/shard_map/source_step0_first/pallas_call | solution.py:312
  24.4 0.3 collective-permute-done.4.other_a
  24.7 0.4 collective-permute-done.5.other_b
  25.1 1.3 %source_step0.1 = (bf16[416,256]{1,0:T(8,128)(2,1)S(1)}, f32[400,256]{1,0:T(8,128)S(1)}, f32[1,256]{1,0:T(1,128)S(1)}) custom-call(f32[400,256]{1,0:T(8,128)S(1)} %source_step0_first.1.first_ref, bf16[400,256]{1,0:T(8,128)(2,1)S(1)} %collective-permute-done.4.other_a, bf16[400,256]{1,0:T(8,128)(2,1)S(1)} %collective-permute-done.5.other_b, ...), custom_call_target="tpu_custom_call" | custom-call | flops 1 | bytes 1 | tf_op jit(solution)/shard_map/source_step0/pallas_call | solution.py:312
  26.4 0.4 collective-permute-start.6
  26.8 1.8 %collective-permute-start.7 = (bf16[416,256]{1,0:T(8,128)(2,1)S(1)}, bf16[416,256]{1,0:T(8,128)(2,1)S(1)}, u32[]{:S(2)}, u32[]{:S(2)}) collective-permute-start(bf16[416,256]{1,0:T(8,128)(2,1)S(1)} %get-tuple-element.62.q_ref), channel_id=1, source_target_pairs={{0,252},{1,253},{2,254},{3,255},{4,0},{5,1},{6,2},{7,3},{8,4},{9,5... | collective-permute-start | bytes 638984 | tf_op jit(solution)/shard_map/ppermute | solution.py:340
  28.6 1.0 %collective-permute-start.9 = (bf16[416,256]{1,0:T(8,128)(2,1)S(1)}, bf16[416,256]{1,0:T(8,128)(2,1)S(1)}, u32[]{:S(2)}, u32[]{:S(2)}) collective-permute-start(bf16[416,256]{1,0:T(8,128)(2,1)S(1)} %get-tuple-element.62.q_ref), channel_id=1, source_target_pairs={{0,254},{1,255},{2,252},{3,253},{4,2},{5,3},{6,0},{7,1},{8,6},{9,7... | collective-permute-start | bytes 638984 | tf_op jit(solution)/shard_map/ppermute | solution.py:340
  29.6 2.7 %destination_step0.1 = (bf16[400,512]{1,0:T(8,128)(2,1)S(1)}, bf16[512,400]{1,0:T(8,128)(2,1)S(1)}, f32[400,512]{1,0:T(8,128)S(1)}, f32[1,512]{1,0:T(1,128)S(1)}) custom-call(bf16[400,512]{1,0:T(8,128)(2,1)S(1)} %collective-permute-done.own_ref, f32[1,1024]{1,0:T(1,128)S(1)} %collective-permute-done.2.old_ref, ...), custom_call_target="tpu_custom_call" | custom-call | flops 1 | bytes 1 | tf_op jit(solution)/shard_map/destination_step0/pallas_call | solution.py:312
  32.3 0.5 collective-permute-start.12
  32.7 0.7 %collective-permute-done.7.qa = bf16[416,256]{1,0:T(8,128)(2,1)S(1)} collective-permute-done((bf16[416,256]{1,0:T(8,128)(2,1)S(1)}, bf16[416,256]{1,0:T(8,128)(2,1)S(1)}, u32[]{:S(2)}, u32[]{:S(2)}) %collective-permute-start.7) | collective-permute-done | bytes 213024 | tf_op jit(solution)/shard_map/ppermute | solution.py:340
  33.4 1.7 %collective-permute-start.8 = (bf16[416,256]{1,0:T(8,128)(2,1)S(1)}, bf16[416,256]{1,0:T(8,128)(2,1)S(1)}, u32[]{:S(2)}, u32[]{:S(2)}) collective-permute-start(bf16[416,256]{1,0:T(8,128)(2,1)S(1)} %collective-permute-done.7.qa), channel_id=1, source_target_pairs={{0,1},{1,0},{2,3},{3,2},{4,5},{5,4},{6,7},{7,6},{8,9},{9,8},{10,11... | collective-permute-start | bytes 638984 | tf_op jit(solution)/shard_map/ppermute | solution.py:340
  35.1 2.5 %collective-permute-done.9.qc = bf16[416,256]{1,0:T(8,128)(2,1)S(1)} collective-permute-done((bf16[416,256]{1,0:T(8,128)(2,1)S(1)}, bf16[416,256]{1,0:T(8,128)(2,1)S(1)}, u32[]{:S(2)}, u32[]{:S(2)}) %collective-permute-start.9) | collective-permute-done | bytes 213024 | tf_op jit(solution)/shard_map/ppermute | solution.py:340
  37.6 1.0 %collective-permute-start.10 = (bf16[416,256]{1,0:T(8,128)(2,1)S(1)}, bf16[416,256]{1,0:T(8,128)(2,1)S(1)}, u32[]{:S(2)}, u32[]{:S(2)}) collective-permute-start(bf16[416,256]{1,0:T(8,128)(2,1)S(1)} %collective-permute-done.9.qc), channel_id=1, source_target_pairs={{0,1},{1,0},{2,3},{3,2},{4,5},{5,4},{6,7},{7,6},{8,9},{9,8},{10,11... | collective-permute-start | bytes 638984 | tf_op jit(solution)/shard_map/ppermute | solution.py:340
  38.6 1.5 %destination_step1_first.1.first_ref = f32[400,512]{1,0:T(8,128)S(1)} custom-call(bf16[512,400]{1,0:T(8,128)(2,1)S(1)} %get-tuple-element.57.turned_ref, bf16[416,256]{1,0:T(8,128)(2,1)S(1)} %collective-permute-done.7.qa, bf16[416,256]{1,0:T(8,128)(2,1)S(1)} %collective-permute-done.8.qb, bf16[416,256]{1,0:T(8,128)(2,1)S(1)} %collective-permute-done.9.qc), custom_call_target="tpu_custom_call" | custom-call | flops 1 | bytes 1 | tf_op jit(solution)/shard_map/destination_step1_first/pallas_call | solution.py:312
  40.1 0.7 %destination_step1.2.refs_0_ = bf16[400,256]{1,0:T(8,128)(2,1)S(1)} custom-call(bf16[512,400]{1,0:T(8,128)(2,1)S(1)} %get-tuple-element.57.turned_ref, f32[400,512]{1,0:T(8,128)S(1)} %destination_step1_first.1.first_ref, bf16[416,256]{1,0:T(8,128)(2,1)S(1)} %collective-permute-done.7.qa, bf16[416,256]{1,0:T(8,128)(2,1)S(1)} %collective-permute-done.10.qd, ...), custom_call_target="tpu_custom_call" | custom-call | flops 1 | bytes 1 | tf_op jit(solution)/shard_map/destination_step1/pallas_call | solution.py:312
  40.8 7.7 %collective-permute-start.11 = (bf16[400,256]{1,0:T(8,128)(2,1)S(1)}, bf16[400,256]{1,0:T(8,128)(2,1)S(1)}, u32[]{:S(2)}, u32[]{:S(2)}) collective-permute-start(bf16[400,256]{1,0:T(8,128)(2,1)S(1)} %destination_step1.2.refs_0_), channel_id=1, source_target_pairs={{0,254},{1,255},{2,252},{3,253},{4,0},{5,1},{6,2},{7,3},{8,4},{9,5... | collective-permute-start | bytes 614408 | tf_op jit(solution)/shard_map/ppermute | solution.py:340
  48.5 0.7 %destination_step1.3 = bf16[400,256]{1,0:T(8,128)(2,1)S(1)} custom-call(bf16[512,400]{1,0:T(8,128)(2,1)S(1)} %get-tuple-element.57.turned_ref, f32[400,512]{1,0:T(8,128)S(1)} %destination_step1_first.1.first_ref, bf16[416,256]{1,0:T(8,128)(2,1)S(1)} %collective-permute-done.7.qa, bf16[416,256]{1,0:T(8,128)(2,1)S(1)} %collective-permute-done.10.qd, ...), custom_call_target="tpu_custom_call" | custom-call | flops 1 | bytes 1 | tf_op jit(solution)/shard_map/destination_step1/pallas_call | solution.py:312
  49.1 0.0 copy-start.1
  49.2 0.6 collective-permute-start.13
  49.8 0.1 collective-permute-start.14
  49.9 0.5 collective-permute-start.15
  50.4 0.8 %collective-permute-done.14.other_b = bf16[128,512]{1,0:T(8,128)(2,1)S(1)} collective-permute-done((bf16[128,512]{1,0:T(8,128)(2,1)S(1)}, bf16[128,512]{1,0:T(8,128)(2,1)S(1)}, u32[]{:S(2)}, u32[]{:S(2)}) %collective-permute-start.14) | collective-permute-done | bytes 131104 | tf_op jit(solution)/shard_map/ppermute | solution.py:340
  51.2 0.2 collective-permute-done.15.other_c
  51.4 2.2 %source_step1.1 = f32[400,256]{1,0:T(8,128)} custom-call(bf16[400,512]{1,0:T(8,128)(2,1)S(1)} %collective-permute-done.12.own_ref, bf16[144,512]{1,0:T(8,128)(2,1)S(1)} %collective-permute-done.13.other_a, bf16[128,512]{1,0:T(8,128)(2,1)S(1)} %collective-permute-done.14.other_b, bf16[128,512]{1,0:T(8,128)(2,1)S(1)} %collective-permute-done.15.other_c, ...), custom_call_target="tpu_custom_call" | custom-call | flops 1 | bytes 1 | tf_op jit(solution)/shard_map/source_step1/pallas_call | solution.py:312
  53.7 0.6 collective-permute-start.17
  54.3 0.1 collective-permute-start.18
  54.4 0.8 %collective-permute-done.17.refs_1_ = bf16[400,128]{1,0:T(8,128)(2,1)S(1)} collective-permute-done((bf16[400,128]{1,0:T(8,128)(2,1)S(1)}, bf16[400,128]{1,0:T(8,128)(2,1)S(1)}, u32[]{:S(2)}, u32[]{:S(2)}) %collective-permute-start.17) | collective-permute-done | bytes 102432 | tf_op jit(solution)/shard_map/ppermute | solution.py:340
  55.2 0.4 collective-permute-done.18.refs_2_
  55.6 0.9 %destination_out.3.refs_1_ = f32[400,1024]{1,0:T(8,128)} custom-call(f32[400,1024]{1,0:T(8,128)S(1)} %bitcast.15, bf16[400,256]{1,0:T(8,128)(2,1)S(1)} %collective-permute-done.11.refs_0_, bf16[400,128]{1,0:T(8,128)(2,1)S(1)} %collective-permute-done.17.refs_1_, bf16[400,128]{1,0:T(8,128)(2,1)S(1)} %collective-permute-done.18.refs_2_), custom_call_target="tpu_custom_call" | custom-call | flops 1 | bytes 1 | tf_op jit(solution)/shard_map/destination_out/pallas_call | solution.py:312
  56.5 0.8 %collective-permute-done.16.refs_0_ = bf16[400,256]{1,0:T(8,128)(2,1)S(1)} collective-permute-done((bf16[400,256]{1,0:T(8,128)(2,1)S(1)}, bf16[400,256]{1,0:T(8,128)(2,1)S(1)}, u32[]{:S(2)}, u32[]{:S(2)}) %collective-permute-start.16) | collective-permute-done | bytes 204832 | tf_op jit(solution)/shard_map/ppermute | solution.py:340
  57.4 0.8 %collective-permute-start.19 = (bf16[400,256]{1,0:T(8,128)(2,1)S(1)}, bf16[400,256]{1,0:T(8,128)(2,1)S(1)}, u32[]{:S(2)}, u32[]{:S(2)}) collective-permute-start(bf16[400,256]{1,0:T(8,128)(2,1)S(1)} %collective-permute-done.16.refs_0_), channel_id=1, source_target_pairs={{0,1},{1,0},{2,3},{3,2},{4,5},{5,4},{6,7},{7,6},{8,9},{9,8},{10,11... | collective-permute-start | bytes 614408 | tf_op jit(solution)/shard_map/ppermute | solution.py:340
  58.2 0.8 %destination_out.4.refs_1_ = f32[400,1024]{1,0:T(8,128)} custom-call(f32[400,1024]{1,0:T(8,128)S(1)} %bitcast.16, bf16[400,256]{1,0:T(8,128)(2,1)S(1)} %collective-permute-done.16.refs_0_, f32[400,1024]{1,0:T(8,128)} %destination_out.3.refs_1_), custom_call_target="tpu_custom_call", output_to_operand_aliasing={{}: (2, {})} | custom-call | flops 1 | bytes 1 | tf_op jit(solution)/shard_map/destination_out/pallas_call | solution.py:312
  59.0 0.3 collective-permute-done.19.refs_0_
  59.2 0.8 %destination_out.5 = f32[400,1024]{1,0:T(8,128)} custom-call(f32[400,1024]{1,0:T(8,128)S(1)} %bitcast.17, bf16[400,256]{1,0:T(8,128)(2,1)S(1)} %collective-permute-done.19.refs_0_, f32[400,1024]{1,0:T(8,128)} %destination_out.4.refs_1_), custom_call_target="tpu_custom_call", output_to_operand_aliasing={{}: (2, {})} | custom-call | flops 1 | bytes 1 | tf_op jit(solution)/shard_map/destination_out/pallas_call | solution.py:312
  (28 shorter events, 0.1 us)
Async XLA Ops:
  1.8 20.4 %collective-permute-start = (bf16[400,512]{1,0:T(8,128)(2,1)S(1)}, bf16[400,512]{1,0:T(8,128)(2,1)S(1)}, u32[]{:S(2)}, u32[]{:S(2)}) collective-permute-start(bf16[400,512]{1,0:T(8,128)(2,1)S(1)} %fusion), channel_id=1, source_target_pairs={{0,4},{1,5},{2,6},{3,7},{4,8},{5,9},{6,10},{7,11},{8,12},{9,13},{1... | collective-permute-start | bytes 1228808 | tf_op jit(solution)/shard_map/ppermute | solution.py:340
  5.1 2.7 %copy-start = (bf16[7424,400]{0,1:T(8,128)(2,1)S(1)}, bf16[7424,400]{0,1:T(8,128)(2,1)}, u32[]{:S(2)}) copy-start(bf16[7424,400]{0,1:T(8,128)(2,1)} %param.13) | copy-start | bytes 17817604
  7.8 1.0 %copy-start.2 = (f32[256,400]{0,1:T(8,128)S(1)}, f32[256,400]{0,1:T(8,128)}, u32[]{:S(2)}) copy-start(f32[256,400]{0,1:T(8,128)} %param.9) | copy-start | bytes 1228804
  8.8 4.3 %copy-start.8 = (f32[1024]{0:T(1024)S(1)}, f32[1024]{0:T(1024)}, u32[]{:S(2)}) copy-start(f32[1024]{0:T(1024)} %param.12) | copy-start | bytes 12292
  8.8 6.0 %copy-start.3 = (s32[1,2,2048]{2,1,0:T(2,128)S(1)}, s32[1,2,2048]{2,1,0:T(2,128)}, u32[]{:S(2)}) copy-start(s32[1,2,2048]{2,1,0:T(2,128)} %param.17) | copy-start | bytes 49156
  8.8 6.0 %copy-start.4 = (s32[1,2,256]{2,1,0:T(2,128)S(1)}, s32[1,2,256]{2,1,0:T(2,128)}, u32[]{:S(2)}) copy-start(s32[1,2,256]{2,1,0:T(2,128)} %param.16) | copy-start | bytes 6148
  8.8 6.0 %copy-start.5 = (s32[1,2,256]{2,1,0:T(2,128)S(1)}, s32[1,2,256]{2,1,0:T(2,128)}, u32[]{:S(2)}) copy-start(s32[1,2,256]{2,1,0:T(2,128)} %param.15) | copy-start | bytes 6148
  8.8 6.0 %copy-start.6 = (s32[1,2,256]{2,1,0:T(2,128)S(1)}, s32[1,2,256]{2,1,0:T(2,128)}, u32[]{:S(2)}) copy-start(s32[1,2,256]{2,1,0:T(2,128)} %param.14) | copy-start | bytes 6148
  8.8 6.0 %copy-start.7 = (f32[256]{0:T(256)S(1)}, f32[256]{0:T(256)}, u32[]{:S(2)}) copy-start(f32[256]{0:T(256)} %param.10) | copy-start | bytes 3076
  10.8 11.5 %collective-permute-start.1 = (bf16[416,256]{1,0:T(8,128)(2,1)S(1)}, bf16[416,256]{1,0:T(8,128)(2,1)S(1)}, u32[]{:S(2)}, u32[]{:S(2)}) collective-permute-start(bf16[416,256]{1,0:T(8,128)(2,1)S(1)} %get-tuple-element.38.q_ref.qa), channel_id=1, source_target_pairs={{0,1},{1,0},{2,3},{3,2},{4,5},{5,4},{6,7},{7,6},{8,9},{9,8},{10,11... | collective-permute-start | bytes 638984 | tf_op jit(solution)/shard_map/ppermute | solution.py:340
  11.8 14.6 %collective-permute-start.3 = (bf16[416,256]{1,0:T(8,128)(2,1)S(1)}, bf16[416,256]{1,0:T(8,128)(2,1)S(1)}, u32[]{:S(2)}, u32[]{:S(2)}) collective-permute-start(bf16[416,256]{1,0:T(8,128)(2,1)S(1)} %get-tuple-element.38.q_ref.qa), channel_id=1, source_target_pairs={{0,2},{1,3},{2,0},{3,1},{4,6},{5,7},{6,4},{7,5},{8,10},{9,11},{10,... | collective-permute-start | bytes 638984 | tf_op jit(solution)/shard_map/ppermute | solution.py:340
  13.1 9.1 %collective-permute-start.2 = (f32[1,1024]{1,0:T(1,128)S(1)}, f32[1,1024]{1,0:T(1,128)S(1)}, u32[]{:S(2)}, u32[]{:S(2)}) collective-permute-start(f32[1,1024]{1,0:T(1,128)S(1)} %bitcast.30), channel_id=1, source_target_pairs={{0,4},{1,5},{2,6},{3,7},{4,8},{5,9},{6,10},{7,11},{8,12},{9,13},{1... | collective-permute-start | bytes 12296 | tf_op jit(solution)/shard_map/ppermute | solution.py:340
  22.3 2.4 %collective-permute-start.4 = (bf16[400,256]{1,0:T(8,128)(2,1)S(1)}, bf16[400,256]{1,0:T(8,128)(2,1)S(1)}, u32[]{:S(2)}, u32[]{:S(2)}) collective-permute-start(bf16[400,256]{1,0:T(8,128)(2,1)S(1)} %get-tuple-element.73), channel_id=1, source_target_pairs={{0,1},{1,0},{2,3},{3,2},{4,5},{5,4},{6,7},{7,6},{8,9},{9,8},{10,11... | collective-permute-start | bytes 614408 | tf_op jit(solution)/shard_map/ppermute | solution.py:340
  23.6 1.5 %collective-permute-start.5 = (bf16[400,256]{1,0:T(8,128)(2,1)S(1)}, bf16[400,256]{1,0:T(8,128)(2,1)S(1)}, u32[]{:S(2)}, u32[]{:S(2)}) collective-permute-start(bf16[400,256]{1,0:T(8,128)(2,1)S(1)} %get-tuple-element.72), channel_id=1, source_target_pairs={{0,1},{1,0},{2,3},{3,2},{4,5},{5,4},{6,7},{7,6},{8,9},{9,8},{10,11... | collective-permute-start | bytes 614408 | tf_op jit(solution)/shard_map/ppermute | solution.py:340
  26.4 3.2 %collective-permute-start.6 = (bf16[416,256]{1,0:T(8,128)(2,1)S(1)}, bf16[416,256]{1,0:T(8,128)(2,1)S(1)}, u32[]{:S(2)}, u32[]{:S(2)}) collective-permute-start(bf16[416,256]{1,0:T(8,128)(2,1)S(1)} %collective-permute-done.3.qb), channel_id=1, source_target_pairs={{0,1},{1,0},{2,3},{3,2},{4,5},{5,4},{6,7},{7,6},{8,9},{9,8},{10,11... | collective-permute-start | bytes 638984 | tf_op jit(solution)/shard_map/ppermute | solution.py:340
  26.8 6.6 %collective-permute-start.7 = (bf16[416,256]{1,0:T(8,128)(2,1)S(1)}, bf16[416,256]{1,0:T(8,128)(2,1)S(1)}, u32[]{:S(2)}, u32[]{:S(2)}) collective-permute-start(bf16[416,256]{1,0:T(8,128)(2,1)S(1)} %get-tuple-element.62.q_ref), channel_id=1, source_target_pairs={{0,252},{1,253},{2,254},{3,255},{4,0},{5,1},{6,2},{7,3},{8,4},{9,5... | collective-permute-start | bytes 638984 | tf_op jit(solution)/shard_map/ppermute | solution.py:340
  28.6 9.0 %collective-permute-start.9 = (bf16[416,256]{1,0:T(8,128)(2,1)S(1)}, bf16[416,256]{1,0:T(8,128)(2,1)S(1)}, u32[]{:S(2)}, u32[]{:S(2)}) collective-permute-start(bf16[416,256]{1,0:T(8,128)(2,1)S(1)} %get-tuple-element.62.q_ref), channel_id=1, source_target_pairs={{0,254},{1,255},{2,252},{3,253},{4,2},{5,3},{6,0},{7,1},{8,6},{9,7... | collective-permute-start | bytes 638984 | tf_op jit(solution)/shard_map/ppermute | solution.py:340
  32.3 16.9 %collective-permute-start.12 = (bf16[400,512]{1,0:T(8,128)(2,1)S(1)}, bf16[400,512]{1,0:T(8,128)(2,1)S(1)}, u32[]{:S(2)}, u32[]{:S(2)}) collective-permute-start(bf16[400,512]{1,0:T(8,128)(2,1)S(1)} %get-tuple-element.60), channel_id=1, source_target_pairs={{0,4},{1,5},{2,6},{3,7},{4,8},{5,9},{6,10},{7,11},{8,12},{9,13},{1... | collective-permute-start | bytes 1228808 | tf_op jit(solution)/shard_map/ppermute | solution.py:340
  33.4 5.2 %collective-permute-start.8 = (bf16[416,256]{1,0:T(8,128)(2,1)S(1)}, bf16[416,256]{1,0:T(8,128)(2,1)S(1)}, u32[]{:S(2)}, u32[]{:S(2)}) collective-permute-start(bf16[416,256]{1,0:T(8,128)(2,1)S(1)} %collective-permute-done.7.qa), channel_id=1, source_target_pairs={{0,1},{1,0},{2,3},{3,2},{4,5},{5,4},{6,7},{7,6},{8,9},{9,8},{10,11... | collective-permute-start | bytes 638984 | tf_op jit(solution)/shard_map/ppermute | solution.py:340
  37.6 2.5 %collective-permute-start.10 = (bf16[416,256]{1,0:T(8,128)(2,1)S(1)}, bf16[416,256]{1,0:T(8,128)(2,1)S(1)}, u32[]{:S(2)}, u32[]{:S(2)}) collective-permute-start(bf16[416,256]{1,0:T(8,128)(2,1)S(1)} %collective-permute-done.9.qc), channel_id=1, source_target_pairs={{0,1},{1,0},{2,3},{3,2},{4,5},{5,4},{6,7},{7,6},{8,9},{9,8},{10,11... | collective-permute-start | bytes 638984 | tf_op jit(solution)/shard_map/ppermute | solution.py:340
  40.8 12.9 %collective-permute-start.11 = (bf16[400,256]{1,0:T(8,128)(2,1)S(1)}, bf16[400,256]{1,0:T(8,128)(2,1)S(1)}, u32[]{:S(2)}, u32[]{:S(2)}) collective-permute-start(bf16[400,256]{1,0:T(8,128)(2,1)S(1)} %destination_step1.2.refs_0_), channel_id=1, source_target_pairs={{0,254},{1,255},{2,252},{3,253},{4,0},{5,1},{6,2},{7,3},{8,4},{9,5... | collective-permute-start | bytes 614408 | tf_op jit(solution)/shard_map/ppermute | solution.py:340
  49.1 6.4 %copy-start.1 = (f32[1024,400]{0,1:T(8,128)S(1)}, f32[1024,400]{0,1:T(8,128)}, u32[]{:S(2)}) copy-start(f32[1024,400]{0,1:T(8,128)} %param.11) | copy-start | bytes 4915204
  49.2 2.2 %collective-permute-start.13 = (bf16[144,512]{1,0:T(8,128)(2,1)S(1)}, bf16[144,512]{1,0:T(8,128)(2,1)S(1)}, u32[]{:S(2)}, u32[]{:S(2)}) collective-permute-start(bf16[144,512]{1,0:T(8,128)(2,1)S(1)} %slice.23), channel_id=1, source_target_pairs={{0,1},{1,0},{2,3},{3,2},{4,5},{5,4},{6,7},{7,6},{8,9},{9,8},{10,11... | collective-permute-start | bytes 442376 | tf_op jit(solution)/shard_map/ppermute | solution.py:340
  49.8 1.4 %collective-permute-start.14 = (bf16[128,512]{1,0:T(8,128)(2,1)S(1)}, bf16[128,512]{1,0:T(8,128)(2,1)S(1)}, u32[]{:S(2)}, u32[]{:S(2)}) collective-permute-start(bf16[128,512]{1,0:T(8,128)(2,1)S(1)} %get-tuple-element.71), channel_id=1, source_target_pairs={{0,1},{1,0},{2,3},{3,2},{4,5},{5,4},{6,7},{7,6},{8,9},{9,8},{10,11... | collective-permute-start | bytes 393224 | tf_op jit(solution)/shard_map/ppermute | solution.py:340
  49.9 1.5 %collective-permute-start.15 = (bf16[128,512]{1,0:T(8,128)(2,1)S(1)}, bf16[128,512]{1,0:T(8,128)(2,1)S(1)}, u32[]{:S(2)}, u32[]{:S(2)}) collective-permute-start(bf16[128,512]{1,0:T(8,128)(2,1)S(1)} %get-tuple-element.70), channel_id=1, source_target_pairs={{0,1},{1,0},{2,3},{3,2},{4,5},{5,4},{6,7},{7,6},{8,9},{9,8},{10,11... | collective-permute-start | bytes 393224 | tf_op jit(solution)/shard_map/ppermute | solution.py:340
  50.4 7.0 %collective-permute-start.16 = (bf16[400,256]{1,0:T(8,128)(2,1)S(1)}, bf16[400,256]{1,0:T(8,128)(2,1)S(1)}, u32[]{:S(2)}, u32[]{:S(2)}) collective-permute-start(bf16[400,256]{1,0:T(8,128)(2,1)S(1)} %destination_step1.3), channel_id=1, source_target_pairs={{0,254},{1,255},{2,252},{3,253},{4,0},{5,1},{6,2},{7,3},{8,4},{9,5... | collective-permute-start | bytes 614408 | tf_op jit(solution)/shard_map/ppermute | solution.py:340
  53.7 1.5 %collective-permute-start.17 = (bf16[400,128]{1,0:T(8,128)(2,1)S(1)}, bf16[400,128]{1,0:T(8,128)(2,1)S(1)}, u32[]{:S(2)}, u32[]{:S(2)}) collective-permute-start(bf16[400,128]{1,0:T(8,128)(2,1)S(1)} %get-tuple-element.75), channel_id=1, source_target_pairs={{0,1},{1,0},{2,3},{3,2},{4,5},{5,4},{6,7},{7,6},{8,9},{9,8},{10,11... | collective-permute-start | bytes 307208 | tf_op jit(solution)/shard_map/ppermute | solution.py:340
  54.3 1.3 %collective-permute-start.18 = (bf16[400,128]{1,0:T(8,128)(2,1)S(1)}, bf16[400,128]{1,0:T(8,128)(2,1)S(1)}, u32[]{:S(2)}, u32[]{:S(2)}) collective-permute-start(bf16[400,128]{1,0:T(8,128)(2,1)S(1)} %get-tuple-element.74), channel_id=1, source_target_pairs={{0,1},{1,0},{2,3},{3,2},{4,5},{5,4},{6,7},{7,6},{8,9},{9,8},{10,11... | collective-permute-start | bytes 307208 | tf_op jit(solution)/shard_map/ppermute | solution.py:340
  57.4 1.9 %collective-permute-start.19 = (bf16[400,256]{1,0:T(8,128)(2,1)S(1)}, bf16[400,256]{1,0:T(8,128)(2,1)S(1)}, u32[]{:S(2)}, u32[]{:S(2)}) collective-permute-start(bf16[400,256]{1,0:T(8,128)(2,1)S(1)} %collective-permute-done.16.refs_0_), channel_id=1, source_target_pairs={{0,1},{1,0},{2,3},{3,2},{4,5},{5,4},{6,7},{7,6},{8,9},{9,8},{10,11... | collective-permute-start | bytes 614408 | tf_op jit(solution)/shard_map/ppermute | solution.py:340

commit v7 on v6

--- a/solution.py
+++ b/solution.py
@@ -118,14 +118,17 @@
 
 def prep_kernel(
     rows, rel_ref, q_ref, rel_index, neg_index, src_ref, state_ref, src_index, dst_index,
-    qt_ref, at_ref, rel_out, count_ref, column_ref, next_ref, next_count_ref,
-    src_out, state_out, src_index_out, dst_index_out,
+    qt_ref, at_ref, rel_out, count_ref, column_ref, next_count_ref,
+    src_out, state_out, src_index_out, hot0_ref, hot1_ref, picked_ref, meta_ref,
 ):
     depth, edges = rel_out.shape
     src_out[...] = src_ref[...]
     state_out[...] = state_ref[...]
     src_index_out[...] = src_index[...]
-    dst_index_out[...] = dst_index[...]
+    hot0_ref[...] = one_hot(edges, src_index[0:1, :])
+    hot1 = one_hot(edges, src_index[1:2, :])
+    hot1_ref[...] = hot1
+    picked_ref[...] = picked(src_ref[...], hot1)
     blocks = rows // LANES
     flip = core() * (rows // 2)
     coarse, fine = count_grid(neg_index[0:1, :] ^ flip, blocks)
@@ -134,7 +137,10 @@
     coarse, fine = count_grid(neg_index[1:2, :] ^ flip, blocks)
     counts = dot_nt(coarse, fine)
     high = jnp.floor(counts * (1.0 / FINE))
-    next_ref[...] = jnp.concatenate([high, counts - high * FINE], axis=0)
+    parts = jnp.concatenate([high, counts - high * FINE], axis=1)
+    gap = jnp.zeros((META // 2, edges), F32)
+    meta = index_rows(dst_index[1:2, :]).astype(F32)
+    meta_ref[...] = (meta + jnp.concatenate([gap, parts], axis=0)).astype(BF)
     lane_row(counts, next_count_ref)
     rel_out[...] = relation_rows(rel_ref, rel_index[1:2, :]).astype(BF)
     query_t, target_at = turned_query(q_ref, depth, flip)
@@ -171,7 +177,7 @@
 
 def src0_kernel(
     negatives, first_ref, other_a, other_b, qt_ref, at_ref, count_ref, src_ref, state_ref,
-    rel0_ref, rel1_ref, src_index, dst_index, next_ref, q_ref, src_out, state_out,
+    rel0_ref, rel1_ref, hot0_ref, hot1_ref, picked_ref, meta_ref, q_ref, src_out, state_out,
 ):
     depth, edges = src_ref.shape
     block = jnp.concatenate([other_a[...], other_b[...]], axis=1)
@@ -179,18 +185,14 @@
     grad = first_ref[...] + query_gradient(
         negatives, [block], qt_ref[...], at_ref[:, 0:1] - half, count_ref[:, half:]
     )
-    gradient = summed(grad * rel0_ref[...].astype(F32), one_hot(edges, src_index[0:1, :]))
+    gradient = dot_nt((grad * rel0_ref[...].astype(F32)).astype(BF), hot0_ref[...])
     state, size = step_size(state_ref[...], gradient)
-    src = src_ref[...] - gradient * size
-    src_out[...] = src
+    delta = gradient * size
+    src_out[...] = src_ref[...] - delta
     state_out[...] = state
-    rows = picked(src, one_hot(edges, src_index[1:2, :]))
+    rows = picked_ref[...] - dot(delta.astype(BF), hot1_ref[...])
     q_ref[:depth, :] = (rows * rel1_ref[...].astype(F32)).astype(BF)
-    blocks = next_ref.shape[0] // 2
-    counts = jnp.concatenate([next_ref[:blocks, :], next_ref[blocks:, :]], axis=1)
-    gap = jnp.zeros((META // 2, edges), F32)
-    meta = index_rows(dst_index[1:2, :]).astype(F32)
-    q_ref[depth:, :] = (meta + jnp.concatenate([gap, counts], axis=0)).astype(BF)
+    q_ref[depth:, :] = meta_ref[...]
 
 
 def src1_kernel(
@@ -267,22 +269,23 @@
     state_out[...] = state
 
 
-def dst1_first_kernel(negatives, turned_ref, qa, qb, qc, grad_out):
-    depth, half = grad_out.shape
-    grad_out[...] = dst_gradient(
-        turned_ref[...], (qa, qb, qc), sent_counts(qa, depth), core() * half, negatives
-    )
-
-
-def dst1_kernel(
-    negatives, start, turned_ref, first_ref, qa, qd, delta_ref, state_ref, *refs
-):
+def dst1_first_kernel(negatives, turned_ref, qa, qb, qc, grad_out, column_out):
+    depth, size = grad_out.shape
+    column = sent_counts(qa, depth)
+    column_out[...] = column
+    flip = core() * turned_ref.shape[0]
+    grad_out[...] = dst_gradient(turned_ref[:size, :], (qa, qb, qc), column, flip, negatives)
+
+
+def dst1_kernel(negatives, start, count, turned_ref, column_ref, delta_ref, state_ref, *refs):
     delta_out = refs[-1]
-    depth, half = delta_ref.shape
+    half = delta_ref.shape[1]
     part = slice(start, start + delta_out.shape[1])
-    gradient = first_ref[:, part] + dst_gradient(
-        turned_ref[part, :], (qd,), sent_counts(qa, depth), core() * half, negatives, start
-    )
+    gradient = dst_gradient(
+        turned_ref[part, :], refs[:count], column_ref[...], core() * half, negatives, start
+    )
+    if start == 0:
+        gradient = gradient + refs[count][...]
     _, size = step_size(state_ref[:, part], gradient)
     delta_out[...] = (delta_ref[:, part] + gradient * size).astype(BF)
 
@@ -371,8 +374,8 @@
     query, dst_state = lax.optimization_barrier((query, dst_state))
     state = moved(dst_state.reshape(1, rows), along=1, copies=True)
     (
-        query_t, target_at, rel1, count0, column, counts_sent, count1,
-        src, src_state, src_index, dst_index,
+        query_t, target_at, rel1, count0, column, count1,
+        src, src_state, src_index, hot0, hot1, picked1, meta1,
     ) = call(
         functools.partial(prep_kernel, rows),
         [
@@ -381,12 +384,14 @@
             ((depth, edges), BF),
             ((1, rows), F32),
             ((LANES, blocks), F32),
-            ((2 * blocks, LANES), F32),
             ((1, rows), F32),
             (src.shape, F32),
             (src_state.shape, F32),
             (src_index.shape, I32),
-            (dst_index.shape, I32),
+            ((edges, edges), BF),
+            ((edges, edges), BF),
+            (src.shape, F32),
+            ((META, edges), BF),
         ],
         [rel, query, rel_index, neg_index, src, src_state, src_index, dst_index],
         "prepare",
@@ -408,7 +413,7 @@
         [((tall, edges), BF), ((depth, edges), F32), ((1, edges), F32)],
         [
             first, *other, query_t, target_at, count0, src, src_state,
-            rel0, rel1, src_index, dst_index, counts_sent,
+            rel0, rel1, hot0, hot1, picked1, meta1,
         ],
         "source_step0",
         limit=24,
@@ -427,22 +432,23 @@
     block1_own = moved(block1, along=1, copies=True)
     next_c = moved(next_own, to=1)
 
-    first = call(
+    piece = half // 2
+    first, column1 = call(
         functools.partial(dst1_first_kernel, negatives),
-        [((depth, half), F32)],
+        [((depth, piece), F32), ((LANES, rows // LANES), F32)],
         [turned1, next_own, next_c, next_y],
         "destination_step1_first",
         limit=24,
     )
     next_cy = moved(next_y, to=1)
-    piece = half // 2
     deltas = []
-    for start in range(0, half, piece):
+    for start, queries in ((0, [next_cy]), (piece, [next_own, next_c, next_y, next_cy])):
+        more = [first] if start == 0 else deltas
         deltas.append(
             call(
-                functools.partial(dst1_kernel, negatives, start),
+                functools.partial(dst1_kernel, negatives, start, len(queries)),
                 [((depth, piece), BF)],
-                [turned1, first, next_own, next_cy, delta0, dst_state1, *deltas],
+                [turned1, column1, delta0, dst_state1, *queries, *more],
                 "destination_step1",
                 limit=24,
             )

time: 60.4 us -> 60.1 us (level)
  transfers between devices with their start and end apart: 20 -> 20, of which waited for: 11 -> 12; matrix products, arithmetic and copies ran while one was open for 1% -> 1% of each run, Pallas kernels for 26% -> 25%
where the time goes in v7:
time: 60.1 us; the launch traced here: 59.9 us
  starting transfers between devices  24.8 us (41%)
  Pallas kernels  16.1 us (27%)
  waiting for transfers between devices  12.3 us (20%)
  local copies, waits for them, and re-layouts  4.99 us (8%)
  between operations  0.98 us (2%)
  other arithmetic  0.72 us (1%)
    ppermute x20, starting transfers between devices, moved(): return lax.ppermute(value, ('wide', 'narrow'), pairs)  24.8 us
    pallas_call x12, Pallas kernels, call(): pl.pallas_call(kernel, out_shape=shapes, in_specs=[anywhere if i in hbm e...  16.1 us
    ppermute x20, waiting for transfers between devices, moved(): return lax.ppermute(value, ('wide', 'narrow'), pairs)  12.3 us
    unnamed x18, local copies, waits for them, and re-layouts  3.72 us
  transfers between devices with their start and end apart: 20, of which 12 were waited for; matrix products, arithmetic and copies ran while one was open for 1% of the time, Pallas kernels for 25%

profile of v7, /device:TPU:1, one launch (start us, length us, event | category | flops | bytes accessed | tf_op | source)
XLA Modules:
  0.0 59.9 jit_solution(668163585551770181)
XLA Ops:
  0.6 1.2 %fusion = bf16[400,512]{1,0:T(8,128)(2,1)S(1)} fusion(f32[1024,400]{0,1:T(8,128)} %param.11, s32[]{:T(128)S(6)} %select_n.3), kind=kLoop, calls=%fused_computation.1 | loop fusion | bytes 819204 | tf_op jit(solution)/shard_map/convert_element_type | solution.py:356
  1.8 2.5 %collective-permute-start = (bf16[400,512]{1,0:T(8,128)(2,1)S(1)}, bf16[400,512]{1,0:T(8,128)(2,1)S(1)}, u32[]{:S(2)}, u32[]{:S(2)}) collective-permute-start(bf16[400,512]{1,0:T(8,128)(2,1)S(1)} %fusion), channel_id=1, source_target_pairs={{0,4},{1,5},{2,6},{3,7},{4,8},{5,9},{6,10},{7,11},{8,12},{9,13},{1... | collective-permute-start | bytes 1228808 | tf_op jit(solution)/shard_map/ppermute | solution.py:343
  4.4 0.7 %pad_add_fusion.index = s32[6,256]{1,0:T(8,128)S(1)} fusion(s32[2,256]{1,0:T(2,128)} %bitcast.21, s32[2,256]{1,0:T(2,128)} %bitcast.23, s32[2,256]{1,0:T(2,128)} %bitcast.25), kind=kLoop, calls=%fused_computation.2 | loop fusion | flops 3072 | bytes 12288 | tf_op jit(solution)/shard_map/concatenate | solution.py:358
  5.1 2.7 %copy-done = bf16[7424,400]{0,1:T(8,128)(2,1)S(1)} copy-done((bf16[7424,400]{0,1:T(8,128)(2,1)S(1)}, bf16[7424,400]{0,1:T(8,128)(2,1)}, u32[]{:S(2)}) %copy-start) | copy-done | bytes 5939224
  7.8 1.0 %copy-done.2 = f32[256,400]{0,1:T(8,128)S(1)} copy-done((f32[256,400]{0,1:T(8,128)S(1)}, f32[256,400]{0,1:T(8,128)}, u32[]{:S(2)}) %copy-start.2) | copy-done | bytes 409624
  8.8 0.0 copy-start.6
  8.8 1.9 %query_step0.1 = (bf16[416,256]{1,0:T(8,128)(2,1)S(1)}, bf16[400,256]{1,0:T(8,128)(2,1)S(1)}) custom-call(bf16[400,7424]{1,0:T(8,128)(2,1)S(1)} %bitcast.13, f32[400,256]{1,0:T(8,128)S(1)} %bitcast.18, s32[6,256]{1,0:T(8,128)S(1)} %pad_add_fusion.index), custom_call_target="tpu_custom_call" | custom-call | flops 1520435200 | bytes 6772736 | tf_op jit(solution)/shard_map/query_step0/pallas_call | solution.py:315
  10.8 1.0 %collective-permute-start.1 = (bf16[416,256]{1,0:T(8,128)(2,1)S(1)}, bf16[416,256]{1,0:T(8,128)(2,1)S(1)}, u32[]{:S(2)}, u32[]{:S(2)}) collective-permute-start(bf16[416,256]{1,0:T(8,128)(2,1)S(1)} %get-tuple-element.42.q_ref.qa), channel_id=1, source_target_pairs={{0,1},{1,0},{2,3},{3,2},{4,5},{5,4},{6,7},{7,6},{8,9},{9,8},{10,11... | collective-permute-start | bytes 638984 | tf_op jit(solution)/shard_map/ppermute | solution.py:343
  11.8 1.3 %collective-permute-start.3 = (bf16[416,256]{1,0:T(8,128)(2,1)S(1)}, bf16[416,256]{1,0:T(8,128)(2,1)S(1)}, u32[]{:S(2)}, u32[]{:S(2)}) collective-permute-start(bf16[416,256]{1,0:T(8,128)(2,1)S(1)} %get-tuple-element.42.q_ref.qa), channel_id=1, source_target_pairs={{0,2},{1,3},{2,0},{3,1},{4,6},{5,7},{6,4},{7,5},{8,10},{9,11},{10,... | collective-permute-start | bytes 638984 | tf_op jit(solution)/shard_map/ppermute | solution.py:343
  13.1 1.6 %collective-permute-start.2 = (f32[1,1024]{1,0:T(1,128)S(1)}, f32[1,1024]{1,0:T(1,128)S(1)}, u32[]{:S(2)}, u32[]{:S(2)}) collective-permute-start(f32[1,1024]{1,0:T(1,128)S(1)} %bitcast.30), channel_id=1, source_target_pairs={{0,4},{1,5},{2,6},{3,7},{4,8},{5,9},{6,10},{7,11},{8,12},{9,13},{1... | collective-permute-start | bytes 12296 | tf_op jit(solution)/shard_map/ppermute | solution.py:343
  14.8 2.5 %prepare.1 = (bf16[256,400]{1,0:T(8,128)(2,1)S(1)}, s32[256,128]{1,0:T(8,128)S(1)}, bf16[400,256]{1,0:T(8,128)(2,1)S(1)}, f32[1,1024]{1,0:T(1,128)S(1)}, f32[128...) custom-call(bf16[400,7424]{1,0:T(8,128)(2,1)S(1)} %bitcast.14, ...), custom_call_target="tpu_custom_call" | custom-call | flops 1520435200 | bytes 8230912 | tf_op jit(solution)/shard_map/prepare/pallas_call | solution.py:315
  17.3 5.0 %collective-permute-done.2.old_ref = f32[1,1024]{1,0:T(1,128)S(1)} collective-permute-done((f32[1,1024]{1,0:T(1,128)S(1)}, f32[1,1024]{1,0:T(1,128)S(1)}, u32[]{:S(2)}, u32[]{:S(2)}) %collective-permute-start.2) | collective-permute-done | bytes 4128 | tf_op jit(solution)/shard_map/ppermute | solution.py:343
  22.3 1.3 %collective-permute-start.4 = (bf16[400,256]{1,0:T(8,128)(2,1)S(1)}, bf16[400,256]{1,0:T(8,128)(2,1)S(1)}, u32[]{:S(2)}, u32[]{:S(2)}) collective-permute-start(bf16[400,256]{1,0:T(8,128)(2,1)S(1)} %get-tuple-element.81), channel_id=1, source_target_pairs={{0,1},{1,0},{2,3},{3,2},{4,5},{5,4},{6,7},{7,6},{8,9},{9,8},{10,11... | collective-permute-start | bytes 614408 | tf_op jit(solution)/shard_map/ppermute | solution.py:343
  23.6 0.1 collective-permute-start.5
  23.7 0.6 %source_step0_first.1.first_ref = f32[400,256]{1,0:T(8,128)S(1)} custom-call(bf16[400,512]{1,0:T(8,128)(2,1)S(1)} %collective-permute-done.own_ref, bf16[256,400]{1,0:T(8,128)(2,1)S(1)} %get-tuple-element.47.qt_ref, s32[256,128]{1,0:T(8,128)S(1)} %get-tuple-element.48.at_ref, f32[1,1024]{1,0:T(1,128)S(1)} %get-tuple-element.49.count_ref), custom_call_target="tpu_custom_call" | custom-call | flops 1 | bytes 1 | tf_op jit(solution)/shard_map/source_step0_first/pallas_call | solution.py:315
  24.4 0.3 collective-permute-done.4.other_a
  24.7 0.4 collective-permute-done.5.other_b
  25.1 1.1 %source_step0.1 = (bf16[416,256]{1,0:T(8,128)(2,1)S(1)}, f32[400,256]{1,0:T(8,128)S(1)}, f32[1,256]{1,0:T(1,128)S(1)}) custom-call(f32[400,256]{1,0:T(8,128)S(1)} %source_step0_first.1.first_ref, bf16[400,256]{1,0:T(8,128)(2,1)S(1)} %collective-permute-done.4.other_a, bf16[400,256]{1,0:T(8,128)(2,1)S(1)} %collective-permute-done.5.other_b, ...), custom_call_target="tpu_custom_call" | custom-call | flops 1 | bytes 1 | tf_op jit(solution)/shard_map/source_step0/pallas_call | solution.py:315
  26.2 0.4 collective-permute-start.6
  26.6 1.8 %collective-permute-start.7 = (bf16[416,256]{1,0:T(8,128)(2,1)S(1)}, bf16[416,256]{1,0:T(8,128)(2,1)S(1)}, u32[]{:S(2)}, u32[]{:S(2)}) collective-permute-start(bf16[416,256]{1,0:T(8,128)(2,1)S(1)} %get-tuple-element.69.q_ref), channel_id=1, source_target_pairs={{0,252},{1,253},{2,254},{3,255},{4,0},{5,1},{6,2},{7,3},{8,4},{9,5... | collective-permute-start | bytes 638984 | tf_op jit(solution)/shard_map/ppermute | solution.py:343
  28.4 1.1 %collective-permute-start.9 = (bf16[416,256]{1,0:T(8,128)(2,1)S(1)}, bf16[416,256]{1,0:T(8,128)(2,1)S(1)}, u32[]{:S(2)}, u32[]{:S(2)}) collective-permute-start(bf16[416,256]{1,0:T(8,128)(2,1)S(1)} %get-tuple-element.69.q_ref), channel_id=1, source_target_pairs={{0,254},{1,255},{2,252},{3,253},{4,2},{5,3},{6,0},{7,1},{8,6},{9,7... | collective-permute-start | bytes 638984 | tf_op jit(solution)/shard_map/ppermute | solution.py:343
  29.6 2.7 %destination_step0.1 = (bf16[400,512]{1,0:T(8,128)(2,1)S(1)}, bf16[512,400]{1,0:T(8,128)(2,1)S(1)}, f32[400,512]{1,0:T(8,128)S(1)}, f32[1,512]{1,0:T(1,128)S(1)}) custom-call(bf16[400,512]{1,0:T(8,128)(2,1)S(1)} %collective-permute-done.own_ref, f32[1,1024]{1,0:T(1,128)S(1)} %collective-permute-done.2.old_ref, ...), custom_call_target="tpu_custom_call" | custom-call | flops 1 | bytes 1 | tf_op jit(solution)/shard_map/destination_step0/pallas_call | solution.py:315
  32.2 0.3 collective-permute-start.12
  32.6 0.7 %collective-permute-done.7.qa.refs_0_ = bf16[416,256]{1,0:T(8,128)(2,1)S(1)} collective-permute-done((bf16[416,256]{1,0:T(8,128)(2,1)S(1)}, bf16[416,256]{1,0:T(8,128)(2,1)S(1)}, u32[]{:S(2)}, u32[]{:S(2)}) %collective-permute-start.7) | collective-permute-done | bytes 213024 | tf_op jit(solution)/shard_map/ppermute | solution.py:343
  33.2 1.7 %collective-permute-start.8 = (bf16[416,256]{1,0:T(8,128)(2,1)S(1)}, bf16[416,256]{1,0:T(8,128)(2,1)S(1)}, u32[]{:S(2)}, u32[]{:S(2)}) collective-permute-start(bf16[416,256]{1,0:T(8,128)(2,1)S(1)} %collective-permute-done.7.qa.refs_0_), channel_id=1, source_target_pairs={{0,1},{1,0},{2,3},{3,2},{4,5},{5,4},{6,7},{7,6},{8,9},{9,8},{10,11... | collective-permute-start | bytes 638984 | tf_op jit(solution)/shard_map/ppermute | solution.py:343
  34.9 2.5 %collective-permute-done.9.qc.refs_2_ = bf16[416,256]{1,0:T(8,128)(2,1)S(1)} collective-permute-done((bf16[416,256]{1,0:T(8,128)(2,1)S(1)}, bf16[416,256]{1,0:T(8,128)(2,1)S(1)}, u32[]{:S(2)}, u32[]{:S(2)}) %collective-permute-start.9) | collective-permute-done | bytes 213024 | tf_op jit(solution)/shard_map/ppermute | solution.py:343
  37.4 1.0 %collective-permute-start.10 = (bf16[416,256]{1,0:T(8,128)(2,1)S(1)}, bf16[416,256]{1,0:T(8,128)(2,1)S(1)}, u32[]{:S(2)}, u32[]{:S(2)}) collective-permute-start(bf16[416,256]{1,0:T(8,128)(2,1)S(1)} %collective-permute-done.9.qc.refs_2_), channel_id=1, source_target_pairs={{0,1},{1,0},{2,3},{3,2},{4,5},{5,4},{6,7},{7,6},{8,9},{9,8},{10,11... | collective-permute-start | bytes 638984 | tf_op jit(solution)/shard_map/ppermute | solution.py:343
  38.4 0.7 %destination_step1_first.1 = (f32[400,256]{1,0:T(8,128)S(1)}, f32[128,8]{1,0:T(8,128)S(1)}) custom-call(bf16[512,400]{1,0:T(8,128)(2,1)S(1)} %get-tuple-element.62.turned_ref, bf16[416,256]{1,0:T(8,128)(2,1)S(1)} %collective-permute-done.7.qa.refs_0_, bf16[416,256]{1,0:T(8,128)(2,1)S(1)} %collective-permute-done.8.qb.refs_1_, ...), custom_call_target="tpu_custom_call" | custom-call | flops 1 | bytes 1 | tf_op jit(solution)/shard_map/destination_step1_first/pallas_call | solution.py:315
  39.2 0.4 collective-permute-done.10.refs_0_.refs_3_
  39.5 0.6 %destination_step1.2.refs_4_ = bf16[400,256]{1,0:T(8,128)(2,1)S(1)} custom-call(bf16[512,400]{1,0:T(8,128)(2,1)S(1)} %get-tuple-element.62.turned_ref, f32[128,8]{1,0:T(8,128)S(1)} %get-tuple-element.63.column_ref, f32[400,512]{1,0:T(8,128)S(1)} %get-tuple-element.64.delta_ref, f32[1,512]{1,0:T(1,128)S(1)} %get-tuple-element.65.state_ref, ...), custom_call_target="tpu_custom_call" | custom-call | flops 1 | bytes 1 | tf_op jit(solution)/shard_map/destination_step1/pallas_call | solution.py:315
  40.2 7.7 %collective-permute-start.11 = (bf16[400,256]{1,0:T(8,128)(2,1)S(1)}, bf16[400,256]{1,0:T(8,128)(2,1)S(1)}, u32[]{:S(2)}, u32[]{:S(2)}) collective-permute-start(bf16[400,256]{1,0:T(8,128)(2,1)S(1)} %destination_step1.2.refs_4_), channel_id=1, source_target_pairs={{0,254},{1,255},{2,252},{3,253},{4,0},{5,1},{6,2},{7,3},{8,4},{9,5... | collective-permute-start | bytes 614408 | tf_op jit(solution)/shard_map/ppermute | solution.py:343
  47.9 1.0 %destination_step1.3 = bf16[400,256]{1,0:T(8,128)(2,1)S(1)} custom-call(bf16[512,400]{1,0:T(8,128)(2,1)S(1)} %get-tuple-element.62.turned_ref, f32[128,8]{1,0:T(8,128)S(1)} %get-tuple-element.63.column_ref, f32[400,512]{1,0:T(8,128)S(1)} %get-tuple-element.64.delta_ref, f32[1,512]{1,0:T(1,128)S(1)} %get-tuple-element.65.state_ref, ...), custom_call_target="tpu_custom_call" | custom-call | flops 1 | bytes 1 | tf_op jit(solution)/shard_map/destination_step1/pallas_call | solution.py:315
  49.0 0.7 %collective-permute-start.13 = (bf16[144,512]{1,0:T(8,128)(2,1)S(1)}, bf16[144,512]{1,0:T(8,128)(2,1)S(1)}, u32[]{:S(2)}, u32[]{:S(2)}) collective-permute-start(bf16[144,512]{1,0:T(8,128)(2,1)S(1)} %slice.23), channel_id=1, source_target_pairs={{0,1},{1,0},{2,3},{3,2},{4,5},{5,4},{6,7},{7,6},{8,9},{9,8},{10,11... | collective-permute-start | bytes 442376 | tf_op jit(solution)/shard_map/ppermute | solution.py:343
  49.7 0.1 collective-permute-start.14
  49.9 0.5 collective-permute-start.15
  50.3 0.8 %collective-permute-done.14.other_b = bf16[128,512]{1,0:T(8,128)(2,1)S(1)} collective-permute-done((bf16[128,512]{1,0:T(8,128)(2,1)S(1)}, bf16[128,512]{1,0:T(8,128)(2,1)S(1)}, u32[]{:S(2)}, u32[]{:S(2)}) %collective-permute-start.14) | collective-permute-done | bytes 131104 | tf_op jit(solution)/shard_map/ppermute | solution.py:343
  51.2 0.2 collective-permute-done.15.other_c
  51.4 2.2 %source_step1.1 = f32[400,256]{1,0:T(8,128)} custom-call(bf16[400,512]{1,0:T(8,128)(2,1)S(1)} %collective-permute-done.12.own_ref, bf16[144,512]{1,0:T(8,128)(2,1)S(1)} %collective-permute-done.13.other_a, bf16[128,512]{1,0:T(8,128)(2,1)S(1)} %collective-permute-done.14.other_b, bf16[128,512]{1,0:T(8,128)(2,1)S(1)} %collective-permute-done.15.other_c, ...), custom_call_target="tpu_custom_call" | custom-call | flops 1 | bytes 1 | tf_op jit(solution)/shard_map/source_step1/pallas_call | solution.py:315
  53.6 0.5 collective-permute-start.17
  54.1 0.1 collective-permute-start.18
  54.2 0.8 %collective-permute-done.17.refs_1_ = bf16[400,128]{1,0:T(8,128)(2,1)S(1)} collective-permute-done((bf16[400,128]{1,0:T(8,128)(2,1)S(1)}, bf16[400,128]{1,0:T(8,128)(2,1)S(1)}, u32[]{:S(2)}, u32[]{:S(2)}) %collective-permute-start.17) | collective-permute-done | bytes 102432 | tf_op jit(solution)/shard_map/ppermute | solution.py:343
  55.0 0.4 collective-permute-done.18.refs_2_
  55.4 0.9 %destination_out.3.refs_1_ = f32[400,1024]{1,0:T(8,128)} custom-call(f32[400,1024]{1,0:T(8,128)S(1)} %bitcast.15, bf16[400,256]{1,0:T(8,128)(2,1)S(1)} %collective-permute-done.11.refs_0_, bf16[400,128]{1,0:T(8,128)(2,1)S(1)} %collective-permute-done.17.refs_1_, bf16[400,128]{1,0:T(8,128)(2,1)S(1)} %collective-permute-done.18.refs_2_), custom_call_target="tpu_custom_call" | custom-call | flops 1 | bytes 1 | tf_op jit(solution)/shard_map/destination_out/pallas_call | solution.py:315
  56.4 0.6 %collective-permute-done.16.refs_0_ = bf16[400,256]{1,0:T(8,128)(2,1)S(1)} collective-permute-done((bf16[400,256]{1,0:T(8,128)(2,1)S(1)}, bf16[400,256]{1,0:T(8,128)(2,1)S(1)}, u32[]{:S(2)}, u32[]{:S(2)}) %collective-permute-start.16) | collective-permute-done | bytes 204832 | tf_op jit(solution)/shard_map/ppermute | solution.py:343
  57.0 0.9 %collective-permute-start.19 = (bf16[400,256]{1,0:T(8,128)(2,1)S(1)}, bf16[400,256]{1,0:T(8,128)(2,1)S(1)}, u32[]{:S(2)}, u32[]{:S(2)}) collective-permute-start(bf16[400,256]{1,0:T(8,128)(2,1)S(1)} %collective-permute-done.16.refs_0_), channel_id=1, source_target_pairs={{0,1},{1,0},{2,3},{3,2},{4,5},{5,4},{6,7},{7,6},{8,9},{9,8},{10,11... | collective-permute-start | bytes 614408 | tf_op jit(solution)/shard_map/ppermute | solution.py:343
  57.9 0.8 %destination_out.4.refs_1_ = f32[400,1024]{1,0:T(8,128)} custom-call(f32[400,1024]{1,0:T(8,128)S(1)} %bitcast.16, bf16[400,256]{1,0:T(8,128)(2,1)S(1)} %collective-permute-done.16.refs_0_, f32[400,1024]{1,0:T(8,128)} %destination_out.3.refs_1_), custom_call_target="tpu_custom_call", output_to_operand_aliasing={{}: (2, {})} | custom-call | flops 1 | bytes 1 | tf_op jit(solution)/shard_map/destination_out/pallas_call | solution.py:315
  58.7 0.3 collective-permute-done.19.refs_0_
  58.9 0.8 %destination_out.5 = f32[400,1024]{1,0:T(8,128)} custom-call(f32[400,1024]{1,0:T(8,128)S(1)} %bitcast.17, bf16[400,256]{1,0:T(8,128)(2,1)S(1)} %collective-permute-done.19.refs_0_, f32[400,1024]{1,0:T(8,128)} %destination_out.4.refs_1_), custom_call_target="tpu_custom_call", output_to_operand_aliasing={{}: (2, {})} | custom-call | flops 1 | bytes 1 | tf_op jit(solution)/shard_map/destination_out/pallas_call | solution.py:315
  (28 shorter events, 0.1 us)
Async XLA Ops:
  1.8 20.4 %collective-permute-start = (bf16[400,512]{1,0:T(8,128)(2,1)S(1)}, bf16[400,512]{1,0:T(8,128)(2,1)S(1)}, u32[]{:S(2)}, u32[]{:S(2)}) collective-permute-start(bf16[400,512]{1,0:T(8,128)(2,1)S(1)} %fusion), channel_id=1, source_target_pairs={{0,4},{1,5},{2,6},{3,7},{4,8},{5,9},{6,10},{7,11},{8,12},{9,13},{1... | collective-permute-start | bytes 1228808 | tf_op jit(solution)/shard_map/ppermute | solution.py:343
  5.1 2.7 %copy-start = (bf16[7424,400]{0,1:T(8,128)(2,1)S(1)}, bf16[7424,400]{0,1:T(8,128)(2,1)}, u32[]{:S(2)}) copy-start(bf16[7424,400]{0,1:T(8,128)(2,1)} %param.13) | copy-start | bytes 17817604
  7.8 1.0 %copy-start.2 = (f32[256,400]{0,1:T(8,128)S(1)}, f32[256,400]{0,1:T(8,128)}, u32[]{:S(2)}) copy-start(f32[256,400]{0,1:T(8,128)} %param.9) | copy-start | bytes 1228804
  8.8 4.3 %copy-start.8 = (f32[1024]{0:T(1024)S(1)}, f32[1024]{0:T(1024)}, u32[]{:S(2)}) copy-start(f32[1024]{0:T(1024)} %param.12) | copy-start | bytes 12292
  8.8 6.0 %copy-start.3 = (s32[1,2,2048]{2,1,0:T(2,128)S(1)}, s32[1,2,2048]{2,1,0:T(2,128)}, u32[]{:S(2)}) copy-start(s32[1,2,2048]{2,1,0:T(2,128)} %param.17) | copy-start | bytes 49156
  8.8 6.0 %copy-start.4 = (s32[1,2,256]{2,1,0:T(2,128)S(1)}, s32[1,2,256]{2,1,0:T(2,128)}, u32[]{:S(2)}) copy-start(s32[1,2,256]{2,1,0:T(2,128)} %param.16) | copy-start | bytes 6148
  8.8 6.0 %copy-start.5 = (s32[1,2,256]{2,1,0:T(2,128)S(1)}, s32[1,2,256]{2,1,0:T(2,128)}, u32[]{:S(2)}) copy-start(s32[1,2,256]{2,1,0:T(2,128)} %param.15) | copy-start | bytes 6148
  8.8 6.0 %copy-start.6 = (s32[1,2,256]{2,1,0:T(2,128)S(1)}, s32[1,2,256]{2,1,0:T(2,128)}, u32[]{:S(2)}) copy-start(s32[1,2,256]{2,1,0:T(2,128)} %param.14) | copy-start | bytes 6148
  8.8 6.0 %copy-start.7 = (f32[256]{0:T(256)S(1)}, f32[256]{0:T(256)}, u32[]{:S(2)}) copy-start(f32[256]{0:T(256)} %param.10) | copy-start | bytes 3076
  10.8 11.5 %collective-permute-start.1 = (bf16[416,256]{1,0:T(8,128)(2,1)S(1)}, bf16[416,256]{1,0:T(8,128)(2,1)S(1)}, u32[]{:S(2)}, u32[]{:S(2)}) collective-permute-start(bf16[416,256]{1,0:T(8,128)(2,1)S(1)} %get-tuple-element.42.q_ref.qa), channel_id=1, source_target_pairs={{0,1},{1,0},{2,3},{3,2},{4,5},{5,4},{6,7},{7,6},{8,9},{9,8},{10,11... | collective-permute-start | bytes 638984 | tf_op jit(solution)/shard_map/ppermute | solution.py:343
  11.8 14.4 %collective-permute-start.3 = (bf16[416,256]{1,0:T(8,128)(2,1)S(1)}, bf16[416,256]{1,0:T(8,128)(2,1)S(1)}, u32[]{:S(2)}, u32[]{:S(2)}) collective-permute-start(bf16[416,256]{1,0:T(8,128)(2,1)S(1)} %get-tuple-element.42.q_ref.qa), channel_id=1, source_target_pairs={{0,2},{1,3},{2,0},{3,1},{4,6},{5,7},{6,4},{7,5},{8,10},{9,11},{10,... | collective-permute-start | bytes 638984 | tf_op jit(solution)/shard_map/ppermute | solution.py:343
  13.1 9.1 %collective-permute-start.2 = (f32[1,1024]{1,0:T(1,128)S(1)}, f32[1,1024]{1,0:T(1,128)S(1)}, u32[]{:S(2)}, u32[]{:S(2)}) collective-permute-start(f32[1,1024]{1,0:T(1,128)S(1)} %bitcast.30), channel_id=1, source_target_pairs={{0,4},{1,5},{2,6},{3,7},{4,8},{5,9},{6,10},{7,11},{8,12},{9,13},{1... | collective-permute-start | bytes 12296 | tf_op jit(solution)/shard_map/ppermute | solution.py:343
  22.3 2.4 %collective-permute-start.4 = (bf16[400,256]{1,0:T(8,128)(2,1)S(1)}, bf16[400,256]{1,0:T(8,128)(2,1)S(1)}, u32[]{:S(2)}, u32[]{:S(2)}) collective-permute-start(bf16[400,256]{1,0:T(8,128)(2,1)S(1)} %get-tuple-element.81), channel_id=1, source_target_pairs={{0,1},{1,0},{2,3},{3,2},{4,5},{5,4},{6,7},{7,6},{8,9},{9,8},{10,11... | collective-permute-start | bytes 614408 | tf_op jit(solution)/shard_map/ppermute | solution.py:343
  23.6 1.5 %collective-permute-start.5 = (bf16[400,256]{1,0:T(8,128)(2,1)S(1)}, bf16[400,256]{1,0:T(8,128)(2,1)S(1)}, u32[]{:S(2)}, u32[]{:S(2)}) collective-permute-start(bf16[400,256]{1,0:T(8,128)(2,1)S(1)} %get-tuple-element.80), channel_id=1, source_target_pairs={{0,1},{1,0},{2,3},{3,2},{4,5},{5,4},{6,7},{7,6},{8,9},{9,8},{10,11... | collective-permute-start | bytes 614408 | tf_op jit(solution)/shard_map/ppermute | solution.py:343
  26.2 3.3 %collective-permute-start.6 = (bf16[416,256]{1,0:T(8,128)(2,1)S(1)}, bf16[416,256]{1,0:T(8,128)(2,1)S(1)}, u32[]{:S(2)}, u32[]{:S(2)}) collective-permute-start(bf16[416,256]{1,0:T(8,128)(2,1)S(1)} %collective-permute-done.3.qb), channel_id=1, source_target_pairs={{0,1},{1,0},{2,3},{3,2},{4,5},{5,4},{6,7},{7,6},{8,9},{9,8},{10,11... | collective-permute-start | bytes 638984 | tf_op jit(solution)/shard_map/ppermute | solution.py:343
  26.6 6.6 %collective-permute-start.7 = (bf16[416,256]{1,0:T(8,128)(2,1)S(1)}, bf16[416,256]{1,0:T(8,128)(2,1)S(1)}, u32[]{:S(2)}, u32[]{:S(2)}) collective-permute-start(bf16[416,256]{1,0:T(8,128)(2,1)S(1)} %get-tuple-element.69.q_ref), channel_id=1, source_target_pairs={{0,252},{1,253},{2,254},{3,255},{4,0},{5,1},{6,2},{7,3},{8,4},{9,5... | collective-permute-start | bytes 638984 | tf_op jit(solution)/shard_map/ppermute | solution.py:343
  28.4 9.0 %collective-permute-start.9 = (bf16[416,256]{1,0:T(8,128)(2,1)S(1)}, bf16[416,256]{1,0:T(8,128)(2,1)S(1)}, u32[]{:S(2)}, u32[]{:S(2)}) collective-permute-start(bf16[416,256]{1,0:T(8,128)(2,1)S(1)} %get-tuple-element.69.q_ref), channel_id=1, source_target_pairs={{0,254},{1,255},{2,252},{3,253},{4,2},{5,3},{6,0},{7,1},{8,6},{9,7... | collective-permute-start | bytes 638984 | tf_op jit(solution)/shard_map/ppermute | solution.py:343
  32.2 16.7 %collective-permute-start.12 = (bf16[400,512]{1,0:T(8,128)(2,1)S(1)}, bf16[400,512]{1,0:T(8,128)(2,1)S(1)}, u32[]{:S(2)}, u32[]{:S(2)}) collective-permute-start(bf16[400,512]{1,0:T(8,128)(2,1)S(1)} %get-tuple-element.67), channel_id=1, source_target_pairs={{0,4},{1,5},{2,6},{3,7},{4,8},{5,9},{6,10},{7,11},{8,12},{9,13},{1... | collective-permute-start | bytes 1228808 | tf_op jit(solution)/shard_map/ppermute | solution.py:343
  33.2 5.2 %collective-permute-start.8 = (bf16[416,256]{1,0:T(8,128)(2,1)S(1)}, bf16[416,256]{1,0:T(8,128)(2,1)S(1)}, u32[]{:S(2)}, u32[]{:S(2)}) collective-permute-start(bf16[416,256]{1,0:T(8,128)(2,1)S(1)} %collective-permute-done.7.qa.refs_0_), channel_id=1, source_target_pairs={{0,1},{1,0},{2,3},{3,2},{4,5},{5,4},{6,7},{7,6},{8,9},{9,8},{10,11... | collective-permute-start | bytes 638984 | tf_op jit(solution)/shard_map/ppermute | solution.py:343
  37.4 2.1 %collective-permute-start.10 = (bf16[416,256]{1,0:T(8,128)(2,1)S(1)}, bf16[416,256]{1,0:T(8,128)(2,1)S(1)}, u32[]{:S(2)}, u32[]{:S(2)}) collective-permute-start(bf16[416,256]{1,0:T(8,128)(2,1)S(1)} %collective-permute-done.9.qc.refs_2_), channel_id=1, source_target_pairs={{0,1},{1,0},{2,3},{3,2},{4,5},{5,4},{6,7},{7,6},{8,9},{9,8},{10,11... | collective-permute-start | bytes 638984 | tf_op jit(solution)/shard_map/ppermute | solution.py:343
  40.2 13.4 %collective-permute-start.11 = (bf16[400,256]{1,0:T(8,128)(2,1)S(1)}, bf16[400,256]{1,0:T(8,128)(2,1)S(1)}, u32[]{:S(2)}, u32[]{:S(2)}) collective-permute-start(bf16[400,256]{1,0:T(8,128)(2,1)S(1)} %destination_step1.2.refs_4_), channel_id=1, source_target_pairs={{0,254},{1,255},{2,252},{3,253},{4,0},{5,1},{6,2},{7,3},{8,4},{9,5... | collective-permute-start | bytes 614408 | tf_op jit(solution)/shard_map/ppermute | solution.py:343
  48.9 6.5 %copy-start.1 = (f32[1024,400]{0,1:T(8,128)S(1)}, f32[1024,400]{0,1:T(8,128)}, u32[]{:S(2)}) copy-start(f32[1024,400]{0,1:T(8,128)} %param.11) | copy-start | bytes 4915204
  49.0 2.4 %collective-permute-start.13 = (bf16[144,512]{1,0:T(8,128)(2,1)S(1)}, bf16[144,512]{1,0:T(8,128)(2,1)S(1)}, u32[]{:S(2)}, u32[]{:S(2)}) collective-permute-start(bf16[144,512]{1,0:T(8,128)(2,1)S(1)} %slice.23), channel_id=1, source_target_pairs={{0,1},{1,0},{2,3},{3,2},{4,5},{5,4},{6,7},{7,6},{8,9},{9,8},{10,11... | collective-permute-start | bytes 442376 | tf_op jit(solution)/shard_map/ppermute | solution.py:343
  49.7 1.4 %collective-permute-start.14 = (bf16[128,512]{1,0:T(8,128)(2,1)S(1)}, bf16[128,512]{1,0:T(8,128)(2,1)S(1)}, u32[]{:S(2)}, u32[]{:S(2)}) collective-permute-start(bf16[128,512]{1,0:T(8,128)(2,1)S(1)} %get-tuple-element.79), channel_id=1, source_target_pairs={{0,1},{1,0},{2,3},{3,2},{4,5},{5,4},{6,7},{7,6},{8,9},{9,8},{10,11... | collective-permute-start | bytes 393224 | tf_op jit(solution)/shard_map/ppermute | solution.py:343
  49.9 1.5 %collective-permute-start.15 = (bf16[128,512]{1,0:T(8,128)(2,1)S(1)}, bf16[128,512]{1,0:T(8,128)(2,1)S(1)}, u32[]{:S(2)}, u32[]{:S(2)}) collective-permute-start(bf16[128,512]{1,0:T(8,128)(2,1)S(1)} %get-tuple-element.78), channel_id=1, source_target_pairs={{0,1},{1,0},{2,3},{3,2},{4,5},{5,4},{6,7},{7,6},{8,9},{9,8},{10,11... | collective-permute-start | bytes 393224 | tf_op jit(solution)/shard_map/ppermute | solution.py:343
  50.3 6.6 %collective-permute-start.16 = (bf16[400,256]{1,0:T(8,128)(2,1)S(1)}, bf16[400,256]{1,0:T(8,128)(2,1)S(1)}, u32[]{:S(2)}, u32[]{:S(2)}) collective-permute-start(bf16[400,256]{1,0:T(8,128)(2,1)S(1)} %destination_step1.3), channel_id=1, source_target_pairs={{0,254},{1,255},{2,252},{3,253},{4,0},{5,1},{6,2},{7,3},{8,4},{9,5... | collective-permute-start | bytes 614408 | tf_op jit(solution)/shard_map/ppermute | solution.py:343
  53.6 1.4 %collective-permute-start.17 = (bf16[400,128]{1,0:T(8,128)(2,1)S(1)}, bf16[400,128]{1,0:T(8,128)(2,1)S(1)}, u32[]{:S(2)}, u32[]{:S(2)}) collective-permute-start(bf16[400,128]{1,0:T(8,128)(2,1)S(1)} %get-tuple-element.83), channel_id=1, source_target_pairs={{0,1},{1,0},{2,3},{3,2},{4,5},{5,4},{6,7},{7,6},{8,9},{9,8},{10,11... | collective-permute-start | bytes 307208 | tf_op jit(solution)/shard_map/ppermute | solution.py:343
  54.1 1.3 %collective-permute-start.18 = (bf16[400,128]{1,0:T(8,128)(2,1)S(1)}, bf16[400,128]{1,0:T(8,128)(2,1)S(1)}, u32[]{:S(2)}, u32[]{:S(2)}) collective-permute-start(bf16[400,128]{1,0:T(8,128)(2,1)S(1)} %get-tuple-element.82), channel_id=1, source_target_pairs={{0,1},{1,0},{2,3},{3,2},{4,5},{5,4},{6,7},{7,6},{8,9},{9,8},{10,11... | collective-permute-start | bytes 307208 | tf_op jit(solution)/shard_map/ppermute | solution.py:343
  57.0 2.0 %collective-permute-start.19 = (bf16[400,256]{1,0:T(8,128)(2,1)S(1)}, bf16[400,256]{1,0:T(8,128)(2,1)S(1)}, u32[]{:S(2)}, u32[]{:S(2)}) collective-permute-start(bf16[400,256]{1,0:T(8,128)(2,1)S(1)} %collective-permute-done.16.refs_0_), channel_id=1, source_target_pairs={{0,1},{1,0},{2,3},{3,2},{4,5},{5,4},{6,7},{7,6},{8,9},{9,8},{10,11... | collective-permute-start | bytes 614408 | tf_op jit(solution)/shard_map/ppermute | solution.py:343

commit v8 on v7

--- a/solution.py
+++ b/solution.py
@@ -418,7 +418,7 @@
         "source_step0",
         limit=24,
     )
-    next_own, next_y = moved(query1, along=-1), moved(query1, along=-1, to=2)
+    next_own, next_y = (moved(query1, along=-1, to=to, copies=True) for to in (0, 2))
     query_y, query1 = lax.optimization_barrier((query_y, query1))
     query_cy = moved(query_y, to=1)
 

time: 60.1 us -> 60.7 us (level)
  starting transfers between devices: 24.8 us -> 25.8 us
    ppermute x20, starting transfers between devices: 24.8 us -> 25.8 us  [moved(): return lax.ppermute(value, ('wide', 'narrow'), pairs)]
where the time goes in v8:
time: 60.7 us; the launch traced here: 60.5 us
  starting transfers between devices  25.8 us (43%)
  Pallas kernels  16.1 us (27%)
  waiting for transfers between devices  11.9 us (20%)
  local copies, waits for them, and re-layouts  4.99 us (8%)
  between operations  0.98 us (2%)
  other arithmetic  0.72 us (1%)
    ppermute x20, starting transfers between devices, moved(): return lax.ppermute(value, ('wide', 'narrow'), pairs)  25.8 us
    pallas_call x12, Pallas kernels, call(): pl.pallas_call(kernel, out_shape=shapes, in_specs=[anywhere if i in hbm e...  16.1 us
    ppermute x20, waiting for transfers between devices, moved(): return lax.ppermute(value, ('wide', 'narrow'), pairs)  11.9 us
    unnamed x18, local copies, waits for them, and re-layouts  3.72 us
  transfers between devices with their start and end apart: 20, of which 12 were waited for; matrix products, arithmetic and copies ran while one was open for 1% of the time, Pallas kernels for 25%

profile of v8, /device:TPU:1, one launch (start us, length us, event | category | flops | bytes accessed | tf_op | source)
XLA Modules:
  0.0 60.5 jit_solution(1210470987700377809)
XLA Ops:
  0.6 1.2 %fusion = bf16[400,512]{1,0:T(8,128)(2,1)S(1)} fusion(f32[1024,400]{0,1:T(8,128)} %param.11, s32[]{:T(128)S(6)} %select_n.3), kind=kLoop, calls=%fused_computation.1 | loop fusion | bytes 819204 | tf_op jit(solution)/shard_map/convert_element_type | solution.py:356
  1.8 2.5 %collective-permute-start = (bf16[400,512]{1,0:T(8,128)(2,1)S(1)}, bf16[400,512]{1,0:T(8,128)(2,1)S(1)}, u32[]{:S(2)}, u32[]{:S(2)}) collective-permute-start(bf16[400,512]{1,0:T(8,128)(2,1)S(1)} %fusion), channel_id=1, source_target_pairs={{0,4},{1,5},{2,6},{3,7},{4,8},{5,9},{6,10},{7,11},{8,12},{9,13},{1... | collective-permute-start | bytes 1228808 | tf_op jit(solution)/shard_map/ppermute | solution.py:343
  4.4 0.7 %pad_add_fusion.index = s32[6,256]{1,0:T(8,128)S(1)} fusion(s32[2,256]{1,0:T(2,128)} %bitcast.21, s32[2,256]{1,0:T(2,128)} %bitcast.23, s32[2,256]{1,0:T(2,128)} %bitcast.25), kind=kLoop, calls=%fused_computation.2 | loop fusion | flops 3072 | bytes 12288 | tf_op jit(solution)/shard_map/concatenate | solution.py:358
  5.1 2.7 %copy-done = bf16[7424,400]{0,1:T(8,128)(2,1)S(1)} copy-done((bf16[7424,400]{0,1:T(8,128)(2,1)S(1)}, bf16[7424,400]{0,1:T(8,128)(2,1)}, u32[]{:S(2)}) %copy-start) | copy-done | bytes 5939224
  7.8 1.0 %copy-done.2 = f32[256,400]{0,1:T(8,128)S(1)} copy-done((f32[256,400]{0,1:T(8,128)S(1)}, f32[256,400]{0,1:T(8,128)}, u32[]{:S(2)}) %copy-start.2) | copy-done | bytes 409624
  8.8 0.0 copy-start.7
  8.8 1.9 %query_step0.1 = (bf16[416,256]{1,0:T(8,128)(2,1)S(1)}, bf16[400,256]{1,0:T(8,128)(2,1)S(1)}) custom-call(bf16[400,7424]{1,0:T(8,128)(2,1)S(1)} %bitcast.13, f32[400,256]{1,0:T(8,128)S(1)} %bitcast.18, s32[6,256]{1,0:T(8,128)S(1)} %pad_add_fusion.index), custom_call_target="tpu_custom_call" | custom-call | flops 1520435200 | bytes 6772736 | tf_op jit(solution)/shard_map/query_step0/pallas_call | solution.py:315
  10.8 1.0 %collective-permute-start.1 = (bf16[416,256]{1,0:T(8,128)(2,1)S(1)}, bf16[416,256]{1,0:T(8,128)(2,1)S(1)}, u32[]{:S(2)}, u32[]{:S(2)}) collective-permute-start(bf16[416,256]{1,0:T(8,128)(2,1)S(1)} %get-tuple-element.42.q_ref.qa), channel_id=1, source_target_pairs={{0,1},{1,0},{2,3},{3,2},{4,5},{5,4},{6,7},{7,6},{8,9},{9,8},{10,11... | collective-permute-start | bytes 638984 | tf_op jit(solution)/shard_map/ppermute | solution.py:343
  11.8 1.3 %collective-permute-start.3 = (bf16[416,256]{1,0:T(8,128)(2,1)S(1)}, bf16[416,256]{1,0:T(8,128)(2,1)S(1)}, u32[]{:S(2)}, u32[]{:S(2)}) collective-permute-start(bf16[416,256]{1,0:T(8,128)(2,1)S(1)} %get-tuple-element.42.q_ref.qa), channel_id=1, source_target_pairs={{0,2},{1,3},{2,0},{3,1},{4,6},{5,7},{6,4},{7,5},{8,10},{9,11},{10,... | collective-permute-start | bytes 638984 | tf_op jit(solution)/shard_map/ppermute | solution.py:343
  13.1 1.6 %collective-permute-start.2 = (f32[1,1024]{1,0:T(1,128)S(1)}, f32[1,1024]{1,0:T(1,128)S(1)}, u32[]{:S(2)}, u32[]{:S(2)}) collective-permute-start(f32[1,1024]{1,0:T(1,128)S(1)} %bitcast.30), channel_id=1, source_target_pairs={{0,4},{1,5},{2,6},{3,7},{4,8},{5,9},{6,10},{7,11},{8,12},{9,13},{1... | collective-permute-start | bytes 12296 | tf_op jit(solution)/shard_map/ppermute | solution.py:343
  14.8 2.5 %prepare.1 = (bf16[256,400]{1,0:T(8,128)(2,1)S(1)}, s32[256,128]{1,0:T(8,128)S(1)}, bf16[400,256]{1,0:T(8,128)(2,1)S(1)}, f32[1,1024]{1,0:T(1,128)S(1)}, f32[128...) custom-call(bf16[400,7424]{1,0:T(8,128)(2,1)S(1)} %bitcast.14, ...), custom_call_target="tpu_custom_call" | custom-call | flops 1520435200 | bytes 8230912 | tf_op jit(solution)/shard_map/prepare/pallas_call | solution.py:315
  17.3 5.0 %collective-permute-done.2.old_ref = f32[1,1024]{1,0:T(1,128)S(1)} collective-permute-done((f32[1,1024]{1,0:T(1,128)S(1)}, f32[1,1024]{1,0:T(1,128)S(1)}, u32[]{:S(2)}, u32[]{:S(2)}) %collective-permute-start.2) | collective-permute-done | bytes 4128 | tf_op jit(solution)/shard_map/ppermute | solution.py:343
  22.3 1.3 %collective-permute-start.4 = (bf16[400,256]{1,0:T(8,128)(2,1)S(1)}, bf16[400,256]{1,0:T(8,128)(2,1)S(1)}, u32[]{:S(2)}, u32[]{:S(2)}) collective-permute-start(bf16[400,256]{1,0:T(8,128)(2,1)S(1)} %get-tuple-element.81), channel_id=1, source_target_pairs={{0,1},{1,0},{2,3},{3,2},{4,5},{5,4},{6,7},{7,6},{8,9},{9,8},{10,11... | collective-permute-start | bytes 614408 | tf_op jit(solution)/shard_map/ppermute | solution.py:343
  23.6 0.1 collective-permute-start.5
  23.7 0.6 %source_step0_first.1.first_ref = f32[400,256]{1,0:T(8,128)S(1)} custom-call(bf16[400,512]{1,0:T(8,128)(2,1)S(1)} %collective-permute-done.own_ref, bf16[256,400]{1,0:T(8,128)(2,1)S(1)} %get-tuple-element.47.qt_ref, s32[256,128]{1,0:T(8,128)S(1)} %get-tuple-element.48.at_ref, f32[1,1024]{1,0:T(1,128)S(1)} %get-tuple-element.49.count_ref), custom_call_target="tpu_custom_call" | custom-call | flops 1 | bytes 1 | tf_op jit(solution)/shard_map/source_step0_first/pallas_call | solution.py:315
  24.4 0.3 collective-permute-done.4.other_a
  24.7 0.4 collective-permute-done.5.other_b
  25.1 1.1 %source_step0.1 = (bf16[416,256]{1,0:T(8,128)(2,1)S(1)}, f32[400,256]{1,0:T(8,128)S(1)}, f32[1,256]{1,0:T(1,128)S(1)}) custom-call(f32[400,256]{1,0:T(8,128)S(1)} %source_step0_first.1.first_ref, bf16[400,256]{1,0:T(8,128)(2,1)S(1)} %collective-permute-done.4.other_a, bf16[400,256]{1,0:T(8,128)(2,1)S(1)} %collective-permute-done.5.other_b, ...), custom_call_target="tpu_custom_call" | custom-call | flops 1 | bytes 1 | tf_op jit(solution)/shard_map/source_step0/pallas_call | solution.py:315
  26.2 0.4 collective-permute-start.6
  26.6 1.5 %collective-permute-start.7 = (bf16[416,256]{1,0:T(8,128)(2,1)S(1)}, bf16[416,256]{1,0:T(8,128)(2,1)S(1)}, u32[]{:S(2)}, u32[]{:S(2)}) collective-permute-start(bf16[416,256]{1,0:T(8,128)(2,1)S(1)} %get-tuple-element.69.q_ref), channel_id=1, source_target_pairs={{0,254},{1,255},{2,252},{3,253},{4,0},{5,1},{6,2},{7,3},{8,4},{9,5... | collective-permute-start | bytes 638984 | tf_op jit(solution)/shard_map/ppermute | solution.py:343
  28.1 2.1 %collective-permute-start.9 = (bf16[416,256]{1,0:T(8,128)(2,1)S(1)}, bf16[416,256]{1,0:T(8,128)(2,1)S(1)}, u32[]{:S(2)}, u32[]{:S(2)}) collective-permute-start(bf16[416,256]{1,0:T(8,128)(2,1)S(1)} %get-tuple-element.69.q_ref), channel_id=1, source_target_pairs={{0,252},{1,253},{2,254},{3,255},{4,2},{5,3},{6,0},{7,1},{8,6},{9,7... | collective-permute-start | bytes 638984 | tf_op jit(solution)/shard_map/ppermute | solution.py:343
  30.1 2.7 %destination_step0.1 = (bf16[400,512]{1,0:T(8,128)(2,1)S(1)}, bf16[512,400]{1,0:T(8,128)(2,1)S(1)}, f32[400,512]{1,0:T(8,128)S(1)}, f32[1,512]{1,0:T(1,128)S(1)}) custom-call(bf16[400,512]{1,0:T(8,128)(2,1)S(1)} %collective-permute-done.own_ref, f32[1,1024]{1,0:T(1,128)S(1)} %collective-permute-done.2.old_ref, ...), custom_call_target="tpu_custom_call" | custom-call | flops 1 | bytes 1 | tf_op jit(solution)/shard_map/destination_step0/pallas_call | solution.py:315
  32.8 0.1 collective-permute-start.12
  32.9 0.3 collective-permute-done.7.qa.refs_0_
  33.2 1.7 %collective-permute-start.8 = (bf16[416,256]{1,0:T(8,128)(2,1)S(1)}, bf16[416,256]{1,0:T(8,128)(2,1)S(1)}, u32[]{:S(2)}, u32[]{:S(2)}) collective-permute-start(bf16[416,256]{1,0:T(8,128)(2,1)S(1)} %collective-permute-done.7.qa.refs_0_), channel_id=1, source_target_pairs={{0,1},{1,0},{2,3},{3,2},{4,5},{5,4},{6,7},{7,6},{8,9},{9,8},{10,11... | collective-permute-start | bytes 638984 | tf_op jit(solution)/shard_map/ppermute | solution.py:343
  34.9 2.5 %collective-permute-done.9.qc.refs_2_ = bf16[416,256]{1,0:T(8,128)(2,1)S(1)} collective-permute-done((bf16[416,256]{1,0:T(8,128)(2,1)S(1)}, bf16[416,256]{1,0:T(8,128)(2,1)S(1)}, u32[]{:S(2)}, u32[]{:S(2)}) %collective-permute-start.9) | collective-permute-done | bytes 213024 | tf_op jit(solution)/shard_map/ppermute | solution.py:343
  37.4 1.0 %collective-permute-start.10 = (bf16[416,256]{1,0:T(8,128)(2,1)S(1)}, bf16[416,256]{1,0:T(8,128)(2,1)S(1)}, u32[]{:S(2)}, u32[]{:S(2)}) collective-permute-start(bf16[416,256]{1,0:T(8,128)(2,1)S(1)} %collective-permute-done.9.qc.refs_2_), channel_id=1, source_target_pairs={{0,1},{1,0},{2,3},{3,2},{4,5},{5,4},{6,7},{7,6},{8,9},{9,8},{10,11... | collective-permute-start | bytes 638984 | tf_op jit(solution)/shard_map/ppermute | solution.py:343
  38.4 0.7 %destination_step1_first.1 = (f32[400,256]{1,0:T(8,128)S(1)}, f32[128,8]{1,0:T(8,128)S(1)}) custom-call(bf16[512,400]{1,0:T(8,128)(2,1)S(1)} %get-tuple-element.62.turned_ref, bf16[416,256]{1,0:T(8,128)(2,1)S(1)} %collective-permute-done.7.qa.refs_0_, bf16[416,256]{1,0:T(8,128)(2,1)S(1)} %collective-permute-done.8.qb.refs_1_, ...), custom_call_target="tpu_custom_call" | custom-call | flops 1 | bytes 1 | tf_op jit(solution)/shard_map/destination_step1_first/pallas_call | solution.py:315
  39.1 0.4 collective-permute-done.10.refs_0_.refs_3_
  39.5 0.6 %destination_step1.2.refs_4_ = bf16[400,256]{1,0:T(8,128)(2,1)S(1)} custom-call(bf16[512,400]{1,0:T(8,128)(2,1)S(1)} %get-tuple-element.62.turned_ref, f32[128,8]{1,0:T(8,128)S(1)} %get-tuple-element.63.column_ref, f32[400,512]{1,0:T(8,128)S(1)} %get-tuple-element.64.delta_ref, f32[1,512]{1,0:T(1,128)S(1)} %get-tuple-element.65.state_ref, ...), custom_call_target="tpu_custom_call" | custom-call | flops 1 | bytes 1 | tf_op jit(solution)/shard_map/destination_step1/pallas_call | solution.py:315
  40.1 7.4 %collective-permute-start.11 = (bf16[400,256]{1,0:T(8,128)(2,1)S(1)}, bf16[400,256]{1,0:T(8,128)(2,1)S(1)}, u32[]{:S(2)}, u32[]{:S(2)}) collective-permute-start(bf16[400,256]{1,0:T(8,128)(2,1)S(1)} %destination_step1.2.refs_4_), channel_id=1, source_target_pairs={{0,254},{1,255},{2,252},{3,253},{4,0},{5,1},{6,2},{7,3},{8,4},{9,5... | collective-permute-start | bytes 614408 | tf_op jit(solution)/shard_map/ppermute | solution.py:343
  47.5 1.0 %destination_step1.3 = bf16[400,256]{1,0:T(8,128)(2,1)S(1)} custom-call(bf16[512,400]{1,0:T(8,128)(2,1)S(1)} %get-tuple-element.62.turned_ref, f32[128,8]{1,0:T(8,128)S(1)} %get-tuple-element.63.column_ref, f32[400,512]{1,0:T(8,128)S(1)} %get-tuple-element.64.delta_ref, f32[1,512]{1,0:T(1,128)S(1)} %get-tuple-element.65.state_ref, ...), custom_call_target="tpu_custom_call" | custom-call | flops 1 | bytes 1 | tf_op jit(solution)/shard_map/destination_step1/pallas_call | solution.py:315
  48.6 1.7 %collective-permute-start.13 = (bf16[144,512]{1,0:T(8,128)(2,1)S(1)}, bf16[144,512]{1,0:T(8,128)(2,1)S(1)}, u32[]{:S(2)}, u32[]{:S(2)}) collective-permute-start(bf16[144,512]{1,0:T(8,128)(2,1)S(1)} %slice.23), channel_id=1, source_target_pairs={{0,1},{1,0},{2,3},{3,2},{4,5},{5,4},{6,7},{7,6},{8,9},{9,8},{10,11... | collective-permute-start | bytes 442376 | tf_op jit(solution)/shard_map/ppermute | solution.py:343
  50.3 0.1 collective-permute-start.14
  50.4 0.5 collective-permute-start.15
  50.9 0.8 %collective-permute-done.14.other_b = bf16[128,512]{1,0:T(8,128)(2,1)S(1)} collective-permute-done((bf16[128,512]{1,0:T(8,128)(2,1)S(1)}, bf16[128,512]{1,0:T(8,128)(2,1)S(1)}, u32[]{:S(2)}, u32[]{:S(2)}) %collective-permute-start.14) | collective-permute-done | bytes 131104 | tf_op jit(solution)/shard_map/ppermute | solution.py:343
  51.8 0.2 collective-permute-done.15.other_c
  52.0 2.2 %source_step1.1 = f32[400,256]{1,0:T(8,128)} custom-call(bf16[400,512]{1,0:T(8,128)(2,1)S(1)} %collective-permute-done.12.own_ref, bf16[144,512]{1,0:T(8,128)(2,1)S(1)} %collective-permute-done.13.other_a, bf16[128,512]{1,0:T(8,128)(2,1)S(1)} %collective-permute-done.14.other_b, bf16[128,512]{1,0:T(8,128)(2,1)S(1)} %collective-permute-done.15.other_c, ...), custom_call_target="tpu_custom_call" | custom-call | flops 1 | bytes 1 | tf_op jit(solution)/shard_map/source_step1/pallas_call | solution.py:315
  54.2 0.4 collective-permute-start.17
  54.6 0.2 collective-permute-start.18
  54.8 0.8 %collective-permute-done.17.refs_1_ = bf16[400,128]{1,0:T(8,128)(2,1)S(1)} collective-permute-done((bf16[400,128]{1,0:T(8,128)(2,1)S(1)}, bf16[400,128]{1,0:T(8,128)(2,1)S(1)}, u32[]{:S(2)}, u32[]{:S(2)}) %collective-permute-start.17) | collective-permute-done | bytes 102432 | tf_op jit(solution)/shard_map/ppermute | solution.py:343
  55.6 0.3 collective-permute-done.18.refs_2_
  55.9 0.9 %destination_out.3.refs_1_ = f32[400,1024]{1,0:T(8,128)} custom-call(f32[400,1024]{1,0:T(8,128)S(1)} %bitcast.15, bf16[400,256]{1,0:T(8,128)(2,1)S(1)} %collective-permute-done.11.refs_0_, bf16[400,128]{1,0:T(8,128)(2,1)S(1)} %collective-permute-done.17.refs_1_, bf16[400,128]{1,0:T(8,128)(2,1)S(1)} %collective-permute-done.18.refs_2_), custom_call_target="tpu_custom_call" | custom-call | flops 1 | bytes 1 | tf_op jit(solution)/shard_map/destination_out/pallas_call | solution.py:315
  56.9 0.7 %collective-permute-done.16.refs_0_ = bf16[400,256]{1,0:T(8,128)(2,1)S(1)} collective-permute-done((bf16[400,256]{1,0:T(8,128)(2,1)S(1)}, bf16[400,256]{1,0:T(8,128)(2,1)S(1)}, u32[]{:S(2)}, u32[]{:S(2)}) %collective-permute-start.16) | collective-permute-done | bytes 204832 | tf_op jit(solution)/shard_map/ppermute | solution.py:343
  57.6 0.9 %collective-permute-start.19 = (bf16[400,256]{1,0:T(8,128)(2,1)S(1)}, bf16[400,256]{1,0:T(8,128)(2,1)S(1)}, u32[]{:S(2)}, u32[]{:S(2)}) collective-permute-start(bf16[400,256]{1,0:T(8,128)(2,1)S(1)} %collective-permute-done.16.refs_0_), channel_id=1, source_target_pairs={{0,1},{1,0},{2,3},{3,2},{4,5},{5,4},{6,7},{7,6},{8,9},{9,8},{10,11... | collective-permute-start | bytes 614408 | tf_op jit(solution)/shard_map/ppermute | solution.py:343
  58.4 0.8 %destination_out.4.refs_1_ = f32[400,1024]{1,0:T(8,128)} custom-call(f32[400,1024]{1,0:T(8,128)S(1)} %bitcast.16, bf16[400,256]{1,0:T(8,128)(2,1)S(1)} %collective-permute-done.16.refs_0_, f32[400,1024]{1,0:T(8,128)} %destination_out.3.refs_1_), custom_call_target="tpu_custom_call", output_to_operand_aliasing={{}: (2, {})} | custom-call | flops 1 | bytes 1 | tf_op jit(solution)/shard_map/destination_out/pallas_call | solution.py:315
  59.2 0.3 collective-permute-done.19.refs_0_
  59.5 0.8 %destination_out.5 = f32[400,1024]{1,0:T(8,128)} custom-call(f32[400,1024]{1,0:T(8,128)S(1)} %bitcast.17, bf16[400,256]{1,0:T(8,128)(2,1)S(1)} %collective-permute-done.19.refs_0_, f32[400,1024]{1,0:T(8,128)} %destination_out.4.refs_1_), custom_call_target="tpu_custom_call", output_to_operand_aliasing={{}: (2, {})} | custom-call | flops 1 | bytes 1 | tf_op jit(solution)/shard_map/destination_out/pallas_call | solution.py:315
  (28 shorter events, 0.1 us)
Async XLA Ops:
  1.8 20.4 %collective-permute-start = (bf16[400,512]{1,0:T(8,128)(2,1)S(1)}, bf16[400,512]{1,0:T(8,128)(2,1)S(1)}, u32[]{:S(2)}, u32[]{:S(2)}) collective-permute-start(bf16[400,512]{1,0:T(8,128)(2,1)S(1)} %fusion), channel_id=1, source_target_pairs={{0,4},{1,5},{2,6},{3,7},{4,8},{5,9},{6,10},{7,11},{8,12},{9,13},{1... | collective-permute-start | bytes 1228808 | tf_op jit(solution)/shard_map/ppermute | solution.py:343
  5.1 2.7 %copy-start = (bf16[7424,400]{0,1:T(8,128)(2,1)S(1)}, bf16[7424,400]{0,1:T(8,128)(2,1)}, u32[]{:S(2)}) copy-start(bf16[7424,400]{0,1:T(8,128)(2,1)} %param.13) | copy-start | bytes 17817604
  7.8 1.0 %copy-start.2 = (f32[256,400]{0,1:T(8,128)S(1)}, f32[256,400]{0,1:T(8,128)}, u32[]{:S(2)}) copy-start(f32[256,400]{0,1:T(8,128)} %param.9) | copy-start | bytes 1228804
  8.8 4.3 %copy-start.8 = (f32[1024]{0:T(1024)S(1)}, f32[1024]{0:T(1024)}, u32[]{:S(2)}) copy-start(f32[1024]{0:T(1024)} %param.12) | copy-start | bytes 12292
  8.8 6.0 %copy-start.3 = (s32[1,2,2048]{2,1,0:T(2,128)S(1)}, s32[1,2,2048]{2,1,0:T(2,128)}, u32[]{:S(2)}) copy-start(s32[1,2,2048]{2,1,0:T(2,128)} %param.17) | copy-start | bytes 49156
  8.8 6.0 %copy-start.4 = (s32[1,2,256]{2,1,0:T(2,128)S(1)}, s32[1,2,256]{2,1,0:T(2,128)}, u32[]{:S(2)}) copy-start(s32[1,2,256]{2,1,0:T(2,128)} %param.16) | copy-start | bytes 6148
  8.8 6.0 %copy-start.5 = (s32[1,2,256]{2,1,0:T(2,128)S(1)}, s32[1,2,256]{2,1,0:T(2,128)}, u32[]{:S(2)}) copy-start(s32[1,2,256]{2,1,0:T(2,128)} %param.15) | copy-start | bytes 6148
  8.8 6.0 %copy-start.6 = (s32[1,2,256]{2,1,0:T(2,128)S(1)}, s32[1,2,256]{2,1,0:T(2,128)}, u32[]{:S(2)}) copy-start(s32[1,2,256]{2,1,0:T(2,128)} %param.14) | copy-start | bytes 6148
  8.8 6.0 %copy-start.7 = (f32[256]{0:T(256)S(1)}, f32[256]{0:T(256)}, u32[]{:S(2)}) copy-start(f32[256]{0:T(256)} %param.10) | copy-start | bytes 3076
  10.8 11.5 %collective-permute-start.1 = (bf16[416,256]{1,0:T(8,128)(2,1)S(1)}, bf16[416,256]{1,0:T(8,128)(2,1)S(1)}, u32[]{:S(2)}, u32[]{:S(2)}) collective-permute-start(bf16[416,256]{1,0:T(8,128)(2,1)S(1)} %get-tuple-element.42.q_ref.qa), channel_id=1, source_target_pairs={{0,1},{1,0},{2,3},{3,2},{4,5},{5,4},{6,7},{7,6},{8,9},{9,8},{10,11... | collective-permute-start | bytes 638984 | tf_op jit(solution)/shard_map/ppermute | solution.py:343
  11.8 14.4 %collective-permute-start.3 = (bf16[416,256]{1,0:T(8,128)(2,1)S(1)}, bf16[416,256]{1,0:T(8,128)(2,1)S(1)}, u32[]{:S(2)}, u32[]{:S(2)}) collective-permute-start(bf16[416,256]{1,0:T(8,128)(2,1)S(1)} %get-tuple-element.42.q_ref.qa), channel_id=1, source_target_pairs={{0,2},{1,3},{2,0},{3,1},{4,6},{5,7},{6,4},{7,5},{8,10},{9,11},{10,... | collective-permute-start | bytes 638984 | tf_op jit(solution)/shard_map/ppermute | solution.py:343
  13.1 9.1 %collective-permute-start.2 = (f32[1,1024]{1,0:T(1,128)S(1)}, f32[1,1024]{1,0:T(1,128)S(1)}, u32[]{:S(2)}, u32[]{:S(2)}) collective-permute-start(f32[1,1024]{1,0:T(1,128)S(1)} %bitcast.30), channel_id=1, source_target_pairs={{0,4},{1,5},{2,6},{3,7},{4,8},{5,9},{6,10},{7,11},{8,12},{9,13},{1... | collective-permute-start | bytes 12296 | tf_op jit(solution)/shard_map/ppermute | solution.py:343
  22.3 2.4 %collective-permute-start.4 = (bf16[400,256]{1,0:T(8,128)(2,1)S(1)}, bf16[400,256]{1,0:T(8,128)(2,1)S(1)}, u32[]{:S(2)}, u32[]{:S(2)}) collective-permute-start(bf16[400,256]{1,0:T(8,128)(2,1)S(1)} %get-tuple-element.81), channel_id=1, source_target_pairs={{0,1},{1,0},{2,3},{3,2},{4,5},{5,4},{6,7},{7,6},{8,9},{9,8},{10,11... | collective-permute-start | bytes 614408 | tf_op jit(solution)/shard_map/ppermute | solution.py:343
  23.6 1.5 %collective-permute-start.5 = (bf16[400,256]{1,0:T(8,128)(2,1)S(1)}, bf16[400,256]{1,0:T(8,128)(2,1)S(1)}, u32[]{:S(2)}, u32[]{:S(2)}) collective-permute-start(bf16[400,256]{1,0:T(8,128)(2,1)S(1)} %get-tuple-element.80), channel_id=1, source_target_pairs={{0,1},{1,0},{2,3},{3,2},{4,5},{5,4},{6,7},{7,6},{8,9},{9,8},{10,11... | collective-permute-start | bytes 614408 | tf_op jit(solution)/shard_map/ppermute | solution.py:343
  26.2 3.9 %collective-permute-start.6 = (bf16[416,256]{1,0:T(8,128)(2,1)S(1)}, bf16[416,256]{1,0:T(8,128)(2,1)S(1)}, u32[]{:S(2)}, u32[]{:S(2)}) collective-permute-start(bf16[416,256]{1,0:T(8,128)(2,1)S(1)} %collective-permute-done.3.qb), channel_id=1, source_target_pairs={{0,1},{1,0},{2,3},{3,2},{4,5},{5,4},{6,7},{7,6},{8,9},{9,8},{10,11... | collective-permute-start | bytes 638984 | tf_op jit(solution)/shard_map/ppermute | solution.py:343
  26.6 6.6 %collective-permute-start.7 = (bf16[416,256]{1,0:T(8,128)(2,1)S(1)}, bf16[416,256]{1,0:T(8,128)(2,1)S(1)}, u32[]{:S(2)}, u32[]{:S(2)}) collective-permute-start(bf16[416,256]{1,0:T(8,128)(2,1)S(1)} %get-tuple-element.69.q_ref), channel_id=1, source_target_pairs={{0,254},{1,255},{2,252},{3,253},{4,0},{5,1},{6,2},{7,3},{8,4},{9,5... | collective-permute-start | bytes 638984 | tf_op jit(solution)/shard_map/ppermute | solution.py:343
  28.1 9.3 %collective-permute-start.9 = (bf16[416,256]{1,0:T(8,128)(2,1)S(1)}, bf16[416,256]{1,0:T(8,128)(2,1)S(1)}, u32[]{:S(2)}, u32[]{:S(2)}) collective-permute-start(bf16[416,256]{1,0:T(8,128)(2,1)S(1)} %get-tuple-element.69.q_ref), channel_id=1, source_target_pairs={{0,252},{1,253},{2,254},{3,255},{4,2},{5,3},{6,0},{7,1},{8,6},{9,7... | collective-permute-start | bytes 638984 | tf_op jit(solution)/shard_map/ppermute | solution.py:343
  32.8 15.8 %collective-permute-start.12 = (bf16[400,512]{1,0:T(8,128)(2,1)S(1)}, bf16[400,512]{1,0:T(8,128)(2,1)S(1)}, u32[]{:S(2)}, u32[]{:S(2)}) collective-permute-start(bf16[400,512]{1,0:T(8,128)(2,1)S(1)} %get-tuple-element.67), channel_id=1, source_target_pairs={{0,4},{1,5},{2,6},{3,7},{4,8},{5,9},{6,10},{7,11},{8,12},{9,13},{1... | collective-permute-start | bytes 1228808 | tf_op jit(solution)/shard_map/ppermute | solution.py:343
  33.2 5.2 %collective-permute-start.8 = (bf16[416,256]{1,0:T(8,128)(2,1)S(1)}, bf16[416,256]{1,0:T(8,128)(2,1)S(1)}, u32[]{:S(2)}, u32[]{:S(2)}) collective-permute-start(bf16[416,256]{1,0:T(8,128)(2,1)S(1)} %collective-permute-done.7.qa.refs_0_), channel_id=1, source_target_pairs={{0,1},{1,0},{2,3},{3,2},{4,5},{5,4},{6,7},{7,6},{8,9},{9,8},{10,11... | collective-permute-start | bytes 638984 | tf_op jit(solution)/shard_map/ppermute | solution.py:343
  37.4 2.1 %collective-permute-start.10 = (bf16[416,256]{1,0:T(8,128)(2,1)S(1)}, bf16[416,256]{1,0:T(8,128)(2,1)S(1)}, u32[]{:S(2)}, u32[]{:S(2)}) collective-permute-start(bf16[416,256]{1,0:T(8,128)(2,1)S(1)} %collective-permute-done.9.qc.refs_2_), channel_id=1, source_target_pairs={{0,1},{1,0},{2,3},{3,2},{4,5},{5,4},{6,7},{7,6},{8,9},{9,8},{10,11... | collective-permute-start | bytes 638984 | tf_op jit(solution)/shard_map/ppermute | solution.py:343
  40.1 14.1 %collective-permute-start.11 = (bf16[400,256]{1,0:T(8,128)(2,1)S(1)}, bf16[400,256]{1,0:T(8,128)(2,1)S(1)}, u32[]{:S(2)}, u32[]{:S(2)}) collective-permute-start(bf16[400,256]{1,0:T(8,128)(2,1)S(1)} %destination_step1.2.refs_4_), channel_id=1, source_target_pairs={{0,254},{1,255},{2,252},{3,253},{4,0},{5,1},{6,2},{7,3},{8,4},{9,5... | collective-permute-start | bytes 614408 | tf_op jit(solution)/shard_map/ppermute | solution.py:343
  48.6 7.4 %copy-start.1 = (f32[1024,400]{0,1:T(8,128)S(1)}, f32[1024,400]{0,1:T(8,128)}, u32[]{:S(2)}) copy-start(f32[1024,400]{0,1:T(8,128)} %param.11) | copy-start | bytes 4915204
  48.6 3.3 %collective-permute-start.13 = (bf16[144,512]{1,0:T(8,128)(2,1)S(1)}, bf16[144,512]{1,0:T(8,128)(2,1)S(1)}, u32[]{:S(2)}, u32[]{:S(2)}) collective-permute-start(bf16[144,512]{1,0:T(8,128)(2,1)S(1)} %slice.23), channel_id=1, source_target_pairs={{0,1},{1,0},{2,3},{3,2},{4,5},{5,4},{6,7},{7,6},{8,9},{9,8},{10,11... | collective-permute-start | bytes 442376 | tf_op jit(solution)/shard_map/ppermute | solution.py:343
  50.3 1.4 %collective-permute-start.14 = (bf16[128,512]{1,0:T(8,128)(2,1)S(1)}, bf16[128,512]{1,0:T(8,128)(2,1)S(1)}, u32[]{:S(2)}, u32[]{:S(2)}) collective-permute-start(bf16[128,512]{1,0:T(8,128)(2,1)S(1)} %get-tuple-element.79), channel_id=1, source_target_pairs={{0,1},{1,0},{2,3},{3,2},{4,5},{5,4},{6,7},{7,6},{8,9},{9,8},{10,11... | collective-permute-start | bytes 393224 | tf_op jit(solution)/shard_map/ppermute | solution.py:343
  50.4 1.5 %collective-permute-start.15 = (bf16[128,512]{1,0:T(8,128)(2,1)S(1)}, bf16[128,512]{1,0:T(8,128)(2,1)S(1)}, u32[]{:S(2)}, u32[]{:S(2)}) collective-permute-start(bf16[128,512]{1,0:T(8,128)(2,1)S(1)} %get-tuple-element.78), channel_id=1, source_target_pairs={{0,1},{1,0},{2,3},{3,2},{4,5},{5,4},{6,7},{7,6},{8,9},{9,8},{10,11... | collective-permute-start | bytes 393224 | tf_op jit(solution)/shard_map/ppermute | solution.py:343
  50.9 6.6 %collective-permute-start.16 = (bf16[400,256]{1,0:T(8,128)(2,1)S(1)}, bf16[400,256]{1,0:T(8,128)(2,1)S(1)}, u32[]{:S(2)}, u32[]{:S(2)}) collective-permute-start(bf16[400,256]{1,0:T(8,128)(2,1)S(1)} %destination_step1.3), channel_id=1, source_target_pairs={{0,254},{1,255},{2,252},{3,253},{4,0},{5,1},{6,2},{7,3},{8,4},{9,5... | collective-permute-start | bytes 614408 | tf_op jit(solution)/shard_map/ppermute | solution.py:343
  54.2 1.4 %collective-permute-start.17 = (bf16[400,128]{1,0:T(8,128)(2,1)S(1)}, bf16[400,128]{1,0:T(8,128)(2,1)S(1)}, u32[]{:S(2)}, u32[]{:S(2)}) collective-permute-start(bf16[400,128]{1,0:T(8,128)(2,1)S(1)} %get-tuple-element.83), channel_id=1, source_target_pairs={{0,1},{1,0},{2,3},{3,2},{4,5},{5,4},{6,7},{7,6},{8,9},{9,8},{10,11... | collective-permute-start | bytes 307208 | tf_op jit(solution)/shard_map/ppermute | solution.py:343
  54.6 1.3 %collective-permute-start.18 = (bf16[400,128]{1,0:T(8,128)(2,1)S(1)}, bf16[400,128]{1,0:T(8,128)(2,1)S(1)}, u32[]{:S(2)}, u32[]{:S(2)}) collective-permute-start(bf16[400,128]{1,0:T(8,128)(2,1)S(1)} %get-tuple-element.82), channel_id=1, source_target_pairs={{0,1},{1,0},{2,3},{3,2},{4,5},{5,4},{6,7},{7,6},{8,9},{9,8},{10,11... | collective-permute-start | bytes 307208 | tf_op jit(solution)/shard_map/ppermute | solution.py:343
  57.6 2.0 %collective-permute-start.19 = (bf16[400,256]{1,0:T(8,128)(2,1)S(1)}, bf16[400,256]{1,0:T(8,128)(2,1)S(1)}, u32[]{:S(2)}, u32[]{:S(2)}) collective-permute-start(bf16[400,256]{1,0:T(8,128)(2,1)S(1)} %collective-permute-done.16.refs_0_), channel_id=1, source_target_pairs={{0,1},{1,0},{2,3},{3,2},{4,5},{5,4},{6,7},{7,6},{8,9},{9,8},{10,11... | collective-permute-start | bytes 614408 | tf_op jit(solution)/shard_map/ppermute | solution.py:343
